TPU v7x, 32 devices: a whole 2x2x4 slice. The times are simulated.
32 devices in a mesh: seq: 8 (over z, x), grp: 4 (over y, core).
Axes of the slice: x: 2, y: 2, z: 4, core: 2. Of those that a mesh axis runs over, the one named last changes fastest.
Arguments:
- stream_in: bfloat16 [8192, 2048], P(('seq', 'grp')), may hold values from -5 to 5
- query_rows: bfloat16 [8192, 2048], P(('seq', 'grp')), may hold values from -4 to 4
- key_rows: bfloat16 [8192, 2048], P(('seq', 'grp')), may hold values from -4 to 4
- value_rows: bfloat16 [8192, 2048], P(('seq', 'grp')), may hold values from -4 to 4
- log_decay: float32 [16, 8192], P(None, ('seq', 'grp')), may hold values from -1 to 0
- attn_gain: float32 [2048], replicated, may hold values from 0.25 to 1.75
- ffn_gain: float32 [2048], replicated, may hold values from 0.25 to 1.75
- expert_ids: int32 [8192, 8], P(('seq', 'grp')), may hold values from 0 to 15, as said below
- route_weights: float32 [8192, 8], P(('seq', 'grp')), may hold values from 0.1 to 0.5
- response_mask: int32 [8192], P(('seq', 'grp')), may hold values from 0 to 1, as said below
- gate_weight: bfloat16 [2048, 16384], P(None, ('seq', 'grp')), may hold values from -0.125 to 0.125
- up_weight: bfloat16 [2048, 16384], P(None, ('seq', 'grp')), may hold values from -0.125 to 0.125
- down_weight: bfloat16 [16384, 2048], P(('seq', 'grp')), may hold values from -0.1875 to 0.1875
Outputs:
- layer_out: bfloat16 [8192, 2048], P(('seq', 'grp'))
Inputs may be any that keep to these rules, and one draw needn't show every extreme that they name: `response_mask`: the response tokens among each aligned block of 256 tokens form one contiguous run. `expert_ids`: each row names 8 different experts; over the response tokens of one aligned block of 256 tokens no expert is named more than 16 times, and in every draw some block names some expert exactly 16 times.
All inputs are finite; a program needn't handle non-finite values.
Results may differ from a plain program's by a relative error of at most 0.0059.
Values may be sent and summed in bfloat16 or wider, within the bound.
No kernel may reach another device: no remote copies, remote signals or barrier semaphores. Data moves between devices by JAX's collectives and lax.ppermute only.
A program may use at most 320 MiB of HBM per device.

v0:
```python
import jax
import jax.numpy as jnp
from jax import lax
from jax.sharding import PartitionSpec as P

CAP = 16


attn_eps = 1e-05
norm_eps = 1e-06


def carried_in(part, axis, combine, identity):
    place = lax.axis_index(axis)
    gathered = jax.tree.map(lambda a: lax.all_gather(a, axis), part)
    state = jax.tree.map(lambda a, e: jnp.zeros_like(a) + jnp.asarray(e, a.dtype), part, identity)

    def one(step, state):
        return combine(
            state, jax.tree.map(lambda a: lax.dynamic_index_in_dim(a, step, 0, False), gathered)
        )

    return lax.fori_loop(0, place, one, state)


def partner(block, axis, apart):
    count = lax.axis_size(axis)
    route = []
    for low in range(count):
        high = low | 1 << apart
        if high != low and high < count:
            route += [(low, high), (high, low)]
    return lax.ppermute(block, axis, route)


def local_terms(query_blk, key_blk, value_blk, decay_blk):
    length = query_blk.shape[0]
    running = jnp.cumsum(decay_blk, axis=1)
    block_total = running[:, -1]
    row_pos = lax.broadcasted_iota(jnp.int32, (length, length), 0)
    col_pos = lax.broadcasted_iota(jnp.int32, (length, length), 1)
    causal = (row_pos >= col_pos)[None]
    decay_gap = running[:, :, None] - running[:, None, :]
    factor = jnp.where(causal, jnp.exp(jnp.where(causal, decay_gap, 0.0)), 0.0)
    scores = jnp.einsum("thd,shd->hts", query_blk, key_blk, preferred_element_type=jnp.float32)
    weight_matrix = (scores * factor).astype(jnp.bfloat16)
    inside = jnp.einsum(
        "hts,shd->thd", weight_matrix, value_blk, preferred_element_type=jnp.float32
    )
    lifted = (query_blk.astype(jnp.float32) * jnp.exp(running).T[:, :, None]).astype(jnp.bfloat16)
    scaled = (
        key_blk.astype(jnp.float32) * jnp.exp(block_total[:, None] - running).T[:, :, None]
    ).astype(jnp.bfloat16)
    local_state = jnp.einsum("thd,the->hde", scaled, value_blk, preferred_element_type=jnp.float32)
    return (inside, lifted, local_state, jnp.exp(block_total))


def combine_states(earlier, later):
    return (earlier[0] * later[0], later[0][:, None, None] * earlier[1] + later[1])


def shards(
    stream_in,
    query_rows,
    key_rows,
    value_rows,
    log_decay,
    attn_gain,
    ffn_gain,
    expert_ids,
    route_weights,
    response_mask,
    gate_weight,
    up_weight,
    down_weight,
):
    tok_rows, width = stream_in.shape
    head_count = log_decay.shape[0]
    head_dim = width // head_count
    shaped = (tok_rows, head_count, head_dim)
    inside, lifted, local_state, block_decay = local_terms(
        query_rows.reshape(shaped), key_rows.reshape(shaped), value_rows.reshape(shaped), log_decay
    )
    own_pair = (block_decay, local_state)
    identity = (jnp.ones_like(block_decay), jnp.zeros_like(local_state))
    prefix = carried_in(own_pair, ("seq", "grp"), combine_states, identity)
    state_low = prefix[1].astype(jnp.bfloat16)
    carried = jnp.einsum("thd,hde->the", lifted, state_low, preferred_element_type=jnp.float32)
    attended = inside + carried
    normed = attended * lax.rsqrt(jnp.mean(attended * attended, axis=-1, keepdims=True) + attn_eps)
    mixed_rows = stream_in.astype(jnp.float32) + normed.reshape(tok_rows, width) * attn_gain
    ffn_in = (
        mixed_rows
        * lax.rsqrt(jnp.mean(mixed_rows * mixed_rows, axis=-1, keepdims=True) + norm_eps)
        * ffn_gain
    ).astype(jnp.bfloat16)
    devices = lax.axis_size(("seq", "grp"))
    experts = devices // 2
    top_count = expert_ids.shape[1]
    flat_ids = expert_ids.reshape(-1)
    live = jnp.repeat(response_mask, top_count) == 1
    onehot = (
        (flat_ids[:, None] == jnp.arange(experts, dtype=jnp.int32)[None, :]) & live[:, None]
    ).astype(jnp.int32)
    earlier_count = jnp.sum((jnp.cumsum(onehot, axis=0) - onehot) * onehot, axis=1)
    target = jnp.where(live, flat_ids * CAP + earlier_count, experts * CAP)
    source_row = jnp.arange(tok_rows * top_count, dtype=jnp.int32) // top_count
    slot_token = (
        jnp.full((experts * CAP,), tok_rows, jnp.int32).at[target].set(source_row, mode="drop")
    )
    padded_in = jnp.concatenate([ffn_in, jnp.zeros((1, width), jnp.bfloat16)], axis=0)
    slot_rows = padded_in[slot_token]
    half_rows = CAP // 2
    sent = slot_rows.reshape(devices, half_rows, width)
    arrived = lax.all_to_all(sent, ("seq", "grp"), split_axis=0, concat_axis=0, tiled=True)
    partner_rows = partner(arrived, "grp", 0)
    expert_arrived = jnp.concatenate([arrived, partner_rows], axis=1)
    flat_rows = expert_arrived.reshape(-1, width)
    gate_act = jnp.dot(flat_rows, gate_weight, preferred_element_type=jnp.float32)
    up_act = jnp.dot(flat_rows, up_weight, preferred_element_type=jnp.float32)
    hidden = (jax.nn.silu(gate_act) * up_act).astype(jnp.bfloat16)
    partial_value = jnp.dot(hidden, down_weight, preferred_element_type=jnp.float32).astype(
        jnp.bfloat16
    )
    partial_value = partial_value.reshape(expert_arrived.shape)
    theirs = partner(partial_value[:, half_rows:], "grp", 0)
    summed = (partial_value[:, :half_rows].astype(jnp.float32) + theirs.astype(jnp.float32)).astype(
        jnp.bfloat16
    )
    returned = lax.all_to_all(summed, ("seq", "grp"), split_axis=0, concat_axis=0, tiled=True)
    expert_out = returned.reshape(experts * CAP, width)
    out_padded = jnp.concatenate([expert_out, jnp.zeros((1, width), jnp.bfloat16)], axis=0)
    picked = out_padded[target].reshape(tok_rows, top_count, width)
    scale_rows = jnp.where(live.reshape(tok_rows, top_count), route_weights, 0.0)
    moe_sum = jnp.sum(picked.astype(jnp.float32) * scale_rows[:, :, None], axis=1)
    return (mixed_rows + moe_sum).astype(jnp.bfloat16)


def solution(mesh):
    placed = (
        P(("seq", "grp"), None),
        P(("seq", "grp"), None),
        P(("seq", "grp"), None),
        P(("seq", "grp"), None),
        P(None, ("seq", "grp")),
        P(),
        P(),
        P(("seq", "grp"), None),
        P(("seq", "grp"), None),
        P(("seq", "grp")),
        P(None, ("seq", "grp")),
        P(None, ("seq", "grp")),
        P(("seq", "grp"), None),
    )
    return jax.shard_map(
        shards, mesh=mesh, in_specs=placed, out_specs=P(("seq", "grp"), None), check_vma=False
    )
```

profile of v0, /device:TPU:0, one launch (start us, length us, event | category | flops | bytes accessed | tf_op | source)
XLA Modules:
  0.0 380.4 jit_solution(3969268077437532405)
XLA Ops:
  6.5 0.9 copy_bitcast_fusion.1
  7.4 0.6 reduce-window.14
  8.0 0.2 slice_reduce_fusion.1
  8.2 0.1 copy_bitcast_fusion
  8.3 0.2 slice_reduce_fusion.2
  8.5 0.1 exponential_bitcast_fusion.1
  8.5 1.5 copy.79
  10.0 0.0 copy-start.8
  10.0 0.0 copy-start.12
  10.1 2.6 fusion.2
  12.7 0.0 all-gather.4.cloned.1.call-update
  12.7 0.1 copy.71
  12.9 0.1 eq.73
  13.0 0.1 eq.68
  13.1 0.0 copy-done.12
  13.1 0.1 eq.77
  13.2 0.1 broadcast_in_dim.60.clone
  13.3 0.1 eq.67
  13.4 0.1 eq.72
  13.6 0.2 dynamic-update-slice
  13.8 44.0 %all-reduce.2 = f32[512]{0:T(512)S(1)} all-reduce(f32[512]{0:T(512)S(1)} %dynamic-update-slice), channel_id=2, replica_groups=mesh['seq'=8,'grp'=4] {'seq','grp'}, use_global_device_ids=true, to_apply=%add.2 | all-reduce | flops 512 | bytes 4096
  57.8 0.1 reshape.236
  57.9 0.1 copy.70
  58.0 0.1 mul.131
  58.1 0.1 copy.74
  58.2 0.1 copy.75
  58.3 4.5 %reduce-window.16 = s32[16,16,128]{2,1,0:T(8,128)S(1)} reduce-window(s32[16,16,128]{2,1,0:T(8,128)S(1)} %fusion.22, s32[]{:T(128)} %constant.41.clone.1), window={size=1x1x128 pad=0_0x0_0x127_0}, to_apply=%region_6.7 | reduce-window | flops 4161536 | bytes 262148 | tf_op jit(solution)/shard_map/reduce-window.2
  62.9 0.4 slice_reduce_fusion
  63.3 0.2 reduce-window.19
  63.5 0.1 broadcast_add_fusion
  63.6 0.1 fusion.19
  63.7 8.0 %scatter_custom_fusion = s32[256]{0:T(256)S(1)} fusion(s32[2048]{0:T(1024)S(1)} %bitcast.114, s32[2048]{0:T(1024)S(1)} %add_select_fusion, s32[]{:T(128)} %constant.75.clone.1), kind=kCustom, calls=%fused_computation.74 | custom fusion | bytes 1028 | tf_op jit(solution)/shard_map/scatter | solution.py:109
  71.8 4.6 %fusion.1 = f32[16,256,128]{1,2,0:T(8,128)} fusion(bf16[256,16,128]{0,2,1:T(8,128)(2,1)S(1)} %bitcast.102, f32[16,256]{1,0:T(8,128)S(1)} %copy_bitcast_fusion, pred[256,256]{1,0:T(8,128)(4,1)S(1)} %iota_compare_fusion, bf16[256,2048]{1,0:T(8,128)(2,1)} %param.18, bf16[256,2048]{1,0:T(8,128)(2,1)} %param.16), kind=kOutput, calls=%fused_computation.19 | convolution fusion | flops 542113792 | bytes 5324800 | tf_op jit(solution)/shard_map/hts,shd->thd/dot_general | solution.py:47
  76.5 134.9 %all-gather.4.cloned.1.call-done = f32[512,128,128]{2,1,0:T(8,128)} async-done(((f32[16,128,128]{2,1,0:T(8,128)}), f32[512,128,128]{2,1,0:T(8,128)}) %all-gather.4.cloned.1.call-update) | async-done | bytes 33554448 | tf_op jit(solution)/shard_map/all_gather | solution.py:15
  211.4 0.1 broadcast_in_dim.58
  211.5 2.9 multiply_reduce_fusion.1
  214.5 1.5 broadcast_multiply_fusion
  216.0 3.0 copy.68
  219.0 0.0 copy-done.7
  219.0 0.0 copy-start.9
  219.0 2.2 multiply_reduce_fusion
  221.2 0.0 copy-done.2
  221.2 0.5 multiply_convert_fusion.1
  221.7 0.1 concatenate.9
  221.8 2.3 gather_fusion
  224.2 75.1 %all_to_all.10 = bf16[32,8,2048]{2,1,0:T(8,128)(2,1)S(1)} all-to-all(bf16[32,8,2048]{2,1,0:T(8,128)(2,1)} %bitcast.103), channel_id=1, replica_groups=mesh['seq'=8,'grp'=4] {'seq','grp'}, dimensions={0} | all-to-all | bytes 2097152 | tf_op jit(solution)/shard_map/all_to_all | solution.py:115
  299.2 0.0 collective-permute-start
  299.2 2.7 collective-permute-done
  301.9 0.2 pad_maximum_fusion
  302.2 1.3 copy-done.6
  303.5 1.2 fusion.32
  304.8 6.0 %convolution_convert_fusion = bf16[512,2048]{1,0:T(8,128)(2,1)} fusion(bf16[512,2048]{1,0:T(8,128)(2,1)S(1)} %copy-done, f32[512,512]{1,0:T(8,128)S(1)} %fusion.32, bf16[512,2048]{1,0:T(8,128)(2,1)} %bitcast.108, bf16[2048,512]{1,0:T(8,128)(2,1)} %param.26), kind=kOutput, calls=%fused_computation.8 | convolution fusion | flops 2150105088 | bytes 9437184 | tf_op jit(solution)/shard_map/dot_general | solution.py:122
  310.7 1.4 slice.37
  312.2 0.0 copy-start.10
  312.2 0.2 collective-permute-start.1
  312.4 2.5 collective-permute-done.1
  314.9 1.4 add_convert_fusion.1
  316.3 3.6 all-to-all-start.1
  319.9 0.1 copy.76
  320.1 26.1 %all-to-all-done.1 = bf16[32,8,2048]{2,1,0:T(8,128)(2,1)S(1)} async-done(((bf16[32,8,2048]{2,1,0:T(8,128)(2,1)}), bf16[32,8,2048]{2,1,0:T(8,128)(2,1)S(1)}, u32[]{:S(2)}, u32[]{:S(2)}) %all-to-all-start.1) | async-done | bytes 1048608 | tf_op jit(solution)/shard_map/all_to_all | solution.py:130
  346.1 0.1 concatenate.11
  346.2 11.0 %gather_fusion.1 = bf16[2048,2048]{1,0:T(8,128)(2,1)} fusion(bf16[257,2048]{1,0:T(8,128)(2,1)S(1)} %concatenate.11, s32[2048]{0:T(1024)S(1)} %broadcast_clamp_fusion), kind=kCustom, calls=%fused_computation.1 | custom fusion | bytes 16785408 | tf_op jit(solution)/shard_map/gather | solution.py:133
  357.2 12.6 %fusion = f32[256,2048]{1,0:T(8,128)} fusion(bf16[2048,2048]{1,0:T(8,128)(2,1)} %gather_fusion.1, f32[256,8]{1,0:T(8,128)S(1)} %copy.76), kind=kLoop, calls=%fused_computation.6 | loop fusion | flops 12058624 | bytes 10493952 | tf_op jit(solution)/shard_map/reduce_sum | solution.py:135
  369.8 3.7 add_convert_fusion
  (36 shorter events, 0.2 us)
Async XLA Ops:
  6.5 298.2 %copy-start = (bf16[512,2048]{1,0:T(8,128)(2,1)S(1)}, bf16[512,2048]{1,0:T(8,128)(2,1)}, u32[]{:S(2)}) copy-start(bf16[512,2048]{1,0:T(8,128)(2,1)} %param.27) | copy-start | bytes 6291460
  6.5 204.9 %all-gather.4.cloned.1.call-start = ((), (), s32[]{:S(2)}) async-start(), calls=%async_computation.2 | async-start | bytes 34603008 | tf_op jit(solution)/shard_map/all_gather | solution.py:15
  10.0 2.7 copy-start.8
  10.0 3.0 copy-start.12
  216.0 3.0 copy-start.3
  216.0 3.1 copy-start.7
  219.0 2.2 copy-start.2
  219.0 2.2 copy-start.9
  299.2 4.3 %copy-start.11 = (bf16[2048,512]{1,0:T(8,128)(2,1)S(1)}, bf16[2048,512]{1,0:T(8,128)(2,1)}, u32[]{:S(2)}) copy-start(bf16[2048,512]{1,0:T(8,128)(2,1)} %param.25) | copy-start | bytes 6291460
  299.2 2.7 collective-permute-start
  302.1 1.4 copy-start.6
  310.7 4.2 %copy-start.5 = (bf16[512,2048]{1,0:T(8,128)(2,1)S(1)}, bf16[512,2048]{1,0:T(8,128)(2,1)}, u32[]{:S(2)}) copy-start(bf16[512,2048]{1,0:T(8,128)(2,1)} %convolution_convert_fusion) | copy-start | bytes 6291460
  312.2 7.7 %copy-start.10 = (f32[256,8]{0,1:T(8,128)S(1)}, f32[256,8]{0,1:T(8,128)}, u32[]{:S(2)}) copy-start(f32[256,8]{0,1:T(8,128)} %param.23) | copy-start | bytes 24580
  312.2 2.7 collective-permute-start.1
  316.3 29.9 %all-to-all-start.1 = ((bf16[32,8,2048]{2,1,0:T(8,128)(2,1)}), bf16[32,8,2048]{2,1,0:T(8,128)(2,1)S(1)}, u32[]{:S(2)}, u32[]{:S(2)}) async-start(bf16[32,8,2048]{2,1,0:T(8,128)(2,1)} %add_convert_fusion.1), calls=%async_computation.1 | async-start | bytes 2097152 | tf_op jit(solution)/shard_map/all_to_all | solution.py:130
  357.2 12.6 %copy-start.4 = (bf16[256,2048]{1,0:T(8,128)(2,1)S(1)}, bf16[256,2048]{1,0:T(8,128)(2,1)}, u32[]{:S(2)}) copy-start(bf16[256,2048]{1,0:T(8,128)(2,1)} %param.15) | copy-start | bytes 3145732
  357.2 16.3 %copy-start.1 = (bf16[512,2048]{1,0:T(8,128)(2,1)S(1)}, bf16[512,2048]{1,0:T(8,128)(2,1)}, u32[]{:S(2)}) copy-start(bf16[512,2048]{1,0:T(8,128)(2,1)} %param.27) | copy-start | bytes 6291460
Sparse Core Ops, SparseCore 0:
  12.8 198.5 all-gather.3
where the time goes:
time: 382 us; the launch traced here: 380 us
  waiting for transfers between devices  166 us (43%)
  blocking collectives  119 us (31%)
  local copies, waits for them, and re-layouts  32.3 us (8%)
  other arithmetic  27.9 us (7%)
  matrix products  17.4 us (5%)
  between operations  13.7 us (4%)
    all_gather x1, waiting for transfers between devices, carried_in(): gathered = jax.tree.map(lambda a: lax.all_gather(a, axis), part)  135 us
    all_to_all x1, blocking collectives, shards(): lax.all_to_all(sent, ('seq', 'grp'), split_axis=0, concat_axis=0, tiled=T...  75.1 us
    unnamed x1, blocking collectives  44 us
    all_to_all x1, waiting for transfers between devices, shards(): lax.all_to_all(summed, ('seq', 'grp'), split_axis=0, concat_axis=0, tiled...  26.1 us
    reduce_sum x1, other arithmetic, shards(): jnp.sum(picked.astype(jnp.float32) * scale_rows[:, :, None], axis=1)  12.6 us
    gather x1, local copies, waits for them, and re-layouts, shards(): picked = out_padded[target].reshape(tok_rows, top_count, width)  11 us
    scatter x1, local copies, waits for them, and re-layouts, shards(): jnp.full((experts * CAP,), tok_rows, jnp.int32).at[target]  8.04 us
  transfers between devices with their start and end apart: 4, of which 4 were waited for; matrix products, arithmetic and copies ran while one was open for 5% of the time, Pallas kernels for 0%

commit v1 on v0

v1 whole, which is shorter than its diff:
```python
import functools

import jax
import jax.numpy as jnp
from jax import lax
from jax.experimental import pallas as pl
from jax.experimental.pallas import tpu as pltpu
from jax.sharding import PartitionSpec as P

CAP = 16
TAIL = 8
TAIL16 = 16
ATTN_EPS = 1e-05
NORM_EPS = 1e-06
BOTH = ("seq", "grp")
F32 = jnp.float32
BF16 = jnp.bfloat16
VMEM = pl.BlockSpec(memory_space=pltpu.VMEM)
SMEM = pl.BlockSpec(memory_space=pltpu.SMEM)


def params(mb=32):
    return pltpu.CompilerParams(vmem_limit_bytes=mb * 1024 * 1024)


def cost(flops, nbytes):
    return pl.CostEstimate(flops=flops, bytes_accessed=nbytes, transcendentals=0)


def mm(a, b, ca=1, cb=0):
    return lax.dot_general(a, b, (((ca,), (cb,)), ((), ())), preferred_element_type=F32)


def lower_tri(n):
    rows = lax.broadcasted_iota(jnp.int32, (n, n), 0)
    cols = lax.broadcasted_iota(jnp.int32, (n, n), 1)
    return rows >= cols


def running_cols(dec):
    tri = lower_tri(dec.shape[1]).astype(F32)
    return lax.dot_general(
        tri, dec, (((1,), (1,)), ((), ())), precision=lax.Precision.HIGHEST, preferred_element_type=F32
    )


def running_rows(dec):
    tri = lower_tri(dec.shape[1]).astype(F32)
    return lax.dot_general(
        dec, tri, (((1,), (1,)), ((), ())), precision=lax.Precision.HIGHEST, preferred_element_type=F32
    )


def partner(x):
    count = lax.axis_size("grp")
    return lax.ppermute(x, "grp", [(i, i ^ 1) for i in range(count)])


def across_pairs(x):
    count = lax.axis_size(BOTH)
    groups = [list(range(k, count, 2)) for k in range(2)]
    return lax.all_to_all(x, BOTH, 0, 0, tiled=True, axis_index_groups=groups)


def states_kernel(k_ref, key_ref, val_ref, decr_ref, own_ref, send_ref):
    heads, tok = decr_ref.shape
    half = heads // 2
    hd = own_ref.shape[1]
    k = k_ref[0]
    run = running_cols(decr_ref[...])
    total = run[tok - 1 : tok, :]
    fac = jnp.exp(total - run)
    for r in range(heads):
        side = r // half
        off = pl.multiple_of((side ^ k) * (half * hd) + (r % half) * hd, hd)
        kh = key_ref[:, pl.ds(off, hd)].astype(F32)
        scaled = (kh * fac[:, r : r + 1]).astype(BF16)
        st = mm(scaled, val_ref[:, pl.ds(off, hd)], 0, 0)
        dst = own_ref if side == 0 else send_ref
        dst[(r % half) * hd : (r % half + 1) * hd, :] = st
    tail = jnp.broadcast_to(jnp.pad(total, ((0, 0), (0, hd - heads))), (TAIL, hd))
    own_ref[half * hd :, :] = tail
    send_ref[half * hd :, :] = tail


def pair_kernel(k_ref, own_ref, recv_ref, out_ref, *, half, rows):
    hd = own_ref.shape[1]
    first = k_ref[0] == 0
    base = half * hd
    mine = own_ref[base : base + 1, :]
    theirs = recv_ref[base : base + 1, :]
    pieces = out_ref.shape[0]
    tail_row = lax.broadcasted_iota(jnp.int32, (TAIL16, hd), 0)
    for p in range(pieces):
        j = p * rows // hd
        mt = mine[:, j : j + 1]
        pt = theirs[:, half + j : half + j + 1]
        one = jnp.ones_like(mt)
        a = jnp.where(first, jnp.exp(pt), one)
        b = jnp.where(first, one, jnp.exp(mt))
        lo = p * rows
        chip = own_ref[lo : lo + rows, :] * a + recv_ref[lo : lo + rows, :] * b
        out_ref[p, 0:rows, :] = chip.astype(BF16)
        d = jnp.broadcast_to(jnp.exp(mt + pt), (TAIL16, hd))
        d0 = d.astype(BF16).astype(F32)
        d1 = (d - d0).astype(BF16).astype(F32)
        d2 = d - d0 - d1
        tail = jnp.where(tail_row == 0, d0, jnp.where(tail_row == 1, d1, jnp.where(tail_row == 2, d2, 0.0)))
        out_ref[p, rows : rows + TAIL16, :] = tail.astype(BF16)


def scan_kernel(in_ref, out_ref):
    count, rows, hd = out_ref.shape
    state = jnp.zeros((rows, hd), F32)
    for c in range(count):
        out_ref[c, :, :] = state.astype(BF16)
        tail = in_ref[c, rows : rows + TAIL16, :].astype(F32)
        d = tail[0:1, :] + tail[1:2, :] + tail[2:3, :]
        state = state * d + in_ref[c, 0:rows, :].astype(F32)


def split_kernel(k_ref, pref_ref, own_ref, recv_ref, keep_ref, give_ref, *, half):
    hd = own_ref.shape[1]
    first = k_ref[0] == 0
    base = half * hd
    mine = own_ref[base : base + 1, :]
    theirs = recv_ref[base : base + 1, :]
    for j in range(half):
        sl = slice(j * hd, (j + 1) * hd)
        d0 = jnp.exp(jnp.where(first, mine[:, j : j + 1], theirs[:, half + j : half + j + 1]))
        s0 = jnp.where(first, own_ref[sl, :], recv_ref[sl, :])
        before = pref_ref[sl, :].astype(F32)
        after = before * d0 + s0
        keep_ref[sl, :] = jnp.where(first, before, after).astype(BF16)
        give_ref[sl, :] = jnp.where(first, after, before).astype(BF16)


def inside_kernel(dec_ref, q_ref, key_ref, val_ref, inside_ref, lifted_ref):
    heads, tok = dec_ref.shape
    hd = q_ref.shape[1] // heads
    dec = dec_ref[...]
    run_c = running_cols(dec)
    run_r = running_rows(dec)
    lift = jnp.exp(run_c)
    cut = tok // 2
    tri = lower_tri(cut)
    for h in range(heads):
        cols = slice(h * hd, (h + 1) * hd)
        q = q_ref[:, cols]
        kk = key_ref[:, cols]
        v = val_ref[:, cols]
        lifted_ref[:, cols] = (q.astype(F32) * lift[:, h : h + 1]).astype(BF16)
        rc = run_c[:, h : h + 1]
        rr = run_r[h : h + 1, :]
        f_aa = jnp.where(tri, jnp.exp(rc[:cut] - rr[:, :cut]), 0.0)
        f_bb = jnp.where(tri, jnp.exp(rc[cut:] - rr[:, cut:]), 0.0)
        f_ba = jnp.exp(rc[cut:] - rr[:, :cut])
        w_aa = (mm(q[:cut], kk[:cut], 1, 1) * f_aa).astype(BF16)
        s_b = mm(q[cut:], kk, 1, 1)
        w_b = (s_b * jnp.concatenate([f_ba, f_bb], axis=1)).astype(BF16)
        inside_ref[:cut, cols] = mm(w_aa, v[:cut])
        inside_ref[cut:, cols] = mm(w_b, v)


def head_norm(att):
    return att * lax.rsqrt(jnp.mean(att * att, axis=-1, keepdims=True) + ATTN_EPS)


def rows_kernel(k_ref, lifted_ref, inside_ref, stream_ref, keep_ref, other_ref, again_ref, fgain_ref, disp_ref, sent_ref, mixed_ref):
    hd = keep_ref.shape[1]
    half = keep_ref.shape[0] // hd
    k = k_ref[0]
    rows, width = lifted_ref.shape
    for r in range(2 * half):
        side = r // half
        off = pl.multiple_of((side ^ k) * (half * hd) + (r % half) * hd, hd)
        cols = pl.ds(off, hd)
        src = keep_ref if side == 0 else other_ref
        att = inside_ref[:, cols] + mm(lifted_ref[:, cols], src[(r % half) * hd : (r % half + 1) * hd, :])
        mixed_ref[:, cols] = stream_ref[:, cols].astype(F32) + head_norm(att) * again_ref[:, cols]
    mixed = mixed_ref[...]
    scale = lax.rsqrt(jnp.mean(mixed * mixed, axis=-1, keepdims=True) + NORM_EPS)
    ffn = (mixed * scale * fgain_ref[...]).astype(BF16)
    sent_ref[...] = mm(disp_ref[...], ffn, 0, 0).astype(BF16)


def mixed_kernel(k_ref, lifted_ref, inside_ref, stream_ref, keep_ref, other_ref, again_ref, mixed_ref):
    hd = keep_ref.shape[1]
    half = keep_ref.shape[0] // hd
    mine = pl.program_id(0) == k_ref[0]
    for j in range(half):
        cols = slice(j * hd, (j + 1) * hd)
        st = jnp.where(mine, keep_ref[cols, :].astype(F32), other_ref[cols, :].astype(F32)).astype(BF16)
        att = inside_ref[:, cols] + mm(lifted_ref[:, cols], st)
        mixed_ref[:, cols] = stream_ref[:, cols].astype(F32) + head_norm(att) * again_ref[:, cols]


def route_kernel(ids_ref, wts_ref, live_ref, disp_ref, chi_ref, clo_ref, *, experts):
    tok, top = ids_ref.shape
    slots = experts * CAP
    live = live_ref[...] == 1
    lane = lax.broadcasted_iota(jnp.int32, (tok, experts), 1)
    chosen = jnp.zeros((tok, experts), F32)
    weight = jnp.zeros((tok, experts), F32)
    for j in range(top):
        hit = (ids_ref[:, j : j + 1] == lane) & live
        chosen = jnp.where(hit, 1.0, chosen)
        weight = jnp.where(hit, wts_ref[:, j : j + 1], weight)
    rows = lax.broadcasted_iota(jnp.int32, (tok, tok), 0)
    cols = lax.broadcasted_iota(jnp.int32, (tok, tok), 1)
    before = jnp.where(rows > cols, 1.0, 0.0).astype(BF16)
    place = mm(before, chosen.astype(BF16))
    place = jnp.where(chosen > 0.0, place, -1.0)
    e_row = lax.broadcasted_iota(jnp.int32, (experts, slots), 0)
    s_col = lax.broadcasted_iota(jnp.int32, (experts, slots), 1)
    spread = jnp.where(s_col // CAP == e_row, 1.0, 0.0).astype(BF16)
    slot_of = lax.broadcasted_iota(jnp.int32, (tok, slots), 1) % CAP
    hit = mm(place.astype(BF16), spread) == slot_of.astype(F32)
    w_hi = weight.astype(BF16)
    w_lo = (weight - w_hi.astype(F32)).astype(BF16)
    disp_ref[...] = jnp.where(hit, 1.0, 0.0)
    chi_ref[...] = jnp.where(hit, mm(w_hi, spread), 0.0).astype(BF16)
    clo_ref[...] = jnp.where(hit, mm(w_lo, spread), 0.0).astype(BF16)


def final_kernel(mixed_ref, chi_ref, clo_ref, back_ref, out_ref):
    back = back_ref[...]
    moe = mm(chi_ref[...], back) + mm(clo_ref[...], back)
    out_ref[...] = (mixed_ref[...] + moe).astype(BF16)


def shards(
    stream_in,
    query_rows,
    key_rows,
    value_rows,
    log_decay,
    attn_gain,
    ffn_gain,
    expert_ids,
    route_weights,
    response_mask,
    gate_weight,
    up_weight,
    down_weight,
):
    tok, width = stream_in.shape
    heads = log_decay.shape[0]
    hd = width // heads
    half = heads // 2
    devices = lax.axis_size(BOTH)
    pairs = devices // 2
    experts = devices // 2
    slots = experts * CAP
    top = expert_ids.shape[1]
    resp = min(tok, slots // top)
    rows = half * hd // pairs
    me = lax.axis_index(BOTH)
    bit = (me & 1).reshape(1).astype(jnp.int32)
    sds = jax.ShapeDtypeStruct

    decr = jnp.where(bit[0] == 0, log_decay, jnp.concatenate([log_decay[half:], log_decay[:half]], axis=0))
    own, send = pl.pallas_call(
        states_kernel,
        out_shape=[sds((half * hd + TAIL, hd), F32)] * 2,
        in_specs=[SMEM, VMEM, VMEM, VMEM],
        out_specs=[VMEM, VMEM],
        compiler_params=params(),
        cost_estimate=cost(2 * tok * width * hd, 3 << 20),
        name="states",
    )(bit, key_rows, value_rows, decr)
    recv = partner(send)
    packed = pl.pallas_call(
        functools.partial(pair_kernel, half=half, rows=rows),
        out_shape=sds((pairs, rows + TAIL16, hd), BF16),
        in_specs=[SMEM, VMEM, VMEM],
        out_specs=VMEM,
        compiler_params=params(),
        name="pair",
    )(bit, own, recv)
    gathered = across_pairs(packed)
    scanned = pl.pallas_call(
        scan_kernel,
        out_shape=sds((pairs, rows, hd), BF16),
        in_specs=[VMEM],
        out_specs=VMEM,
        compiler_params=params(),
        name="scan",
    )(gathered)
    pref = across_pairs(scanned).reshape(half * hd, hd)
    keep, give = pl.pallas_call(
        functools.partial(split_kernel, half=half),
        out_shape=[sds((half * hd, hd), BF16)] * 2,
        in_specs=[SMEM] + [VMEM] * 3,
        out_specs=[VMEM, VMEM],
        compiler_params=params(),
        name="split",
    )(bit, pref, own, recv)
    other = partner(give)

    col = pl.BlockSpec((tok, width // 2), lambda i: (0, i))
    inside, lifted = pl.pallas_call(
        inside_kernel,
        grid=(2,),
        out_shape=[sds((tok, width), F32), sds((tok, width), BF16)],
        in_specs=[pl.BlockSpec((half, tok), lambda i: (i, 0)), col, col, col],
        out_specs=[col, col],
        compiler_params=params(),
        cost_estimate=cost(4 * tok * tok * width, 6 << 20),
        name="inside",
    )(log_decay, query_rows, key_rows, value_rows)
    disp, chi, clo = pl.pallas_call(
        functools.partial(route_kernel, experts=experts),
        out_shape=[sds((tok, slots), F32), sds((tok, slots), BF16), sds((tok, slots), BF16)],
        in_specs=[VMEM] * 3,
        out_specs=[VMEM] * 3,
        compiler_params=params(),
        cost_estimate=cost(8 * tok * tok * slots, 1 << 20),
        name="route",
    )(expert_ids, route_weights, response_mask.reshape(tok, 1))

    start = jnp.minimum(jnp.argmax(response_mask), tok - resp)
    cut = functools.partial(lax.dynamic_slice_in_dim, start_index=start, slice_size=resp, axis=0)
    again = attn_gain.reshape(1, width)
    sent = pl.pallas_call(
        rows_kernel,
        out_shape=sds((slots, width), BF16),
        in_specs=[SMEM] + [VMEM] * 8,
        out_specs=VMEM,
        scratch_shapes=[pltpu.VMEM((resp, width), F32)],
        compiler_params=params(),
        name="rows",
    )(
        bit,
        cut(lifted),
        cut(inside),
        cut(stream_in),
        keep,
        other,
        again,
        ffn_gain.reshape(1, width),
        cut(disp).astype(BF16),
    )
    half_rows = CAP // 2
    arrived = lax.all_to_all(sent.reshape(devices, half_rows, width), BOTH, 0, 0, tiled=True)

    gain_col = pl.BlockSpec((1, width // 2), lambda i: (0, i))
    state_all = pl.BlockSpec((half * hd, hd), lambda i: (0, 0))
    mixed = pl.pallas_call(
        mixed_kernel,
        grid=(2,),
        out_shape=sds((tok, width), F32),
        in_specs=[SMEM, col, col, col, state_all, state_all, gain_col],
        out_specs=col,
        compiler_params=params(),
        cost_estimate=cost(2 * tok * width * hd, 7 << 20),
        name="mixed",
    )(bit, lifted, inside, stream_in, keep, other, again)

    mine = arrived.reshape(devices * half_rows, width)
    theirs = partner(mine)
    flat = jnp.concatenate([mine, theirs], axis=0)
    gate_act = jnp.dot(flat, gate_weight, preferred_element_type=F32)
    up_act = jnp.dot(flat, up_weight, preferred_element_type=F32)
    hidden = (jax.nn.silu(gate_act) * up_act).astype(BF16)
    part = jnp.dot(hidden, down_weight, preferred_element_type=F32).astype(BF16)
    count = devices * half_rows
    added = partner(part[count:])
    summed = (part[:count].astype(F32) + added.astype(F32)).astype(BF16)
    back = lax.all_to_all(summed.reshape(devices, half_rows, width), BOTH, 0, 0, tiled=True)
    back = back.reshape(slots, width)

    steps = 4
    fcol = pl.BlockSpec((tok, width // steps), lambda i: (0, i))
    whole = pl.BlockSpec((tok, slots), lambda i: (0, 0))
    return pl.pallas_call(
        final_kernel,
        grid=(steps,),
        out_shape=sds((tok, width), BF16),
        in_specs=[fcol, whole, whole, pl.BlockSpec((slots, width // steps), lambda i: (0, i))],
        out_specs=fcol,
        compiler_params=params(),
        name="final",
    )(mixed, chi, clo, back)


def solution(mesh):
    lead = P(BOTH, None)
    placed = (
        lead,
        lead,
        lead,
        lead,
        P(None, BOTH),
        P(),
        P(),
        lead,
        lead,
        P(BOTH),
        P(None, BOTH),
        P(None, BOTH),
        lead,
    )
    return jax.shard_map(shards, mesh=mesh, in_specs=placed, out_specs=lead, check_vma=False)
```

time: 382 us -> 144 us (0.38)
  waiting for transfers between devices: 166 us -> 25.4 us
  blocking collectives: 119 us -> 51.7 us
  other arithmetic: 27.9 us -> 2.8 us
  between operations: 13.7 us -> 0.9 us
  Pallas kernels: 0 us -> 12.6 us
  matrix products: 17.4 us -> 8.28 us
    all_gather x1 -> x0, waiting for transfers between devices: 135 us -> none  [carried_in(): gathered = jax.tree.map(lambda a: lax.all_gather(a, axis), part)]
    unnamed x1 -> x0, blocking collectives: 44 us -> none
    unnamed x29 -> x76, local copies, waits for them, and re-layouts: 1.81 us -> 28.5 us
    all_to_all x1 -> x2, blocking collectives: 75.1 us -> 51.7 us  [the longest x1 32 us: shards(): lax.all_to_all(sent.reshape(devices, half_rows, width), BOTH, 0, 0, tiled...]
    reduce_sum x3 -> x0, other arithmetic: 14.8 us -> none  [the longest x1 12.6 us: shards(): jnp.sum(picked.astype(jnp.float32) * scale_rows[:, :, None], axis=1)]
    gather x2 -> x0, local copies, waits for them, and re-layouts: 13.3 us -> none  [the longest x1 11 us: shards(): picked = out_padded[target].reshape(tok_rows, top_count, width)]
    pallas_call x0 -> x9, Pallas kernels: none -> 12.6 us  [the longest x1 4.06 us: shards(): pl.pallas_call(inside_kernel, grid=(2,), out_shape=[sds((tok, width), F32...]
    dot_general x5 -> x2, matrix products: 17.4 us -> 8.28 us  [the longest x1 6 us: shards(): part = jnp.dot(hidden, down_weight, preferred_element_type=F32).astype(BF16)]
  transfers between devices with their start and end apart: 4 -> 6, of which waited for: 4 -> 4; matrix products, arithmetic and copies ran while one was open for 5% -> 3% of each run, Pallas kernels for 0% -> 5%
where the time goes in v1:
time: 144 us; the launch traced here: 143 us
  blocking collectives  51.7 us (36%)
  local copies, waits for them, and re-layouts  33.5 us (23%)
  waiting for transfers between devices  25.4 us (18%)
  Pallas kernels  12.6 us (9%)
  matrix products  8.28 us (6%)
  starting transfers between devices  7.5 us (5%)
  other arithmetic  2.8 us (2%)
    all_to_all x1, blocking collectives, shards(): lax.all_to_all(sent.reshape(devices, half_rows, width), BOTH, 0, 0, tiled...  32 us
    unnamed x76, local copies, waits for them, and re-layouts  28.5 us
    all_to_all x1, blocking collectives, across_pairs(): return lax.all_to_all(x, BOTH, 0, 0, tiled=True, axis_index_groups=groups)  19.7 us
    all_to_all x1, waiting for transfers between devices, shards(): lax.all_to_all(summed.reshape(devices, half_rows, width), BOTH, 0, 0, til...  18.3 us
    ppermute x4, waiting for transfers between devices, partner(): return lax.ppermute(x, 'grp', [(i, i ^ 1) for i in range(count)])  7.09 us
    dot_general x1, matrix products, shards(): part = jnp.dot(hidden, down_weight, preferred_element_type=F32).astype(BF16)  6 us
    pallas_call x1, Pallas kernels, shards(): pl.pallas_call(inside_kernel, grid=(2,), out_shape=[sds((tok, width), F32...  4.06 us
    all_to_all x1, starting transfers between devices, shards(): lax.all_to_all(summed.reshape(devices, half_rows, width), BOTH, 0, 0, til...  3.62 us
  transfers between devices with their start and end apart: 6, of which 4 were waited for; matrix products, arithmetic and copies ran while one was open for 3% of the time, Pallas kernels for 5%

profile of v1, /device:TPU:0, one launch (start us, length us, event | category | flops | bytes accessed | tf_op | source)
XLA Modules:
  0.0 142.7 jit_solution(14302125199019859601)
XLA Ops:
  0.0 0.9 fusion.8
  0.9 0.7 maximum_select_fusion.decr_ref
  1.6 1.2 copy-done.3
  2.8 1.2 copy-done.5
  4.0 2.0 %states.1 = (f32[1032,128]{1,0:T(8,128)S(1)}, f32[1032,128]{1,0:T(8,128)S(1)}) custom-call(s32[1]{0:T(128)} %bitcast.k_ref, bf16[256,2048]{1,0:T(8,128)(2,1)S(1)} %copy-done.3, bf16[256,2048]{1,0:T(8,128)(2,1)S(1)} %copy-done.5, f32[16,256]{1,0:T(8,128)S(1)} %maximum_select_fusion.decr_ref), custom_call_target="tpu_custom_call" | custom-call | flops 134217728 | bytes 3145728 | tf_op jit(solution)/shard_map/states/pallas_call | solution.py:263
  6.0 0.0 copy-start.34
  6.0 0.0 copy-start.32
  6.0 0.0 copy-start.33
  6.1 0.0 copy-start.4
  6.1 0.0 copy-start.22
  6.1 0.1 collective-permute-start
  6.2 1.9 %collective-permute-done.recv_ref = f32[1032,128]{1,0:T(8,128)S(1)} collective-permute-done((f32[1032,128]{1,0:T(8,128)S(1)}, f32[1032,128]{1,0:T(8,128)S(1)}, u32[]{:S(2)}, u32[]{:S(2)}) %collective-permute-start) | collective-permute-done | bytes 528416 | tf_op jit(solution)/shard_map/ppermute | solution.py:56
  8.1 0.2 pair.1
  8.3 0.5 copy-done.11
  8.9 0.8 copy-done.9
  9.7 19.7 %all_to_all.20.in_ref = bf16[16,80,128]{2,1,0:T(8,128)(2,1)S(1)} all-to-all(bf16[16,80,128]{2,1,0:T(8,128)(2,1)S(1)} %pair.1), channel_id=1, replica_groups={{0,2,4,6,8,10,12,14,16,18,20,22,24,26,28,30},{1,3,5,7,9,11,13,15,17,19,..., dimensions={0} | all-to-all | bytes 655360 | tf_op jit(solution)/shard_map/all_to_all | solution.py:62
  29.4 0.1 scan.1
  29.5 0.7 copy-done.21
  30.2 3.5 %all-to-all-start.1 = ((bf16[16,64,128]{2,1,0:T(8,128)(2,1)}), bf16[16,64,128]{2,1,0:T(8,128)(2,1)S(1)}, u32[]{:S(2)}, u32[]{:S(2)}) async-start(bf16[16,64,128]{2,1,0:T(8,128)(2,1)} %copy-done.21), calls=%async_computation.1 | async-start | bytes 524288 | tf_op jit(solution)/shard_map/all_to_all | solution.py:62
  33.7 0.7 iota_reduce_fusion
  35.1 0.8 copy.16.ids_ref
  35.9 0.8 copy.17.wts_ref
  36.6 0.8 copy.18.live_ref
  37.5 0.9 copy-done.25
  38.4 0.9 copy-done.26
  39.3 0.9 copy-done.27
  40.2 1.0 route.1
  41.2 0.6 copy-done.23
  41.8 0.7 copy-done.30
  42.5 1.2 copy-done.6
  43.7 1.2 copy-done.16
  45.0 4.1 %inside.1 = (f32[256,2048]{1,0:T(8,128)S(1)}, bf16[256,2048]{1,0:T(8,128)(2,1)S(1)}) custom-call(f32[16,256]{1,0:T(8,128)S(1)} %copy-done.22, bf16[256,2048]{1,0:T(8,128)(2,1)S(1)} %copy-done.16, bf16[256,2048]{1,0:T(8,128)(2,1)S(1)} %copy-done.4, bf16[256,2048]{1,0:T(8,128)(2,1)S(1)} %copy-done.6), custom_call_target="tpu_custom_call" | custom-call | flops 536870912 | bytes 6291456 | tf_op jit(solution)/shard_map/inside/pallas_call | solution.py:302
  49.0 0.0 copy-start.14
  49.0 1.0 copy-done.14
  50.0 1.3 copy-done.7
  51.4 0.7 copy-done.19
  52.1 1.0 copy-done.10
  53.2 1.0 copy-done.12
  54.2 0.9 copy-done.20
  55.1 0.3 split.1
  55.5 0.1 collective-permute-start.1
  55.5 0.8 dynamic-slice_convert_fusion.disp_ref
  56.3 1.1 constant_dynamic-slice_fusion
  57.5 0.9 rows.1
  58.3 32.0 %all_to_all.21 = bf16[32,8,2048]{2,1,0:T(8,128)(2,1)S(1)} all-to-all(bf16[32,8,2048]{2,1,0:T(8,128)(2,1)S(1)} %bitcast.14), channel_id=1, replica_groups=mesh['seq'=8,'grp'=4] {'seq','grp'}, dimensions={0} | all-to-all | bytes 2097152 | tf_op jit(solution)/shard_map/all_to_all | solution.py:345
  90.3 2.7 %collective-permute-done.2 = bf16[256,2048]{1,0:T(8,128)(2,1)S(1)} collective-permute-done((bf16[256,2048]{1,0:T(8,128)(2,1)S(1)}, bf16[256,2048]{1,0:T(8,128)(2,1)S(1)}, u32[]{:S(2)}, u32[]{:S(2)}) %collective-permute-start.2) | collective-permute-done | bytes 1048608 | tf_op jit(solution)/shard_map/ppermute | solution.py:56
  93.0 1.0 copy-done.36
  94.0 2.3 %fusion = f32[512,512]{1,0:T(8,128)} fusion(bf16[2048,512]{1,0:T(8,128)(2,1)S(1)} %copy-done.35, bf16[256,2048]{1,0:T(8,128)(2,1)S(1)} %collective-permute-done.2, bf16[256,2048]{1,0:T(8,128)(2,1)S(1)} %bitcast.20), kind=kOutput, calls=%fused_computation.3 | convolution fusion | flops 1077936128 | bytes 5242880 | tf_op jit(solution)/shard_map/dot_general | solution.py:364
  96.3 6.0 %convolution_convert_fusion = bf16[512,2048]{1,0:T(8,128)(2,1)} fusion(bf16[512,2048]{1,0:T(8,128)(2,1)S(1)} %copy-done, f32[512,512]{1,0:T(8,128)} %fusion, bf16[2048,512]{1,0:T(8,128)(2,1)} %param.23, bf16[256,2048]{1,0:T(8,128)(2,1)} %copy-done.36, bf16[256,2048]{1,0:T(8,128)(2,1)S(1)} %bitcast.21), kind=kOutput, calls=%fused_computation | convolution fusion | flops 2154299392 | bytes 9437184 | tf_op jit(solution)/shard_map/dot_general | solution.py:366
  102.3 1.4 %slice.17 = bf16[256,2048]{1,0:T(8,128)(2,1)S(1)} slice(bf16[512,2048]{1,0:T(8,128)(2,1)} %convolution_convert_fusion), slice={[256:512], [0:2048]} | slice | bytes 2097152 | tf_op jit(solution)/shard_map/slice | solution.py:368
  103.7 0.2 collective-permute-start.3
  103.9 2.5 %collective-permute-done.3 = bf16[256,2048]{1,0:T(8,128)(2,1)S(1)} collective-permute-done((bf16[256,2048]{1,0:T(8,128)(2,1)S(1)}, bf16[256,2048]{1,0:T(8,128)(2,1)S(1)}, u32[]{:S(2)}, u32[]{:S(2)}) %collective-permute-start.3) | collective-permute-done | bytes 1048608 | tf_op jit(solution)/shard_map/ppermute | solution.py:56
  106.5 1.4 fusion.2
  107.8 3.6 %all-to-all-start.3 = ((bf16[32,8,2048]{2,1,0:T(8,128)(2,1)}), bf16[32,8,2048]{2,1,0:T(8,128)(2,1)S(1)}, u32[]{:S(2)}, u32[]{:S(2)}) async-start(bf16[32,8,2048]{2,1,0:T(8,128)(2,1)} %fusion.2), calls=%async_computation.3 | async-start | bytes 2097152 | tf_op jit(solution)/shard_map/all_to_all | solution.py:370
  111.5 1.6 %copy-done.8 = f32[256,2048]{1,0:T(8,128)S(1)} copy-done((f32[256,2048]{1,0:T(8,128)S(1)}, f32[256,2048]{1,0:T(8,128)}, u32[]{:S(2)}) %copy-start.8) | copy-done | bytes 2097176
  113.1 1.2 copy-done.13
  114.3 1.2 copy-done.15
  115.5 0.9 copy-done.18
  116.5 1.5 %mixed.1.mixed_ref = f32[256,2048]{1,0:T(8,128)S(1)} custom-call(s32[1]{0:T(128)} %bitcast.k_ref, bf16[256,2048]{1,0:T(8,128)(2,1)S(1)} %copy-done.15, f32[256,2048]{1,0:T(8,128)S(1)} %copy-done.8, bf16[256,2048]{1,0:T(8,128)(2,1)S(1)} %copy-done.13, bf16[1024,128]{1,0:T(8,128)(2,1)S(1)} %get-tuple-element.19.keep_ref, bf16[1024,128]{1,0:T(8,128)(2,1)S(1)} %copy-done.18, ...), custom_call_target="tpu_custom_call" | custom-call | flops 134217728 | bytes 7340032 | tf_op jit(solution)/shard_map/mixed/pallas_call | solution.py:349
  118.0 1.3 copy-done.1
  119.4 18.3 %all-to-all-done.3 = bf16[32,8,2048]{2,1,0:T(8,128)(2,1)S(1)} async-done(((bf16[32,8,2048]{2,1,0:T(8,128)(2,1)}), bf16[32,8,2048]{2,1,0:T(8,128)(2,1)S(1)}, u32[]{:S(2)}, u32[]{:S(2)}) %all-to-all-start.3) | async-done | bytes 1048608 | tf_op jit(solution)/shard_map/all_to_all | solution.py:370
  137.7 1.6 %copy-done.2 = f32[256,2048]{1,0:T(8,128)S(1)} copy-done((f32[256,2048]{1,0:T(8,128)S(1)}, f32[256,2048]{1,0:T(8,128)}, u32[]{:S(2)}) %copy-start.2) | copy-done | bytes 2097176
  139.3 0.9 copy-done.24
  140.2 2.5 %final.1 = bf16[256,2048]{1,0:T(8,128)(2,1)} custom-call(f32[256,2048]{1,0:T(8,128)S(1)} %copy-done.2, bf16[256,256]{1,0:T(8,128)(2,1)S(1)} %get-tuple-element.21.chi_ref, bf16[256,256]{1,0:T(8,128)(2,1)S(1)} %copy-done.24, bf16[256,2048]{1,0:T(8,128)(2,1)S(1)} %bitcast.13), custom_call_target="tpu_custom_call" | custom-call | tf_op jit(solution)/shard_map/final/pallas_call | solution.py:376
  (46 shorter events, 0.1 us)
Async XLA Ops:
  0.0 96.3 %copy-start = (bf16[512,2048]{1,0:T(8,128)(2,1)S(1)}, bf16[512,2048]{1,0:T(8,128)(2,1)}, u32[]{:S(2)}) copy-start(bf16[512,2048]{1,0:T(8,128)(2,1)} %param.25) | copy-start | bytes 6291460
  1.6 1.2 copy-start.3
  2.8 1.2 copy-start.5
  6.0 27.7 %copy-start.34 = (s32[256]{0:T(256)S(1)}, s32[256]{0:T(256)}, u32[]{:S(2)}) copy-start(s32[256]{0:T(256)} %param.22) | copy-start | bytes 3076
  6.0 29.0 %copy-start.32 = (s32[256,8]{0,1:T(8,128)S(1)}, s32[256,8]{0,1:T(8,128)}, u32[]{:S(2)}) copy-start(s32[256,8]{0,1:T(8,128)} %param.20) | copy-start | bytes 24580
  6.0 29.8 %copy-start.33 = (f32[256,8]{0,1:T(8,128)S(1)}, f32[256,8]{0,1:T(8,128)}, u32[]{:S(2)}) copy-start(f32[256,8]{0,1:T(8,128)} %param.21) | copy-start | bytes 24580
  6.1 36.4 %copy-start.4 = (bf16[256,2048]{1,0:T(8,128)(2,1)S(1)}, bf16[256,2048]{1,0:T(8,128)(2,1)}, u32[]{:S(2)}) copy-start(bf16[256,2048]{1,0:T(8,128)(2,1)} %key_ref.3) | copy-start | bytes 3145732
  6.1 36.4 %copy-start.22 = (f32[16,256]{1,0:T(8,128)S(1)}, f32[16,256]{1,0:T(8,128)}, u32[]{:S(2)}) copy-start(f32[16,256]{1,0:T(8,128)} %dec_ref.1) | copy-start | bytes 49156
  6.1 2.0 %collective-permute-start = (f32[1032,128]{1,0:T(8,128)S(1)}, f32[1032,128]{1,0:T(8,128)S(1)}, u32[]{:S(2)}, u32[]{:S(2)}) collective-permute-start(f32[1032,128]{1,0:T(8,128)S(1)} %get-tuple-element.18), channel_id=1, source_target_pairs={{0,1},{1,0},{2,3},{3,2},{4,5},{5,4},{6,7},{7,6},{8,9},{9,8},{10,11... | collective-permute-start | bytes 1585160 | tf_op jit(solution)/shard_map/ppermute | solution.py:56
  8.1 0.8 copy-start.11
  8.9 0.8 copy-start.9
  29.5 0.7 copy-start.21
  30.2 21.2 %all-to-all-start.1 = ((bf16[16,64,128]{2,1,0:T(8,128)(2,1)}), bf16[16,64,128]{2,1,0:T(8,128)(2,1)S(1)}, u32[]{:S(2)}, u32[]{:S(2)}) async-start(bf16[16,64,128]{2,1,0:T(8,128)(2,1)} %copy-done.21), calls=%async_computation.1 | async-start | bytes 524288 | tf_op jit(solution)/shard_map/all_to_all | solution.py:62
  37.5 0.9 copy-start.25
  38.4 0.9 copy-start.26
  39.3 0.9 copy-start.27
  41.1 0.7 copy-start.23
  41.8 0.7 copy-start.30
  42.5 1.2 copy-start.6
  43.7 1.2 copy-start.16
  49.0 1.0 copy-start.14
  50.0 7.4 %copy-start.28 = (f32[2048]{0:T(1024)S(1)}, f32[2048]{0:T(1024)}, u32[]{:S(2)}) copy-start(f32[2048]{0:T(1024)} %param.18) | copy-start | bytes 24580
  50.0 7.4 %copy-start.29 = (f32[2048]{0:T(1024)S(1)}, f32[2048]{0:T(1024)}, u32[]{:S(2)}) copy-start(f32[2048]{0:T(1024)} %param.19) | copy-start | bytes 24580
  50.0 1.4 copy-start.7
  51.4 0.7 copy-start.19
  52.1 1.0 copy-start.10
  53.2 1.0 copy-start.12
  54.2 0.9 copy-start.20
  55.5 1.9 %collective-permute-start.1 = (bf16[1024,128]{1,0:T(8,128)(2,1)S(1)}, bf16[1024,128]{1,0:T(8,128)(2,1)S(1)}, u32[]{:S(2)}, u32[]{:S(2)}) collective-permute-start(bf16[1024,128]{1,0:T(8,128)(2,1)S(1)} %get-tuple-element.20), channel_id=1, source_target_pairs={{0,1},{1,0},{2,3},{3,2},{4,5},{5,4},{6,7},{7,6},{8,9},{9,8},{10,11... | collective-permute-start | bytes 786440 | tf_op jit(solution)/shard_map/ppermute | solution.py:56
  57.4 32.9 %copy-start.17 = (bf16[1024,128]{1,0:T(8,128)(2,1)}, bf16[1024,128]{1,0:T(8,128)(2,1)S(1)}, u32[]{:S(2)}) copy-start(bf16[1024,128]{1,0:T(8,128)(2,1)S(1)} %collective-permute-done.1.other_ref) | copy-start | bytes 786436
  57.4 36.6 %copy-start.35 = (bf16[2048,512]{1,0:T(8,128)(2,1)S(1)}, bf16[2048,512]{1,0:T(8,128)(2,1)}, u32[]{:S(2)}) copy-start(bf16[2048,512]{1,0:T(8,128)(2,1)} %param.24) | copy-start | bytes 6291460
  90.3 2.7 %collective-permute-start.2 = (bf16[256,2048]{1,0:T(8,128)(2,1)S(1)}, bf16[256,2048]{1,0:T(8,128)(2,1)S(1)}, u32[]{:S(2)}, u32[]{:S(2)}) collective-permute-start(bf16[256,2048]{1,0:T(8,128)(2,1)S(1)} %bitcast.19), channel_id=1, source_target_pairs={{0,1},{1,0},{2,3},{3,2},{4,5},{5,4},{6,7},{7,6},{8,9},{9,8},{10,11... | collective-permute-start | bytes 3145736 | tf_op jit(solution)/shard_map/ppermute | solution.py:56
  93.0 1.0 copy-start.36
  102.3 4.2 %copy-start.31 = (bf16[512,2048]{1,0:T(8,128)(2,1)S(1)}, bf16[512,2048]{1,0:T(8,128)(2,1)}, u32[]{:S(2)}) copy-start(bf16[512,2048]{1,0:T(8,128)(2,1)} %convolution_convert_fusion) | copy-start | bytes 6291460
  103.7 2.7 %collective-permute-start.3 = (bf16[256,2048]{1,0:T(8,128)(2,1)S(1)}, bf16[256,2048]{1,0:T(8,128)(2,1)S(1)}, u32[]{:S(2)}, u32[]{:S(2)}) collective-permute-start(bf16[256,2048]{1,0:T(8,128)(2,1)S(1)} %slice.17), channel_id=1, source_target_pairs={{0,1},{1,0},{2,3},{3,2},{4,5},{5,4},{6,7},{7,6},{8,9},{9,8},{10,11... | collective-permute-start | bytes 3145736 | tf_op jit(solution)/shard_map/ppermute | solution.py:56
  107.8 29.9 %all-to-all-start.3 = ((bf16[32,8,2048]{2,1,0:T(8,128)(2,1)}), bf16[32,8,2048]{2,1,0:T(8,128)(2,1)S(1)}, u32[]{:S(2)}, u32[]{:S(2)}) async-start(bf16[32,8,2048]{2,1,0:T(8,128)(2,1)} %fusion.2), calls=%async_computation.3 | async-start | bytes 2097152 | tf_op jit(solution)/shard_map/all_to_all | solution.py:370
  111.5 1.6 %copy-start.8 = (f32[256,2048]{1,0:T(8,128)S(1)}, f32[256,2048]{1,0:T(8,128)}, u32[]{:S(2)}) copy-start(f32[256,2048]{1,0:T(8,128)} %copy-done.7) | copy-start | bytes 6291460
  113.1 1.2 copy-start.13
  114.3 1.2 copy-start.15
  115.5 0.9 copy-start.18
  118.0 1.4 copy-start.1
  137.7 1.6 %copy-start.2 = (f32[256,2048]{1,0:T(8,128)S(1)}, f32[256,2048]{1,0:T(8,128)}, u32[]{:S(2)}) copy-start(f32[256,2048]{1,0:T(8,128)} %copy-done.1) | copy-start | bytes 6291460
  139.3 0.9 copy-start.24

commit v2 on v1

v2 whole, which is shorter than its diff:
```python
import functools

import jax
import jax.numpy as jnp
from jax import lax
from jax.experimental import pallas as pl
from jax.experimental.pallas import tpu as pltpu
from jax.sharding import PartitionSpec as P

CAP = 16
TAIL = 8
TAIL16 = 16
ATTN_EPS = 1e-05
NORM_EPS = 1e-06
BOTH = ("seq", "grp")
F32 = jnp.float32
BF16 = jnp.bfloat16
SMEM = pl.BlockSpec(memory_space=pltpu.SMEM)
HBM = pl.BlockSpec(memory_space=pltpu.HBM)
DMA = pltpu.SemaphoreType.DMA


def params(mb=60):
    return pltpu.CompilerParams(vmem_limit_bytes=mb * 1024 * 1024)


def full(x):
    return pl.BlockSpec(x.shape, lambda i, n=len(x.shape): (0,) * n)


def cost(flops, nbytes):
    return pl.CostEstimate(flops=flops, bytes_accessed=nbytes, transcendentals=0)


def mm(a, b, ca=1, cb=0):
    return lax.dot_general(a, b, (((ca,), (cb,)), ((), ())), preferred_element_type=F32)


def lower_tri(n):
    rows = lax.broadcasted_iota(jnp.int32, (n, n), 0)
    cols = lax.broadcasted_iota(jnp.int32, (n, n), 1)
    return rows >= cols


def running_cols(dec):
    tri = lower_tri(dec.shape[1]).astype(F32)
    return lax.dot_general(
        tri, dec, (((1,), (1,)), ((), ())), precision=lax.Precision.HIGHEST, preferred_element_type=F32
    )


def running_rows(dec):
    tri = lower_tri(dec.shape[1]).astype(F32)
    return lax.dot_general(
        dec, tri, (((1,), (1,)), ((), ())), precision=lax.Precision.HIGHEST, preferred_element_type=F32
    )


def partner(x):
    count = lax.axis_size("grp")
    return lax.ppermute(x, "grp", [(i, i ^ 1) for i in range(count)])


def across_pairs(x):
    count = lax.axis_size(BOTH)
    groups = [list(range(k, count, 2)) for k in range(2)]
    return lax.all_to_all(x, BOTH, 0, 0, tiled=True, axis_index_groups=groups)


def copy(src, dst, sems, n):
    c = pltpu.make_async_copy(src, dst, sems.at[n])
    c.start()
    return c


def states_kernel(k_ref, key_hbm, val_hbm, dec_hbm, own_hbm, send_hbm, key_ref, val_ref, dec_ref, own_ref, send_ref, sems):
    heads, tok = dec_ref.shape
    half = heads // 2
    hd = own_ref.shape[1]
    span = half * hd
    k = k_ref[0]
    get_dec = copy(dec_hbm, dec_ref, sems, 0)
    gets = []
    for n in range(2):
        cols = pl.ds(pl.multiple_of((k ^ 1 ^ n) * span, span), span)
        gets.append(copy(key_hbm.at[:, cols], key_ref.at[n], sems, 1 + 2 * n))
        gets.append(copy(val_hbm.at[:, cols], val_ref.at[n], sems, 2 + 2 * n))
    get_dec.wait()
    mine = dec_ref[pl.ds(pl.multiple_of(k * half, half), half), :]
    theirs = dec_ref[pl.ds(pl.multiple_of((1 - k) * half, half), half), :]
    run = running_cols(jnp.concatenate([mine, theirs], axis=0))
    total = run[tok - 1 : tok, :]
    fac = jnp.exp(total - run)
    tail = jnp.broadcast_to(jnp.pad(total, ((0, 0), (0, hd - heads))), (TAIL, hd))
    puts = []
    for n, dst, out, first in ((0, send_ref, send_hbm, half), (1, own_ref, own_hbm, 0)):
        gets[2 * n].wait()
        gets[2 * n + 1].wait()
        for j in range(half):
            cols = slice(j * hd, (j + 1) * hd)
            scaled = (key_ref[n, :, cols].astype(F32) * fac[:, first + j : first + j + 1]).astype(BF16)
            dst[cols, :] = mm(scaled, val_ref[n, :, cols], 0, 0)
        dst[span:, :] = tail
        puts.append(copy(dst, out, sems, 5 + n))
    for c in puts:
        c.wait()


def pair_kernel(k_ref, own_ref, recv_ref, out_ref, *, half, rows):
    hd = own_ref.shape[1]
    first = k_ref[0] == 0
    base = half * hd
    mine = own_ref[base : base + 1, :]
    theirs = recv_ref[base : base + 1, :]
    pieces = out_ref.shape[0]
    tail_row = lax.broadcasted_iota(jnp.int32, (TAIL16, hd), 0)
    for p in range(pieces):
        j = p * rows // hd
        mt = mine[:, j : j + 1]
        pt = theirs[:, half + j : half + j + 1]
        one = jnp.ones_like(mt)
        a = jnp.where(first, jnp.exp(pt), one)
        b = jnp.where(first, one, jnp.exp(mt))
        lo = p * rows
        chip = own_ref[lo : lo + rows, :] * a + recv_ref[lo : lo + rows, :] * b
        out_ref[p, 0:rows, :] = chip.astype(BF16)
        d = jnp.broadcast_to(jnp.exp(mt + pt), (TAIL16, hd))
        d0 = d.astype(BF16).astype(F32)
        d1 = (d - d0).astype(BF16).astype(F32)
        d2 = d - d0 - d1
        tail = jnp.where(tail_row == 0, d0, jnp.where(tail_row == 1, d1, jnp.where(tail_row == 2, d2, 0.0)))
        out_ref[p, rows : rows + TAIL16, :] = tail.astype(BF16)


def scan_kernel(in_ref, out_ref):
    count, rows, hd = out_ref.shape
    state = jnp.zeros((rows, hd), F32)
    for c in range(count):
        out_ref[c, :, :] = state.astype(BF16)
        tail = in_ref[c, rows : rows + TAIL16, :].astype(F32)
        d = tail[0:1, :] + tail[1:2, :] + tail[2:3, :]
        state = state * d + in_ref[c, 0:rows, :].astype(F32)


def split_kernel(k_ref, pref_ref, own_hbm, recv_hbm, keep_ref, give_ref, first_ref, sem, *, half):
    hd = first_ref.shape[1]
    even = k_ref[0] == 0
    base = half * hd

    @pl.when(even)
    def _():
        pltpu.make_async_copy(own_hbm, first_ref, sem).start()

    @pl.when(jnp.logical_not(even))
    def _():
        pltpu.make_async_copy(recv_hbm, first_ref, sem).start()

    pltpu.make_async_copy(own_hbm, first_ref, sem).wait()
    logs = first_ref[base : base + 1, :]
    for j in range(half):
        sl = slice(j * hd, (j + 1) * hd)
        d0 = jnp.exp(jnp.where(even, logs[:, j : j + 1], logs[:, half + j : half + j + 1]))
        before = pref_ref[sl, :].astype(F32)
        after = before * d0 + first_ref[sl, :]
        keep_ref[sl, :] = jnp.where(even, before, after).astype(BF16)
        give_ref[sl, :] = jnp.where(even, after, before).astype(BF16)


def inside_kernel(start_ref, dec_ref, q_ref, key_ref, val_ref, stream_ref, inside_ref, lifted_ref, ir_ref, lr_ref, sr_ref):
    heads, tok = dec_ref.shape
    hd = q_ref.shape[1] // heads
    dec = dec_ref[...]
    run_c = running_cols(dec)
    run_r = running_rows(dec)
    lift = jnp.exp(run_c)
    cut = tok // 2
    tri = lower_tri(cut)
    resp = ir_ref.shape[0]
    start = start_ref[0]
    picked = lax.broadcasted_iota(jnp.int32, (resp, tok), 0) + start
    pick = jnp.where(lax.broadcasted_iota(jnp.int32, (resp, tok), 1) == picked, 1.0, 0.0).astype(BF16)
    for h in range(heads):
        cols = slice(h * hd, (h + 1) * hd)
        q = q_ref[:, cols]
        kk = key_ref[:, cols]
        v = val_ref[:, cols]
        lifted = (q.astype(F32) * lift[:, h : h + 1]).astype(BF16)
        lifted_ref[:, cols] = lifted
        rc = run_c[:, h : h + 1]
        rr = run_r[h : h + 1, :]
        f_aa = jnp.where(tri, jnp.exp(rc[:cut] - rr[:, :cut]), 0.0)
        f_bb = jnp.where(tri, jnp.exp(rc[cut:] - rr[:, cut:]), 0.0)
        f_ba = jnp.exp(rc[cut:] - rr[:, :cut])
        w_aa = (mm(q[:cut], kk[:cut], 1, 1) * f_aa).astype(BF16)
        s_b = mm(q[cut:], kk, 1, 1)
        w_b = (s_b * jnp.concatenate([f_ba, f_bb], axis=1)).astype(BF16)
        inside_ref[:cut, cols] = mm(w_aa, v[:cut])
        inside_ref[cut:, cols] = mm(w_b, v)
    lr_ref[...] = mm(pick, lifted_ref[...]).astype(BF16)
    sr_ref[...] = mm(pick, stream_ref[...]).astype(BF16)
    rest = inside_ref[...]
    high = rest.astype(BF16)
    rest = rest - high.astype(F32)
    mid = rest.astype(BF16)
    low = (rest - mid.astype(F32)).astype(BF16)
    ir_ref[...] = mm(pick, high) + mm(pick, mid) + mm(pick, low)


def head_norm(att):
    return att * lax.rsqrt(jnp.mean(att * att, axis=-1, keepdims=True) + ATTN_EPS)


def rows_kernel(k_ref, lifted_ref, inside_ref, stream_ref, keep_ref, other_ref, again_ref, fgain_ref, disp_ref, sent_ref, mixed_ref):
    hd = keep_ref.shape[1]
    half = keep_ref.shape[0] // hd
    k = k_ref[0]
    rows, width = lifted_ref.shape
    for r in range(2 * half):
        side = r // half
        off = pl.multiple_of((side ^ k) * (half * hd) + (r % half) * hd, hd)
        cols = pl.ds(off, hd)
        src = keep_ref if side == 0 else other_ref
        att = inside_ref[:, cols] + mm(lifted_ref[:, cols], src[(r % half) * hd : (r % half + 1) * hd, :])
        mixed_ref[:, cols] = stream_ref[:, cols].astype(F32) + head_norm(att) * again_ref[:, cols]
    mixed = mixed_ref[...]
    scale = lax.rsqrt(jnp.mean(mixed * mixed, axis=-1, keepdims=True) + NORM_EPS)
    ffn = (mixed * scale * fgain_ref[...]).astype(BF16)
    sent_ref[...] = mm(disp_ref[...], ffn).astype(BF16)


def mixed_kernel(k_ref, lifted_ref, inside_ref, stream_ref, keep_ref, other_ref, again_ref, mixed_ref):
    hd = keep_ref.shape[1]
    half = keep_ref.shape[0] // hd
    mine = pl.program_id(0) == k_ref[0]
    for j in range(half):
        cols = slice(j * hd, (j + 1) * hd)
        st = jnp.where(mine, keep_ref[cols, :].astype(F32), other_ref[cols, :].astype(F32)).astype(BF16)
        att = inside_ref[:, cols] + mm(lifted_ref[:, cols], st)
        mixed_ref[:, cols] = stream_ref[:, cols].astype(F32) + head_norm(att) * again_ref[:, cols]


def route_kernel(start_ref, ids_ref, wts_ref, live_ref, disp_ref, chi_ref, clo_ref, *, experts):
    top, tok = ids_ref.shape
    slots, resp = disp_ref.shape
    live = live_ref[...] == 1
    e_row = lax.broadcasted_iota(jnp.int32, (experts, tok), 0)
    chosen = jnp.zeros((experts, tok), F32)
    weight = jnp.zeros((experts, tok), F32)
    for j in range(top):
        hit = (ids_ref[j : j + 1, :] == e_row) & live
        chosen = jnp.where(hit, 1.0, chosen)
        weight = jnp.where(hit, wts_ref[j : j + 1, :], weight)
    rows = lax.broadcasted_iota(jnp.int32, (tok, tok), 0)
    cols = lax.broadcasted_iota(jnp.int32, (tok, tok), 1)
    before = jnp.where(rows < cols, 1.0, 0.0).astype(BF16)
    place = mm(chosen.astype(BF16), before)
    place = jnp.where(chosen > 0.0, place, -1.0)
    s_row = lax.broadcasted_iota(jnp.int32, (slots, experts), 0)
    e_col = lax.broadcasted_iota(jnp.int32, (slots, experts), 1)
    spread = jnp.where(s_row // CAP == e_col, 1.0, 0.0).astype(BF16)
    slot_of = lax.broadcasted_iota(jnp.int32, (slots, tok), 0) % CAP
    hit = mm(spread, place.astype(BF16)) == slot_of.astype(F32)
    w_hi = weight.astype(BF16)
    w_lo = (weight - w_hi.astype(F32)).astype(BF16)
    picked = lax.broadcasted_iota(jnp.int32, (tok, resp), 1) + start_ref[0]
    pick = jnp.where(lax.broadcasted_iota(jnp.int32, (tok, resp), 0) == picked, 1.0, 0.0).astype(BF16)
    disp_ref[...] = mm(jnp.where(hit, 1.0, 0.0).astype(BF16), pick).astype(BF16)
    chi_ref[...] = jnp.where(hit, mm(spread, w_hi), 0.0).astype(BF16)
    clo_ref[...] = jnp.where(hit, mm(spread, w_lo), 0.0).astype(BF16)


def expert_kernel(x_hbm, g0, u0, d0, g1, u1, d1, out_hbm, gv, uv, dv, hid_ref, x_ref, out_ref, sems, *, step):
    width, units = g0.shape
    cuts = range(0, units, step)
    gets = [copy(x_hbm, x_ref, sems, 0)]
    for n, (g, u) in enumerate(((g0, u0), (g1, u1))):
        for c in cuts:
            cols = pl.ds(c, step)
            gets.append(copy(g.at[:, cols], gv.at[n, :, cols], sems, len(gets)))
            gets.append(copy(u.at[:, cols], uv.at[n, :, cols], sems, len(gets)))
    for n, d in enumerate((d0, d1)):
        gets.append(copy(d, dv.at[n], sems, len(gets)))
    gets[0].wait()
    at = 1
    block = min(256, x_ref.shape[0])
    blocks = range(0, x_ref.shape[0], block)
    for n in range(2):
        for c in cuts:
            gets[at].wait()
            gets[at + 1].wait()
            at += 2
            for r in blocks:
                x = x_ref[r : r + block, :]
                gate = mm(x, gv[n, :, c : c + step])
                up = mm(x, uv[n, :, c : c + step])
                hid_ref[n, r : r + block, c : c + step] = (gate / (1.0 + jnp.exp(-gate)) * up).astype(BF16)
    gets[at].wait()
    gets[at + 1].wait()
    puts = []
    for r in blocks:
        for c in range(0, width, 256):
            cols = slice(c, c + 256)
            p0 = mm(hid_ref[0, r : r + block, :], dv[0, :, cols]).astype(BF16).astype(F32)
            p1 = mm(hid_ref[1, r : r + block, :], dv[1, :, cols]).astype(BF16).astype(F32)
            out_ref[r : r + block, cols] = (p0 + p1).astype(BF16)
        done = pl.ds(r, block)
        puts.append(copy(out_ref.at[done], out_hbm.at[done], sems, len(gets) + len(puts)))
    for c in puts:
        c.wait()


def final_kernel(mixed_ref, chi_ref, clo_ref, back_ref, out_ref):
    back = back_ref[...]
    moe = mm(chi_ref[...], back, 0, 0) + mm(clo_ref[...], back, 0, 0)
    out_ref[...] = (mixed_ref[...] + moe).astype(BF16)


def shards(
    stream_in,
    query_rows,
    key_rows,
    value_rows,
    log_decay,
    attn_gain,
    ffn_gain,
    expert_ids,
    route_weights,
    response_mask,
    gate_weight,
    up_weight,
    down_weight,
):
    tok, width = stream_in.shape
    heads = log_decay.shape[0]
    hd = width // heads
    half = heads // 2
    devices = lax.axis_size(BOTH)
    pairs = devices // 2
    experts = devices // 2
    slots = experts * CAP
    top = expert_ids.shape[1]
    resp = min(tok, slots // top)
    rows = half * hd // pairs
    me = lax.axis_index(BOTH)
    bit = (me & 1).reshape(1).astype(jnp.int32)
    sds = jax.ShapeDtypeStruct

    span = half * hd
    own, send = pl.pallas_call(
        states_kernel,
        out_shape=[sds((span + TAIL, hd), F32)] * 2,
        in_specs=[SMEM, HBM, HBM, HBM],
        out_specs=[HBM, HBM],
        scratch_shapes=[pltpu.VMEM((2, tok, span), BF16)] * 2
        + [pltpu.VMEM((heads, tok), F32)]
        + [pltpu.VMEM((span + TAIL, hd), F32)] * 2
        + [DMA((7,))],
        compiler_params=params(),
        cost_estimate=cost(2 * tok * width * hd, 3 << 20),
        name="states",
    )(bit, key_rows, value_rows, log_decay)
    recv = partner(send)
    recv, gate_own, up_own, down_own = lax.optimization_barrier((recv, gate_weight, up_weight, down_weight))
    gate_other, up_other, down_other = partner(gate_own), partner(up_own), partner(down_own)
    packed = pl.pallas_call(
        functools.partial(pair_kernel, half=half, rows=rows),
        grid=(1,),
        out_shape=sds((pairs, rows + TAIL16, hd), BF16),
        in_specs=[SMEM, full(own), full(recv)],
        out_specs=full(sds((pairs, rows + TAIL16, hd), BF16)),
        compiler_params=params(8),
        name="pair",
    )(bit, own, recv)
    gathered = across_pairs(packed)
    col = pl.BlockSpec((tok, width // 2), lambda i: (0, i))
    wcol = pl.BlockSpec((resp, width // 2), lambda i: (0, i))
    start = jnp.minimum(jnp.argmax(response_mask), tok - resp).astype(jnp.int32).reshape(1)
    routing = (expert_ids.T, route_weights.T, response_mask.reshape(1, tok))
    tables = [sds((slots, resp), BF16), sds((slots, tok), BF16), sds((slots, tok), BF16)]
    disp, chi, clo = pl.pallas_call(
        functools.partial(route_kernel, experts=experts),
        grid=(1,),
        out_shape=tables,
        in_specs=[SMEM] + [full(a) for a in routing],
        out_specs=[full(a) for a in tables],
        compiler_params=params(),
        cost_estimate=cost(8 * tok * tok * slots, 1 << 20),
        name="route",
    )(start, *routing)
    inside, lifted, inside_r, lifted_r, stream_r = pl.pallas_call(
        inside_kernel,
        grid=(2,),
        out_shape=[
            sds((tok, width), F32),
            sds((tok, width), BF16),
            sds((resp, width), F32),
            sds((resp, width), BF16),
            sds((resp, width), BF16),
        ],
        in_specs=[SMEM, pl.BlockSpec((half, tok), lambda i: (i, 0)), col, col, col, col],
        out_specs=[col, col, wcol, wcol, wcol],
        compiler_params=params(),
        cost_estimate=cost(4 * tok * tok * width, 6 << 20),
        name="inside",
    )(start, log_decay, query_rows, key_rows, value_rows, stream_in)
    gathered, inside, lifted, inside_r, lifted_r, stream_r, disp, chi, clo = lax.optimization_barrier(
        (gathered, inside, lifted, inside_r, lifted_r, stream_r, disp, chi, clo)
    )
    scanned = pl.pallas_call(
        scan_kernel,
        grid=(1,),
        out_shape=sds((pairs, rows, hd), BF16),
        in_specs=[full(gathered)],
        out_specs=full(sds((pairs, rows, hd), BF16)),
        compiler_params=params(8),
        name="scan",
    )(gathered)
    pref = across_pairs(scanned).reshape(half * hd, hd)
    keep, give = pl.pallas_call(
        functools.partial(split_kernel, half=half),
        grid=(1,),
        out_shape=[sds((half * hd, hd), BF16)] * 2,
        in_specs=[SMEM, full(pref), HBM, HBM],
        out_specs=[full(pref)] * 2,
        scratch_shapes=[pltpu.VMEM((span + TAIL, hd), F32), DMA],
        compiler_params=params(8),
        name="split",
    )(bit, pref, own, recv)
    other = partner(give)

    again = attn_gain.reshape(1, width)
    window = (lifted_r, inside_r, stream_r, keep, other, again, ffn_gain.reshape(1, width), disp)
    sent = pl.pallas_call(
        rows_kernel,
        grid=(1,),
        out_shape=sds((slots, width), BF16),
        in_specs=[SMEM] + [full(a) for a in window],
        out_specs=full(sds((slots, width), BF16)),
        scratch_shapes=[pltpu.VMEM((resp, width), F32)],
        compiler_params=params(8),
        name="rows",
    )(bit, *window)
    half_rows = CAP // 2
    arrived = lax.all_to_all(sent.reshape(devices, half_rows, width), BOTH, 0, 0, tiled=True)

    gain_col = pl.BlockSpec((1, width // 2), lambda i: (0, i))
    state_all = pl.BlockSpec((half * hd, hd), lambda i: (0, 0))
    mixed = pl.pallas_call(
        mixed_kernel,
        grid=(2,),
        out_shape=sds((tok, width), F32),
        in_specs=[SMEM, col, col, col, state_all, state_all, gain_col],
        out_specs=col,
        compiler_params=params(32),
        cost_estimate=cost(2 * tok * width * hd, 7 << 20),
        name="mixed",
    )(bit, lifted, inside, stream_in, keep, other, again)

    arrived, mixed = lax.optimization_barrier((arrived, mixed))
    units = gate_weight.shape[1]
    step = min(256, units)
    many = devices * half_rows
    done = pl.pallas_call(
        functools.partial(expert_kernel, step=step),
        out_shape=sds((many, width), BF16),
        in_specs=[HBM] * 7,
        out_specs=HBM,
        scratch_shapes=[pltpu.VMEM((2, width, units), BF16)] * 2
        + [pltpu.VMEM((2, units, width), BF16), pltpu.VMEM((2, many, units), BF16)]
        + [pltpu.VMEM((many, width), BF16)] * 2
        + [DMA((4 * (units // step) + 3 + many // min(256, many),))],
        compiler_params=params(48),
        cost_estimate=cost(12 * many * width * units, 14 << 20),
        name="expert",
    )(arrived.reshape(many, width), gate_own, up_own, down_own, gate_other, up_other, down_other)
    back = lax.all_to_all(done.reshape(devices, half_rows, width), BOTH, 0, 0, tiled=True)
    back = back.reshape(slots, width)

    steps = 4
    fcol = pl.BlockSpec((tok, width // steps), lambda i: (0, i))
    whole = pl.BlockSpec((slots, tok), lambda i: (0, 0))
    return pl.pallas_call(
        final_kernel,
        grid=(steps,),
        out_shape=sds((tok, width), BF16),
        in_specs=[fcol, whole, whole, pl.BlockSpec((slots, width // steps), lambda i: (0, i))],
        out_specs=fcol,
        compiler_params=params(),
        name="final",
    )(mixed, chi, clo, back)


def solution(mesh):
    lead = P(BOTH, None)
    placed = (
        lead,
        lead,
        lead,
        lead,
        P(None, BOTH),
        P(),
        P(),
        lead,
        lead,
        P(BOTH),
        P(None, BOTH),
        P(None, BOTH),
        lead,
    )
    return jax.shard_map(shards, mesh=mesh, in_specs=placed, out_specs=lead, check_vma=False)
```

time: 144 us -> 117 us (0.81)
  local copies, waits for them, and re-layouts: 33.5 us -> 5.22 us
  Pallas kernels: 12.6 us -> 28.2 us
  matrix products: 8.28 us -> 0 us
  blocking collectives: 51.7 us -> 44.6 us
  starting transfers between devices: 7.5 us -> 12.5 us
  other arithmetic: 2.8 us -> 0.67 us
    unnamed x76 -> x26, local copies, waits for them, and re-layouts: 28.5 us -> 5.22 us
    pallas_call x6 -> x7, Pallas kernels: 4.45 us -> 15.6 us  [the longest x1 6.22 us: shards(): pl.pallas_call(functools.partial(expert_kernel, step=step), out_shape=sds...]
    dot_general x2 -> x0, matrix products: 8.28 us -> none  [the longest x1 6 us: shards(): part = jnp.dot(hidden, down_weight, preferred_element_type=F32).astype(BF16)]
    all_to_all x1, blocking collectives: 19.7 us -> 14.9 us  [across_pairs(): return lax.all_to_all(x, BOTH, 0, 0, tiled=True, axis_index_groups=groups)]
    ppermute x4 -> x5, waiting for transfers between devices: 7.09 us -> 2.27 us  [partner(): return lax.ppermute(x, 'grp', [(i, i ^ 1) for i in range(count)])]
    all_to_all x1, starting transfers between devices: 3.53 us -> 8.24 us  [across_pairs(): return lax.all_to_all(x, BOTH, 0, 0, tiled=True, axis_index_groups=groups)]
    pallas_call x1, Pallas kernels: 4.06 us -> 6.7 us  [shards(): pl.pallas_call(inside_kernel, grid=(2,), out_shape=[sds((tok, width), F32...]
    slice x2 -> x0, local copies, waits for them, and re-layouts: 2.31 us -> none  [the longest x1 1.44 us: shards(): added = partner(part[count:])]
  transfers between devices with their start and end apart: 6 -> 7, of which waited for: 4 -> 4; matrix products, arithmetic and copies ran while one was open for 3% -> 1% of each run, Pallas kernels for 5% -> 10%
where the time goes in v2:
time: 117 us; the launch traced here: 116 us
  blocking collectives  44.6 us (38%)
  Pallas kernels  28.2 us (24%)
  waiting for transfers between devices  24.4 us (21%)
  starting transfers between devices  12.5 us (11%)
  local copies, waits for them, and re-layouts  5.22 us (4%)
    all_to_all x1, blocking collectives, shards(): lax.all_to_all(done.reshape(devices, half_rows, width), BOTH, 0, 0, tiled...  29.7 us
    all_to_all x1, waiting for transfers between devices, shards(): lax.all_to_all(sent.reshape(devices, half_rows, width), BOTH, 0, 0, tiled...  20.5 us
    all_to_all x1, blocking collectives, across_pairs(): return lax.all_to_all(x, BOTH, 0, 0, tiled=True, axis_index_groups=groups)  14.9 us
    all_to_all x1, starting transfers between devices, across_pairs(): return lax.all_to_all(x, BOTH, 0, 0, tiled=True, axis_index_groups=groups)  8.24 us
    pallas_call x1, Pallas kernels, shards(): pl.pallas_call(inside_kernel, grid=(2,), out_shape=[sds((tok, width), F32...  6.7 us
    pallas_call x1, Pallas kernels, shards(): pl.pallas_call(functools.partial(expert_kernel, step=step), out_shape=sds...  6.22 us
    unnamed x26, local copies, waits for them, and re-layouts  5.22 us
    pallas_call x1, Pallas kernels, shards(): pl.pallas_call(final_kernel, grid=(steps,), out_shape=sds((tok, width), B...  4.41 us
  transfers between devices with their start and end apart: 7, of which 4 were waited for; matrix products, arithmetic and copies ran while one was open for 1% of the time, Pallas kernels for 10%

profile of v2, /device:TPU:0, one launch (start us, length us, event | category | flops | bytes accessed | tf_op | source)
XLA Modules:
  0.0 116.4 jit_solution(12095742915872544607)
XLA Ops:
  0.0 0.0 copy-start.12
  0.0 4.1 %states.1 = (f32[1032,128]{1,0:T(8,128)}, f32[1032,128]{1,0:T(8,128)}) custom-call(s32[1]{0:T(128)} %bitcast.k_ref, bf16[256,2048]{1,0:T(8,128)(2,1)} %key_ref.1, bf16[256,2048]{1,0:T(8,128)(2,1)} %val_ref.1, f32[16,256]{1,0:T(8,128)} %dec_ref.1), custom_call_target="tpu_custom_call" | custom-call | flops 134217728 | bytes 3145728 | tf_op jit(solution)/shard_map/states/pallas_call | solution.py:349
  4.1 0.5 collective-permute-start
  4.7 1.8 %collective-permute-done.recv_ref.recv_hbm = f32[1032,128]{1,0:T(8,128)S(1)} collective-permute-done((f32[1032,128]{1,0:T(8,128)}, f32[1032,128]{1,0:T(8,128)S(1)}, u32[]{:S(2)}, u32[]{:S(2)}) %collective-permute-start) | collective-permute-done | bytes 528416 | tf_op jit(solution)/shard_map/ppermute | solution.py:61
  6.4 0.0 copy-start.2
  6.4 1.0 copy-done.2
  7.5 1.0 pair.1
  8.4 8.2 %all-to-all-start = ((bf16[16,80,128]{2,1,0:T(8,128)(2,1)}), bf16[16,80,128]{2,1,0:T(8,128)(2,1)S(1)}, u32[]{:S(2)}, u32[]{:S(2)}) async-start(bf16[16,80,128]{2,1,0:T(8,128)(2,1)} %pair.1), calls=%async_computation | async-start | bytes 655360 | tf_op jit(solution)/shard_map/all_to_all | solution.py:67
  16.7 0.0 copy-done.12
  16.7 0.7 iota_reduce_fusion
  18.0 2.0 %route.1 = (bf16[256,32]{1,0:T(8,128)(2,1)}, bf16[256,256]{1,0:T(8,128)(2,1)}, bf16[256,256]{1,0:T(8,128)(2,1)}) custom-call(s32[1]{0:T(128)} %bitcast.1.start_ref, s32[8,256]{1,0:T(8,128)} %bitcast.20, f32[8,256]{1,0:T(8,128)} %bitcast.21, s32[1,256]{1,0:T(1,128)} %bitcast.19), custom_call_target="tpu_custom_call" | custom-call | flops 134217728 | bytes 1048576 | tf_op jit(solution)/shard_map/route/pallas_call | solution.py:380
  20.0 0.0 copy-start.3
  20.0 6.7 %inside.1 = (f32[256,2048]{1,0:T(8,128)}, bf16[256,2048]{1,0:T(8,128)(2,1)}, f32[32,2048]{1,0:T(8,128)}, bf16[32,2048]{1,0:T(8,128)(2,1)}, bf16[32,2048]{1,0:T(8,128)(2,1)}) custom-call(s32[1]{0:T(128)} %bitcast.1.start_ref, f32[16,256]{1,0:T(8,128)} %dec_ref.1, bf16[256,2048]{1,0:T(8,128)(2,1)} %q_ref.1, bf16[256,2048]{1,0:T(8,128)(2,1)} %key_ref.1, ...), custom_call_target="tpu_custom_call" | custom-call | flops 536870912 | bytes 6291456 | tf_op jit(solution)/shard_map/inside/pallas_call | solution.py:390
  26.7 0.0 copy-start.6
  26.7 0.0 copy-start.7
  26.7 0.0 copy-start.8
  26.7 0.0 copy-start.9
  26.7 0.0 copy-start.10
  26.7 0.0 copy-start.11
  26.7 1.6 %all-to-all-done.in_ref = bf16[16,80,128]{2,1,0:T(8,128)(2,1)S(1)} async-done(((bf16[16,80,128]{2,1,0:T(8,128)(2,1)}), bf16[16,80,128]{2,1,0:T(8,128)(2,1)S(1)}, u32[]{:S(2)}, u32[]{:S(2)}) %all-to-all-start) | async-done | bytes 327712 | tf_op jit(solution)/shard_map/all_to_all | solution.py:67
  28.3 0.1 scan.1
  28.4 14.9 %all_to_all.20 = bf16[16,64,128]{2,1,0:T(8,128)(2,1)S(1)} all-to-all(bf16[16,64,128]{2,1,0:T(8,128)(2,1)S(1)} %scan.1), channel_id=1, replica_groups={{0,2,4,6,8,10,12,14,16,18,20,22,24,26,28,30},{1,3,5,7,9,11,13,15,17,19,..., dimensions={0} | all-to-all | bytes 524288 | tf_op jit(solution)/shard_map/all_to_all | solution.py:67
  43.3 0.0 copy-done.3
  43.3 0.3 split.1
  43.6 0.1 collective-permute-start.1
  43.7 0.5 collective-permute-start.2
  44.2 0.1 collective-permute-start.3
  44.3 0.4 collective-permute-start.4
  44.7 0.5 collective-permute-done.1.other_ref
  45.2 0.0 copy-done.6
  45.2 0.0 copy-done.7
  45.2 0.0 copy-done.8
  45.2 0.0 copy-done.9
  45.2 0.0 copy-done.10
  45.2 0.0 copy-done.11
  45.2 0.0 copy-start.1
  45.3 1.9 %rows.1 = bf16[256,2048]{1,0:T(8,128)(2,1)} custom-call(s32[1]{0:T(128)} %bitcast.k_ref, bf16[32,2048]{1,0:T(8,128)(2,1)S(1)} %copy-done.7, f32[32,2048]{1,0:T(8,128)S(1)} %copy-done.6, bf16[32,2048]{1,0:T(8,128)(2,1)S(1)} %copy-done.8, bf16[1024,128]{1,0:T(8,128)(2,1)S(1)} %get-tuple-element.49.keep_ref, ...), custom_call_target="tpu_custom_call" | custom-call | tf_op jit(solution)/shard_map/rows/pallas_call | solution.py:433
  47.2 2.6 %all-to-all-start.2 = ((bf16[32,8,2048]{2,1,0:T(8,128)(2,1)}), bf16[32,8,2048]{2,1,0:T(8,128)(2,1)S(1)}, u32[]{:S(2)}, u32[]{:S(2)}) async-start(bf16[32,8,2048]{2,1,0:T(8,128)(2,1)} %bitcast.8), calls=%async_computation.2 | async-start | bytes 2097152 | tf_op jit(solution)/shard_map/all_to_all | solution.py:444
  49.8 0.0 copy-done.1
  49.8 0.0 copy-start.4
  49.9 1.6 %copy-done.4 = f32[256,2048]{1,0:T(8,128)S(1)} copy-done((f32[256,2048]{1,0:T(8,128)S(1)}, f32[256,2048]{1,0:T(8,128)}, u32[]{:S(2)}) %copy-start.4) | copy-done | bytes 2097176
  51.4 0.0 copy-start.5
  51.4 1.2 %copy-done.5 = bf16[256,2048]{1,0:T(8,128)(2,1)S(1)} copy-done((bf16[256,2048]{1,0:T(8,128)(2,1)S(1)}, bf16[256,2048]{1,0:T(8,128)(2,1)}, u32[]{:S(2)}) %copy-start.5) | copy-done | bytes 1048600
  52.7 1.5 %mixed.1.mixed_ref = f32[256,2048]{1,0:T(8,128)S(1)} custom-call(s32[1]{0:T(128)} %bitcast.k_ref, bf16[256,2048]{1,0:T(8,128)(2,1)S(1)} %copy-done.5, f32[256,2048]{1,0:T(8,128)S(1)} %copy-done.4, bf16[256,2048]{1,0:T(8,128)(2,1)S(1)} %copy-done.1, bf16[1024,128]{1,0:T(8,128)(2,1)S(1)} %get-tuple-element.49.keep_ref, ...), custom_call_target="tpu_custom_call" | custom-call | flops 134217728 | bytes 7340032 | tf_op jit(solution)/shard_map/mixed/pallas_call | solution.py:448
  54.2 0.0 copy-start
  54.2 1.3 %copy-done = f32[256,2048]{1,0:T(8,128)} copy-done((f32[256,2048]{1,0:T(8,128)}, f32[256,2048]{1,0:T(8,128)S(1)}, u32[]{:S(2)}) %copy-start) | copy-done | bytes 2097176
  55.5 20.5 %all-to-all-done.2 = bf16[32,8,2048]{2,1,0:T(8,128)(2,1)S(1)} async-done(((bf16[32,8,2048]{2,1,0:T(8,128)(2,1)}), bf16[32,8,2048]{2,1,0:T(8,128)(2,1)S(1)}, u32[]{:S(2)}, u32[]{:S(2)}) %all-to-all-start.2) | async-done | bytes 1048608 | tf_op jit(solution)/shard_map/all_to_all | solution.py:444
  76.1 0.0 collective-permute-done.2.g1
  76.1 0.0 collective-permute-done.3.u1
  76.1 0.0 collective-permute-done.4.d1
  76.1 6.2 %expert.1 = bf16[256,2048]{1,0:T(8,128)(2,1)S(1)} custom-call(bf16[256,2048]{1,0:T(8,128)(2,1)S(1)} %bitcast.12, bf16[2048,512]{1,0:T(8,128)(2,1)} %g0, bf16[2048,512]{1,0:T(8,128)(2,1)} %u0, bf16[512,2048]{1,0:T(8,128)(2,1)} %d0, bf16[2048,512]{1,0:T(8,128)(2,1)} %collective-permute-done.2.g1, bf16[2048,512]{1,0:T(8,128)(2,1)} %collective-permute-done.3.u1, ...), custom_call_target="tpu_custom_call" | custom-call | flops 3221225472 | bytes 14680064 | tf_op jit(solution)/shard_map/expert/pallas_call | solution.py:463
  82.3 29.7 %all_to_all.21 = bf16[32,8,2048]{2,1,0:T(8,128)(2,1)} all-to-all(bf16[32,8,2048]{2,1,0:T(8,128)(2,1)S(1)} %bitcast.13), channel_id=1, replica_groups=mesh['seq'=8,'grp'=4] {'seq','grp'}, dimensions={0} | all-to-all | bytes 2097152 | tf_op jit(solution)/shard_map/all_to_all | solution.py:476
  112.0 4.4 %final.1 = bf16[256,2048]{1,0:T(8,128)(2,1)} custom-call(f32[256,2048]{1,0:T(8,128)} %copy-done, bf16[256,256]{1,0:T(8,128)(2,1)} %get-tuple-element.55.chi_ref, bf16[256,256]{1,0:T(8,128)(2,1)} %get-tuple-element.56.clo_ref, bf16[256,2048]{1,0:T(8,128)(2,1)} %bitcast.18), custom_call_target="tpu_custom_call" | custom-call | tf_op jit(solution)/shard_map/final/pallas_call | solution.py:482
Async XLA Ops:
  0.0 16.7 %copy-start.12 = (s32[256]{0:T(256)S(1)}, s32[256]{0:T(256)}, u32[]{:S(2)}) copy-start(s32[256]{0:T(256)} %param.22) | copy-start | bytes 3076
  4.1 2.3 %collective-permute-start = (f32[1032,128]{1,0:T(8,128)}, f32[1032,128]{1,0:T(8,128)S(1)}, u32[]{:S(2)}, u32[]{:S(2)}) collective-permute-start(f32[1032,128]{1,0:T(8,128)} %get-tuple-element.34), channel_id=1, source_target_pairs={{0,1},{1,0},{2,3},{3,2},{4,5},{5,4},{6,7},{7,6},{8,9},{9,8},{10,11... | collective-permute-start | bytes 1585160 | tf_op jit(solution)/shard_map/ppermute | solution.py:61
  6.4 1.0 copy-start.2
  8.4 19.9 %all-to-all-start = ((bf16[16,80,128]{2,1,0:T(8,128)(2,1)}), bf16[16,80,128]{2,1,0:T(8,128)(2,1)S(1)}, u32[]{:S(2)}, u32[]{:S(2)}) async-start(bf16[16,80,128]{2,1,0:T(8,128)(2,1)} %pair.1), calls=%async_computation | async-start | bytes 655360 | tf_op jit(solution)/shard_map/all_to_all | solution.py:67
  20.0 23.3 %copy-start.3 = (f32[1032,128]{1,0:T(8,128)S(1)}, f32[1032,128]{1,0:T(8,128)}, u32[]{:S(2)}) copy-start(f32[1032,128]{1,0:T(8,128)} %get-tuple-element.33.own_ref.own_hbm) | copy-start | bytes 1585156
  26.7 18.5 %copy-start.6 = (f32[32,2048]{1,0:T(8,128)S(1)}, f32[32,2048]{1,0:T(8,128)}, u32[]{:S(2)}) copy-start(f32[32,2048]{1,0:T(8,128)} %get-tuple-element.46.inside_ref) | copy-start | bytes 786436
  26.7 18.5 %copy-start.7 = (bf16[32,2048]{1,0:T(8,128)(2,1)S(1)}, bf16[32,2048]{1,0:T(8,128)(2,1)}, u32[]{:S(2)}) copy-start(bf16[32,2048]{1,0:T(8,128)(2,1)} %get-tuple-element.45.lifted_ref) | copy-start | bytes 393220
  26.7 18.5 %copy-start.8 = (bf16[32,2048]{1,0:T(8,128)(2,1)S(1)}, bf16[32,2048]{1,0:T(8,128)(2,1)}, u32[]{:S(2)}) copy-start(bf16[32,2048]{1,0:T(8,128)(2,1)} %get-tuple-element.47.stream_ref) | copy-start | bytes 393220
  26.7 18.5 %copy-start.9 = (bf16[256,32]{1,0:T(8,128)(2,1)S(1)}, bf16[256,32]{1,0:T(8,128)(2,1)}, u32[]{:S(2)}) copy-start(bf16[256,32]{1,0:T(8,128)(2,1)} %get-tuple-element.51.disp_ref) | copy-start | bytes 49156
  26.7 18.5 %copy-start.10 = (f32[2048]{0:T(1024)S(1)}, f32[2048]{0:T(1024)}, u32[]{:S(2)}) copy-start(f32[2048]{0:T(1024)} %param.18) | copy-start | bytes 24580
  26.7 18.5 %copy-start.11 = (f32[2048]{0:T(1024)S(1)}, f32[2048]{0:T(1024)}, u32[]{:S(2)}) copy-start(f32[2048]{0:T(1024)} %param.19) | copy-start | bytes 24580
  43.6 1.6 %collective-permute-start.1 = (bf16[1024,128]{1,0:T(8,128)(2,1)S(1)}, bf16[1024,128]{1,0:T(8,128)(2,1)S(1)}, u32[]{:S(2)}, u32[]{:S(2)}) collective-permute-start(bf16[1024,128]{1,0:T(8,128)(2,1)S(1)} %get-tuple-element.50), channel_id=1, source_target_pairs={{0,1},{1,0},{2,3},{3,2},{4,5},{5,4},{6,7},{7,6},{8,9},{9,8},{10,11... | collective-permute-start | bytes 786440 | tf_op jit(solution)/shard_map/ppermute | solution.py:61
  43.7 32.4 %collective-permute-start.2 = (bf16[2048,512]{1,0:T(8,128)(2,1)}, bf16[2048,512]{1,0:T(8,128)(2,1)}, u32[]{:S(2)}, u32[]{:S(2)}) collective-permute-start(bf16[2048,512]{1,0:T(8,128)(2,1)} %g0), channel_id=1, source_target_pairs={{0,1},{1,0},{2,3},{3,2},{4,5},{5,4},{6,7},{7,6},{8,9},{9,8},{10,11... | collective-permute-start | bytes 6291464 | tf_op jit(solution)/shard_map/ppermute | solution.py:61
  44.2 31.9 %collective-permute-start.3 = (bf16[2048,512]{1,0:T(8,128)(2,1)}, bf16[2048,512]{1,0:T(8,128)(2,1)}, u32[]{:S(2)}, u32[]{:S(2)}) collective-permute-start(bf16[2048,512]{1,0:T(8,128)(2,1)} %u0), channel_id=1, source_target_pairs={{0,1},{1,0},{2,3},{3,2},{4,5},{5,4},{6,7},{7,6},{8,9},{9,8},{10,11... | collective-permute-start | bytes 6291464 | tf_op jit(solution)/shard_map/ppermute | solution.py:61
  44.3 31.8 %collective-permute-start.4 = (bf16[512,2048]{1,0:T(8,128)(2,1)}, bf16[512,2048]{1,0:T(8,128)(2,1)}, u32[]{:S(2)}, u32[]{:S(2)}) collective-permute-start(bf16[512,2048]{1,0:T(8,128)(2,1)} %d0), channel_id=1, source_target_pairs={{0,1},{1,0},{2,3},{3,2},{4,5},{5,4},{6,7},{7,6},{8,9},{9,8},{10,11... | collective-permute-start | bytes 6291464 | tf_op jit(solution)/shard_map/ppermute | solution.py:61
  45.2 4.6 %copy-start.1 = (bf16[256,2048]{1,0:T(8,128)(2,1)S(1)}, bf16[256,2048]{1,0:T(8,128)(2,1)}, u32[]{:S(2)}) copy-start(bf16[256,2048]{1,0:T(8,128)(2,1)} %stream_ref.3) | copy-start | bytes 3145732
  47.2 28.9 %all-to-all-start.2 = ((bf16[32,8,2048]{2,1,0:T(8,128)(2,1)}), bf16[32,8,2048]{2,1,0:T(8,128)(2,1)S(1)}, u32[]{:S(2)}, u32[]{:S(2)}) async-start(bf16[32,8,2048]{2,1,0:T(8,128)(2,1)} %bitcast.8), calls=%async_computation.2 | async-start | bytes 2097152 | tf_op jit(solution)/shard_map/all_to_all | solution.py:444
  49.8 1.6 %copy-start.4 = (f32[256,2048]{1,0:T(8,128)S(1)}, f32[256,2048]{1,0:T(8,128)}, u32[]{:S(2)}) copy-start(f32[256,2048]{1,0:T(8,128)} %get-tuple-element.53.inside_ref) | copy-start | bytes 6291460
  51.4 1.2 %copy-start.5 = (bf16[256,2048]{1,0:T(8,128)(2,1)S(1)}, bf16[256,2048]{1,0:T(8,128)(2,1)}, u32[]{:S(2)}) copy-start(bf16[256,2048]{1,0:T(8,128)(2,1)} %get-tuple-element.52.lifted_ref) | copy-start | bytes 3145732
  54.2 1.3 %copy-start = (f32[256,2048]{1,0:T(8,128)}, f32[256,2048]{1,0:T(8,128)S(1)}, u32[]{:S(2)}) copy-start(f32[256,2048]{1,0:T(8,128)S(1)} %mixed.1.mixed_ref) | copy-start | bytes 6291460

commit v3 on v2

--- a/solution.py
+++ b/solution.py
@@ -12,6 +12,8 @@
 TAIL16 = 16
 ATTN_EPS = 1e-05
 NORM_EPS = 1e-06
+PLANES = 4
+PARTS = 2
 BOTH = ("seq", "grp")
 F32 = jnp.float32
 BF16 = jnp.bfloat16
@@ -59,6 +61,10 @@
 def partner(x):
     count = lax.axis_size("grp")
     return lax.ppermute(x, "grp", [(i, i ^ 1) for i in range(count)])
+
+
+def apart(x, distance):
+    return lax.ppermute(x, BOTH, [(i, i ^ distance) for i in range(lax.axis_size(BOTH))])
 
 
 def across_pairs(x):
@@ -210,11 +216,11 @@
     return att * lax.rsqrt(jnp.mean(att * att, axis=-1, keepdims=True) + ATTN_EPS)
 
 
-def rows_kernel(k_ref, lifted_ref, inside_ref, stream_ref, keep_ref, other_ref, again_ref, fgain_ref, disp_ref, sent_ref, mixed_ref):
+def rows_kernel(k_ref, lifted_ref, inside_ref, stream_ref, keep_ref, other_ref, again_ref, fgain_ref, *refs):
+    *out_refs, mixed_ref = refs
     hd = keep_ref.shape[1]
     half = keep_ref.shape[0] // hd
     k = k_ref[0]
-    rows, width = lifted_ref.shape
     for r in range(2 * half):
         side = r // half
         off = pl.multiple_of((side ^ k) * (half * hd) + (r % half) * hd, hd)
@@ -225,10 +231,12 @@
     mixed = mixed_ref[...]
     scale = lax.rsqrt(jnp.mean(mixed * mixed, axis=-1, keepdims=True) + NORM_EPS)
     ffn = (mixed * scale * fgain_ref[...]).astype(BF16)
-    sent_ref[...] = mm(disp_ref[...], ffn).astype(BF16)
-
-
-def mixed_kernel(k_ref, lifted_ref, inside_ref, stream_ref, keep_ref, other_ref, again_ref, mixed_ref):
+    part = ffn.shape[1] // len(out_refs)
+    for c, out_ref in enumerate(out_refs):
+        out_ref[...] = ffn[:, c * part : (c + 1) * part]
+
+
+def mixed_kernel(k_ref, from_ref, lifted_ref, inside_ref, stream_ref, keep_ref, other_ref, again_ref, base_ref, near_ref, mixed_ref):
     hd = keep_ref.shape[1]
     half = keep_ref.shape[0] // hd
     mine = pl.program_id(0) == k_ref[0]
@@ -237,11 +245,17 @@
         st = jnp.where(mine, keep_ref[cols, :].astype(F32), other_ref[cols, :].astype(F32)).astype(BF16)
         att = inside_ref[:, cols] + mm(lifted_ref[:, cols], st)
         mixed_ref[:, cols] = stream_ref[:, cols].astype(F32) + head_norm(att) * again_ref[:, cols]
-
-
-def route_kernel(start_ref, ids_ref, wts_ref, live_ref, disp_ref, chi_ref, clo_ref, *, experts):
+    base_ref[...] = mixed_ref[...].astype(BF16)
+    near_ref[...] = mixed_ref[pl.ds(pl.multiple_of(from_ref[0], 16), near_ref.shape[0]), :]
+
+
+def route_kernel(start_ref, plane_ref, ids_ref, wts_ref, live_ref, *refs, experts):
+    *out_refs, tab_ref = refs
     top, tok = ids_ref.shape
-    slots, resp = disp_ref.shape
+    slots = experts * CAP
+    planes = len(out_refs)
+    span = slots // planes
+    resp = tab_ref.shape[2]
     live = live_ref[...] == 1
     e_row = lax.broadcasted_iota(jnp.int32, (experts, tok), 0)
     chosen = jnp.zeros((experts, tok), F32)
@@ -264,55 +278,120 @@
     w_lo = (weight - w_hi.astype(F32)).astype(BF16)
     picked = lax.broadcasted_iota(jnp.int32, (tok, resp), 1) + start_ref[0]
     pick = jnp.where(lax.broadcasted_iota(jnp.int32, (tok, resp), 0) == picked, 1.0, 0.0).astype(BF16)
-    disp_ref[...] = mm(jnp.where(hit, 1.0, 0.0).astype(BF16), pick).astype(BF16)
-    chi_ref[...] = jnp.where(hit, mm(spread, w_hi), 0.0).astype(BF16)
-    clo_ref[...] = jnp.where(hit, mm(spread, w_lo), 0.0).astype(BF16)
-
-
-def expert_kernel(x_hbm, g0, u0, d0, g1, u1, d1, out_hbm, gv, uv, dv, hid_ref, x_ref, out_ref, sems, *, step):
-    width, units = g0.shape
+    zero = jnp.zeros((slots, tok), F32)
+    tables = (jnp.where(hit, 1.0, zero), jnp.where(hit, mm(spread, w_hi), zero), jnp.where(hit, mm(spread, w_lo), zero))
+    for n, table in enumerate(tables):
+        table = mm(table.astype(BF16), pick).astype(BF16)
+        for p in range(planes):
+            tab_ref[p, n * span : (n + 1) * span, :] = table[p * span : (p + 1) * span, :]
+    for m, out_ref in enumerate(out_refs):
+        out_ref[...] = tab_ref[plane_ref[0] ^ m, :, :]
+
+
+def table_rows(tab_ref, n, at, count):
+    lead = n * count * CAP
+    rows = [tab_ref[pl.ds(pl.multiple_of(lead + (at ^ m) * CAP, CAP), CAP), :] for m in range(count)]
+    return jnp.concatenate(rows, axis=0)
+
+
+def gather_kernel(at_ref, *refs, planes, count):
+    tabs, rows, outs = refs[:planes], refs[planes : 2 * planes], refs[2 * planes :]
+    for m in range(planes):
+        got = mm(table_rows(tabs[m], 0, at_ref[0], count), rows[m][...]).astype(BF16)
+        for q in range(count):
+            outs[q][m * CAP : (m + 1) * CAP, :] = got[q * CAP : (q + 1) * CAP, :]
+
+
+def combine_kernel(at_ref, *refs, planes, count):
+    tabs, results, outs = refs[:planes], refs[planes : planes + count], refs[planes + count :]
+    for m in range(planes):
+        got = jnp.concatenate([results[q][m * CAP : (m + 1) * CAP, :] for q in range(count)], axis=0)
+        hi = table_rows(tabs[m], 1, at_ref[0], count)
+        lo = table_rows(tabs[m], 2, at_ref[0], count)
+        outs[m][...] = (mm(hi, got, 0, 0) + mm(lo, got, 0, 0)).astype(outs[m].dtype)
+
+
+def expert_kernel(*refs, count, parts, step):
+    xs, refs = refs[: count * parts], refs[count * parts :]
+    (g0, u0, d0, g1, u1, d1), refs = refs[:6], refs[6:]
+    outs, refs = refs[:count], refs[count:]
+    hid_out, gv, uv, dv, hid_ref, x_ref, sems = refs
+    units = g0.shape[1]
+    rows, part = xs[0].shape
     cuts = range(0, units, step)
-    gets = [copy(x_hbm, x_ref, sems, 0)]
+    gets = []
+    for q in range(count):
+        for c in range(parts):
+            dst = x_ref.at[pl.ds(q * rows, rows), pl.ds(c * part, part)]
+            gets.append(copy(xs[c * count + q], dst, sems, len(gets)))
+    at = len(gets)
     for n, (g, u) in enumerate(((g0, u0), (g1, u1))):
         for c in cuts:
             cols = pl.ds(c, step)
             gets.append(copy(g.at[:, cols], gv.at[n, :, cols], sems, len(gets)))
             gets.append(copy(u.at[:, cols], uv.at[n, :, cols], sems, len(gets)))
     for n, d in enumerate((d0, d1)):
-        gets.append(copy(d, dv.at[n], sems, len(gets)))
-    gets[0].wait()
-    at = 1
-    block = min(256, x_ref.shape[0])
-    blocks = range(0, x_ref.shape[0], block)
+        gets.append(copy(d.at[:, pl.ds(0, part)], dv.at[n], sems, len(gets)))
+    for c in gets[:at]:
+        c.wait()
+    many = count * rows
+    block = min(256, many)
     for n in range(2):
         for c in cuts:
             gets[at].wait()
             gets[at + 1].wait()
             at += 2
-            for r in blocks:
+            for r in range(0, many, block):
                 x = x_ref[r : r + block, :]
                 gate = mm(x, gv[n, :, c : c + step])
                 up = mm(x, uv[n, :, c : c + step])
                 hid_ref[n, r : r + block, c : c + step] = (gate / (1.0 + jnp.exp(-gate)) * up).astype(BF16)
+    put = copy(hid_ref, hid_out, sems, len(gets))
     gets[at].wait()
     gets[at + 1].wait()
-    puts = []
-    for r in blocks:
-        for c in range(0, width, 256):
+    down(hid_ref, dv, outs, block)
+    put.wait()
+
+
+def down(hid_ref, down_ref, outs, block):
+    rows, part = outs[0].shape
+    for r in range(0, rows * len(outs), block):
+        for c in range(0, part, 256):
             cols = slice(c, c + 256)
-            p0 = mm(hid_ref[0, r : r + block, :], dv[0, :, cols]).astype(BF16).astype(F32)
-            p1 = mm(hid_ref[1, r : r + block, :], dv[1, :, cols]).astype(BF16).astype(F32)
-            out_ref[r : r + block, cols] = (p0 + p1).astype(BF16)
-        done = pl.ds(r, block)
-        puts.append(copy(out_ref.at[done], out_hbm.at[done], sems, len(gets) + len(puts)))
-    for c in puts:
+            p0 = mm(hid_ref[0, r : r + block, :], down_ref[0, :, cols]).astype(BF16).astype(F32)
+            p1 = mm(hid_ref[1, r : r + block, :], down_ref[1, :, cols]).astype(BF16).astype(F32)
+            p = (p0 + p1).astype(BF16)
+            for q in range(r // rows, (r + block) // rows):
+                outs[q][:, cols] = p[q * rows - r : (q + 1) * rows - r, :]
+
+
+def down_kernel(hid_ref, d0, d1, *refs, count, first):
+    outs, (dv, sems) = refs[:count], refs[count:]
+    part = outs[0].shape[1]
+    gets = [copy(d.at[:, pl.ds(first, part)], dv.at[n], sems, n) for n, d in enumerate((d0, d1))]
+    for c in gets:
         c.wait()
-
-
-def final_kernel(mixed_ref, chi_ref, clo_ref, back_ref, out_ref):
-    back = back_ref[...]
-    moe = mm(chi_ref[...], back, 0, 0) + mm(clo_ref[...], back, 0, 0)
-    out_ref[...] = (mixed_ref[...] + moe).astype(BF16)
+    down(hid_ref, dv, outs, min(256, hid_ref.shape[1]))
+
+
+def final_kernel(start_ref, from_ref, base_hbm, near_ref, *refs, parts, planes):
+    shares, (out_hbm, res_ref, sem) = refs[: parts * planes], refs[parts * planes :]
+    many, width = near_ref.shape
+    resp, part = shares[0].shape
+    row = lax.broadcasted_iota(jnp.int32, (many, resp), 0)
+    place = lax.broadcasted_iota(jnp.int32, (many, resp), 1) + (start_ref[0] - from_ref[0])
+    spread = jnp.where(row == place, 1.0, 0.0).astype(BF16)
+    for c in range(parts):
+        cols = slice(c * part, (c + 1) * part)
+        total = shares[c * planes][...]
+        for m in range(1, planes):
+            total = total + shares[c * planes + m][...].astype(F32)
+        hi = total.astype(BF16)
+        lo = (total - hi.astype(F32)).astype(BF16)
+        res_ref[:, cols] = (near_ref[:, cols] + mm(spread, hi) + mm(spread, lo)).astype(BF16)
+    put = pltpu.make_async_copy(res_ref, out_hbm.at[pl.ds(pl.multiple_of(from_ref[0], 16), many)], sem)
+    put.start()
+    put.wait()
 
 
 def shards(
@@ -341,6 +420,9 @@
     top = expert_ids.shape[1]
     resp = min(tok, slots // top)
     rows = half * hd // pairs
+    planes = PLANES
+    count = pairs // planes
+    part = width // PARTS
     me = lax.axis_index(BOTH)
     bit = (me & 1).reshape(1).astype(jnp.int32)
     sds = jax.ShapeDtypeStruct
@@ -375,18 +457,22 @@
     col = pl.BlockSpec((tok, width // 2), lambda i: (0, i))
     wcol = pl.BlockSpec((resp, width // 2), lambda i: (0, i))
     start = jnp.minimum(jnp.argmax(response_mask), tok - resp).astype(jnp.int32).reshape(1)
+    plane = lax.shift_right_logical(me, (2 * count).bit_length() - 1).reshape(1).astype(jnp.int32)
+    at = (lax.shift_right_logical(me, 1) & (count - 1)).reshape(1).astype(jnp.int32)
     routing = (expert_ids.T, route_weights.T, response_mask.reshape(1, tok))
-    tables = [sds((slots, resp), BF16), sds((slots, tok), BF16), sds((slots, tok), BF16)]
-    disp, chi, clo = pl.pallas_call(
+    table = sds((3 * count * CAP, resp), BF16)
+    tables = pl.pallas_call(
         functools.partial(route_kernel, experts=experts),
         grid=(1,),
-        out_shape=tables,
-        in_specs=[SMEM] + [full(a) for a in routing],
-        out_specs=[full(a) for a in tables],
+        out_shape=[table] * planes,
+        in_specs=[SMEM, SMEM] + [full(a) for a in routing],
+        out_specs=[full(table)] * planes,
+        scratch_shapes=[pltpu.VMEM((planes,) + table.shape, BF16)],
         compiler_params=params(),
         cost_estimate=cost(8 * tok * tok * slots, 1 << 20),
         name="route",
-    )(start, *routing)
+    )(start, plane, *routing)
+    tables = [tables[0]] + [apart(tables[m], 2 * count * m) for m in range(1, planes)]
     inside, lifted, inside_r, lifted_r, stream_r = pl.pallas_call(
         inside_kernel,
         grid=(2,),
@@ -403,8 +489,8 @@
         cost_estimate=cost(4 * tok * tok * width, 6 << 20),
         name="inside",
     )(start, log_decay, query_rows, key_rows, value_rows, stream_in)
-    gathered, inside, lifted, inside_r, lifted_r, stream_r, disp, chi, clo = lax.optimization_barrier(
-        (gathered, inside, lifted, inside_r, lifted_r, stream_r, disp, chi, clo)
+    gathered, inside, lifted, inside_r, lifted_r, stream_r = lax.optimization_barrier(
+        (gathered, inside, lifted, inside_r, lifted_r, stream_r)
     )
     scanned = pl.pallas_call(
         scan_kernel,
@@ -416,6 +502,7 @@
         name="scan",
     )(gathered)
     pref = across_pairs(scanned).reshape(half * hd, hd)
+    pref, *tables = lax.optimization_barrier((pref, *tables))
     keep, give = pl.pallas_call(
         functools.partial(split_kernel, half=half),
         grid=(1,),
@@ -429,65 +516,108 @@
     other = partner(give)
 
     again = attn_gain.reshape(1, width)
-    window = (lifted_r, inside_r, stream_r, keep, other, again, ffn_gain.reshape(1, width), disp)
-    sent = pl.pallas_call(
+    window = (lifted_r, inside_r, stream_r, keep, other, again, ffn_gain.reshape(1, width))
+    row_part = sds((resp, part), BF16)
+    ready = pl.pallas_call(
         rows_kernel,
         grid=(1,),
-        out_shape=sds((slots, width), BF16),
+        out_shape=[row_part] * PARTS,
         in_specs=[SMEM] + [full(a) for a in window],
-        out_specs=full(sds((slots, width), BF16)),
+        out_specs=[full(row_part)] * PARTS,
         scratch_shapes=[pltpu.VMEM((resp, width), F32)],
         compiler_params=params(8),
         name="rows",
     )(bit, *window)
-    half_rows = CAP // 2
-    arrived = lax.all_to_all(sent.reshape(devices, half_rows, width), BOTH, 0, 0, tiled=True)
+    lines = [[ready[c]] + [apart(ready[c], 2 * count * m) for m in range(1, planes)] for c in range(PARTS)]
+    chunk = sds((planes * CAP, part), BF16)
+    arrived = []
+    for c in range(PARTS):
+        operands = (*tables, *lines[c])
+        chunks = pl.pallas_call(
+            functools.partial(gather_kernel, planes=planes, count=count),
+            grid=(1,),
+            out_shape=[chunk] * count,
+            in_specs=[SMEM] + [full(a) for a in operands],
+            out_specs=[full(chunk)] * count,
+            compiler_params=params(8),
+            name="gather",
+        )(at, *operands)
+        arrived += [chunks[0]] + [apart(chunks[m], 2 * m) for m in range(1, count)]
 
     gain_col = pl.BlockSpec((1, width // 2), lambda i: (0, i))
     state_all = pl.BlockSpec((half * hd, hd), lambda i: (0, 0))
-    mixed = pl.pallas_call(
+    near = min(tok, resp + 16)
+    first = jnp.minimum(start & -16, tok - near)
+    near_col = pl.BlockSpec((near, width // 2), lambda i: (0, i))
+    base, around = pl.pallas_call(
         mixed_kernel,
         grid=(2,),
-        out_shape=sds((tok, width), F32),
-        in_specs=[SMEM, col, col, col, state_all, state_all, gain_col],
-        out_specs=col,
+        out_shape=[sds((tok, width), BF16), sds((near, width), F32)],
+        in_specs=[SMEM, SMEM, col, col, col, state_all, state_all, gain_col],
+        out_specs=[col, near_col],
+        scratch_shapes=[pltpu.VMEM((tok, width // 2), F32)],
         compiler_params=params(32),
         cost_estimate=cost(2 * tok * width * hd, 7 << 20),
         name="mixed",
-    )(bit, lifted, inside, stream_in, keep, other, again)
-
-    arrived, mixed = lax.optimization_barrier((arrived, mixed))
+    )(bit, first, lifted, inside, stream_in, keep, other, again)
+    base, around, *arrived = lax.optimization_barrier((base, around, *arrived))
+
     units = gate_weight.shape[1]
     step = min(256, units)
-    many = devices * half_rows
-    done = pl.pallas_call(
-        functools.partial(expert_kernel, step=step),
-        out_shape=sds((many, width), BF16),
-        in_specs=[HBM] * 7,
+    many = count * chunk.shape[0]
+    hidden = sds((2, many, units), BF16)
+    *results, hid = pl.pallas_call(
+        functools.partial(expert_kernel, count=count, parts=PARTS, step=step),
+        grid=(1,),
+        out_shape=[chunk] * count + [hidden],
+        in_specs=[HBM] * (count * PARTS + 6),
+        out_specs=[full(chunk)] * count + [HBM],
+        scratch_shapes=[pltpu.VMEM((2, width, units), BF16)] * 2
+        + [pltpu.VMEM((2, units, part), BF16), pltpu.VMEM(hidden.shape, BF16), pltpu.VMEM((many, width), BF16)]
+        + [DMA((count * PARTS + 4 * (units // step) + 3,))],
+        compiler_params=params(48),
+        cost_estimate=cost(10 * many * width * units, 12 << 20),
+        name="expert",
+    )(*arrived, gate_own, up_own, down_own, gate_other, up_other, down_other)
+    shares = []
+    for c in range(PARTS):
+        if c:
+            results = pl.pallas_call(
+                functools.partial(down_kernel, count=count, first=c * part),
+                grid=(1,),
+                out_shape=[chunk] * count,
+                in_specs=[full(hid), HBM, HBM],
+                out_specs=[full(chunk)] * count,
+                scratch_shapes=[pltpu.VMEM((2, units, part), BF16), DMA((2,))],
+                compiler_params=params(48),
+                cost_estimate=cost(2 * many * width * units, 2 << 20),
+                name="down",
+            )(hid, down_own, down_other)
+        back = [results[0]] + [apart(results[m], 2 * m) for m in range(1, count)]
+        operands = (*tables, *back)
+        kinds = [sds((resp, part), F32)] + [row_part] * (planes - 1)
+        sums = pl.pallas_call(
+            functools.partial(combine_kernel, planes=planes, count=count),
+            grid=(1,),
+            out_shape=kinds,
+            in_specs=[SMEM] + [full(a) for a in operands],
+            out_specs=[full(a) for a in kinds],
+            compiler_params=params(8),
+            name="combine",
+        )(at, *operands)
+        shares += [sums[0]] + [apart(sums[m], 2 * count * m) for m in range(1, planes)]
+
+    return pl.pallas_call(
+        functools.partial(final_kernel, parts=PARTS, planes=planes),
+        grid=(1,),
+        out_shape=sds((tok, width), BF16),
+        in_specs=[SMEM, SMEM, HBM, full(around)] + [full(a) for a in shares],
         out_specs=HBM,
-        scratch_shapes=[pltpu.VMEM((2, width, units), BF16)] * 2
-        + [pltpu.VMEM((2, units, width), BF16), pltpu.VMEM((2, many, units), BF16)]
-        + [pltpu.VMEM((many, width), BF16)] * 2
-        + [DMA((4 * (units // step) + 3 + many // min(256, many),))],
-        compiler_params=params(48),
-        cost_estimate=cost(12 * many * width * units, 14 << 20),
-        name="expert",
-    )(arrived.reshape(many, width), gate_own, up_own, down_own, gate_other, up_other, down_other)
-    back = lax.all_to_all(done.reshape(devices, half_rows, width), BOTH, 0, 0, tiled=True)
-    back = back.reshape(slots, width)
-
-    steps = 4
-    fcol = pl.BlockSpec((tok, width // steps), lambda i: (0, i))
-    whole = pl.BlockSpec((slots, tok), lambda i: (0, 0))
-    return pl.pallas_call(
-        final_kernel,
-        grid=(steps,),
-        out_shape=sds((tok, width), BF16),
-        in_specs=[fcol, whole, whole, pl.BlockSpec((slots, width // steps), lambda i: (0, i))],
-        out_specs=fcol,
-        compiler_params=params(),
+        scratch_shapes=[pltpu.VMEM((near, width), BF16), DMA],
+        input_output_aliases={2: 0},
+        compiler_params=params(8),
         name="final",
-    )(mixed, chi, clo, back)
+    )(start, first, base, around, *shares)
 
 
 def solution(mesh):

time: 117 us -> 136 us (1.16)
  blocking collectives: 44.6 us -> 0 us
  starting transfers between devices: 12.5 us -> 56.5 us
  local copies, waits for them, and re-layouts: 5.22 us -> 22.6 us
    all_to_all x2 -> x0, blocking collectives: 44.6 us -> none  [the longest x1 29.7 us: shards(): lax.all_to_all(done.reshape(devices, half_rows, width), BOTH, 0, 0, tiled...]
    ppermute x0 -> x27, starting transfers between devices: none -> 43.4 us  [apart(): lax.ppermute(x, BOTH, [(i, i ^ distance) for i in range(lax.axis_size(BOT...]
    all_to_all x1 -> x0, waiting for transfers between devices: 20.5 us -> none  [shards(): lax.all_to_all(sent.reshape(devices, half_rows, width), BOTH, 0, 0, tiled...]
    ppermute x0 -> x27, waiting for transfers between devices: none -> 18.1 us  [apart(): lax.ppermute(x, BOTH, [(i, i ^ distance) for i in range(lax.axis_size(BOT...]
    unnamed x26 -> x68, local copies, waits for them, and re-layouts: 5.22 us -> 22.6 us
    all_to_all x1 -> x2, starting transfers between devices: 8.24 us -> 11.7 us  [across_pairs(): return lax.all_to_all(x, BOTH, 0, 0, tiled=True, axis_index_groups=groups)]
    all_to_all x1 -> x0, starting transfers between devices: 2.64 us -> none  [shards(): lax.all_to_all(sent.reshape(devices, half_rows, width), BOTH, 0, 0, tiled...]
    all_to_all x1 -> x2, waiting for transfers between devices: 1.57 us -> 3.85 us  [across_pairs(): return lax.all_to_all(x, BOTH, 0, 0, tiled=True, axis_index_groups=groups)]
  transfers between devices with their start and end apart: 7 -> 34, of which waited for: 4 -> 13; matrix products, arithmetic and copies ran while one was open for 1% -> 1% of each run, Pallas kernels for 10% -> 13%
where the time goes in v3:
time: 136 us; the launch traced here: 135 us
  starting transfers between devices  56.5 us (42%)
  Pallas kernels  28.5 us (21%)
  waiting for transfers between devices  25.2 us (19%)
  local copies, waits for them, and re-layouts  22.6 us (17%)
    ppermute x27, starting transfers between devices, apart(): lax.ppermute(x, BOTH, [(i, i ^ distance) for i in range(lax.axis_size(BOT...  43.4 us
    unnamed x68, local copies, waits for them, and re-layouts  22.6 us
    ppermute x27, waiting for transfers between devices, apart(): lax.ppermute(x, BOTH, [(i, i ^ distance) for i in range(lax.axis_size(BOT...  18.1 us
    all_to_all x2, starting transfers between devices, across_pairs(): return lax.all_to_all(x, BOTH, 0, 0, tiled=True, axis_index_groups=groups)  11.7 us
    pallas_call x1, Pallas kernels, shards(): pl.pallas_call(inside_kernel, grid=(2,), out_shape=[sds((tok, width), F32...  6.67 us
    pallas_call x1, Pallas kernels, shards(): pl.pallas_call(functools.partial(expert_kernel, count=count, parts=PARTS,...  5.51 us
    pallas_call x1, Pallas kernels, shards(): pl.pallas_call(states_kernel, out_shape=[sds((span + TAIL, hd), F32)] * 2...  4.25 us
    all_to_all x2, waiting for transfers between devices, across_pairs(): return lax.all_to_all(x, BOTH, 0, 0, tiled=True, axis_index_groups=groups)  3.85 us
  transfers between devices with their start and end apart: 34, of which 13 were waited for; matrix products, arithmetic and copies ran while one was open for 1% of the time, Pallas kernels for 13%

profile of v3, /device:TPU:0, one launch (start us, length us, event | category | flops | bytes accessed | tf_op | source)
XLA Modules:
  0.0 134.6 jit_solution(13209875480164850153)
XLA Ops:
  0.0 4.2 %states.1 = (f32[1032,128]{1,0:T(8,128)}, f32[1032,128]{1,0:T(8,128)}) custom-call(s32[1]{0:T(128)} %bitcast.1.k_ref, bf16[256,2048]{1,0:T(8,128)(2,1)} %key_ref.1, bf16[256,2048]{1,0:T(8,128)(2,1)} %val_ref.1, f32[16,256]{1,0:T(8,128)} %dec_ref.1), custom_call_target="tpu_custom_call" | custom-call | flops 134217728 | bytes 3145728 | tf_op jit(solution)/shard_map/states/pallas_call | solution.py:431
  4.8 1.8 %collective-permute-done.recv_ref.recv_hbm = f32[1032,128]{1,0:T(8,128)S(1)} collective-permute-done((f32[1032,128]{1,0:T(8,128)}, f32[1032,128]{1,0:T(8,128)S(1)}, u32[]{:S(2)}, u32[]{:S(2)}) %collective-permute-start) | collective-permute-done | bytes 528416 | tf_op jit(solution)/shard_map/ppermute | solution.py:63
  7.4 1.0 copy-done.3
  8.5 1.0 pair.1
  9.5 0.8 copy-done.5
  10.2 8.0 %all-to-all-start = ((bf16[16,80,128]{2,1,0:T(8,128)(2,1)}), bf16[16,80,128]{2,1,0:T(8,128)(2,1)S(1)}, u32[]{:S(2)}, u32[]{:S(2)}) async-start(bf16[16,80,128]{2,1,0:T(8,128)(2,1)} %pair.1), calls=%async_computation | async-start | bytes 655360 | tf_op jit(solution)/shard_map/all_to_all | solution.py:73
  19.6 6.7 %inside.1 = (f32[256,2048]{1,0:T(8,128)}, bf16[256,2048]{1,0:T(8,128)(2,1)}, f32[32,2048]{1,0:T(8,128)}, bf16[32,2048]{1,0:T(8,128)(2,1)}, bf16[32,2048]{1,0:T(8,128)(2,1)}) custom-call(s32[1]{0:T(128)} %bitcast.start_ref, f32[16,256]{1,0:T(8,128)} %dec_ref.1, bf16[256,2048]{1,0:T(8,128)(2,1)} %q_ref.1, bf16[256,2048]{1,0:T(8,128)(2,1)} %key_ref.1, ...), custom_call_target="tpu_custom_call" | custom-call | flops 536870912 | bytes 6291456 | tf_op jit(solution)/shard_map/inside/pallas_call | solution.py:476
  26.3 3.8 %all-to-all-done.in_ref = bf16[16,80,128]{2,1,0:T(8,128)(2,1)S(1)} async-done(((bf16[16,80,128]{2,1,0:T(8,128)(2,1)}), bf16[16,80,128]{2,1,0:T(8,128)(2,1)S(1)}, u32[]{:S(2)}, u32[]{:S(2)}) %all-to-all-start) | async-done | bytes 327712 | tf_op jit(solution)/shard_map/all_to_all | solution.py:73
  30.2 0.7 copy-done.9
  30.9 3.7 %all-to-all-start.1 = ((bf16[16,64,128]{2,1,0:T(8,128)(2,1)}), bf16[16,64,128]{2,1,0:T(8,128)(2,1)S(1)}, u32[]{:S(2)}, u32[]{:S(2)}) async-start(bf16[16,64,128]{2,1,0:T(8,128)(2,1)} %copy-done.9), calls=%async_computation.1 | async-start | bytes 524288 | tf_op jit(solution)/shard_map/all_to_all | solution.py:73
  34.6 2.0 %route.1 = (bf16[192,32]{1,0:T(8,128)(2,1)}, bf16[192,32]{1,0:T(8,128)(2,1)}, bf16[192,32]{1,0:T(8,128)(2,1)}, bf16[192,32]{1,0:T(8,128)(2,1)}) custom-call(s32[1]{0:T(128)} %bitcast.start_ref, s32[1]{0:T(128)} %bitcast.3.plane_ref, s32[8,256]{1,0:T(8,128)} %bitcast.15, f32[8,256]{1,0:T(8,128)} %bitcast.16, s32[1,256]{1,0:T(1,128)} %bitcast.14), custom_call_target="tpu_custom_call" | custom-call | flops 134217728 | bytes 1048576 | tf_op jit(solution)/shard_map/route/pallas_call | solution.py:464
  36.5 1.9 %collective-permute-start.1 = (bf16[192,32]{1,0:T(8,128)(2,1)}, bf16[192,32]{1,0:T(8,128)(2,1)S(1)}, u32[]{:S(2)}, u32[]{:S(2)}) collective-permute-start(bf16[192,32]{1,0:T(8,128)(2,1)} %get-tuple-element.86), channel_id=1, source_target_pairs={{0,8},{1,9},{2,10},{3,11},{4,12},{5,13},{6,14},{7,15},{8,0},{9,1},... | collective-permute-start | bytes 36872 | tf_op jit(solution)/shard_map/ppermute | solution.py:67
  38.4 2.4 %collective-permute-start.2 = (bf16[192,32]{1,0:T(8,128)(2,1)}, bf16[192,32]{1,0:T(8,128)(2,1)S(1)}, u32[]{:S(2)}, u32[]{:S(2)}) collective-permute-start(bf16[192,32]{1,0:T(8,128)(2,1)} %get-tuple-element.87), channel_id=1, source_target_pairs={{0,16},{1,17},{2,18},{3,19},{4,20},{5,21},{6,22},{7,23},{8,24},{9,... | collective-permute-start | bytes 36872 | tf_op jit(solution)/shard_map/ppermute | solution.py:67
  40.8 0.9 collective-permute-done.1.refs_1_
  41.7 3.0 %collective-permute-start.3 = (bf16[192,32]{1,0:T(8,128)(2,1)}, bf16[192,32]{1,0:T(8,128)(2,1)S(1)}, u32[]{:S(2)}, u32[]{:S(2)}) collective-permute-start(bf16[192,32]{1,0:T(8,128)(2,1)} %get-tuple-element.88), channel_id=1, source_target_pairs={{0,24},{1,25},{2,26},{3,27},{4,28},{5,29},{6,30},{7,31},{8,16},{9,... | collective-permute-start | bytes 36872 | tf_op jit(solution)/shard_map/ppermute | solution.py:67
  44.7 0.8 collective-permute-done.2.refs_2_
  45.5 2.3 %collective-permute-done.3.refs_3_ = bf16[192,32]{1,0:T(8,128)(2,1)S(1)} collective-permute-done((bf16[192,32]{1,0:T(8,128)(2,1)}, bf16[192,32]{1,0:T(8,128)(2,1)S(1)}, u32[]{:S(2)}, u32[]{:S(2)}) %collective-permute-start.3) | collective-permute-done | bytes 12320 | tf_op jit(solution)/shard_map/ppermute | solution.py:67
  48.4 1.0 copy-done.4
  49.5 1.0 copy-done.6
  51.1 1.5 %collective-permute-done.4.other_ref = bf16[1024,128]{1,0:T(8,128)(2,1)S(1)} collective-permute-done((bf16[1024,128]{1,0:T(8,128)(2,1)S(1)}, bf16[1024,128]{1,0:T(8,128)(2,1)S(1)}, u32[]{:S(2)}, u32[]{:S(2)}) %collective-permute-start.4) | collective-permute-done | bytes 262176 | tf_op jit(solution)/shard_map/ppermute | solution.py:63
  52.6 0.9 copy-done.17
  53.6 0.9 copy-done.18
  54.5 0.9 copy-done.19
  56.8 1.1 rows.1
  58.5 3.5 %collective-permute-start.6 = (bf16[32,1024]{1,0:T(8,128)(2,1)S(1)}, bf16[32,1024]{1,0:T(8,128)(2,1)S(1)}, u32[]{:S(2)}, u32[]{:S(2)}) collective-permute-start(bf16[32,1024]{1,0:T(8,128)(2,1)S(1)} %get-tuple-element.101.refs_4_), channel_id=1, source_target_pairs={{0,16},{1,17},{2,18},{3,19},{4,20},{5,21},{6,22},{7,23},{8,24},{9,... | collective-permute-start | bytes 196616 | tf_op jit(solution)/shard_map/ppermute | solution.py:67
  62.1 0.8 collective-permute-done.5.refs_5_
  63.4 4.1 %collective-permute-start.7 = (bf16[32,1024]{1,0:T(8,128)(2,1)S(1)}, bf16[32,1024]{1,0:T(8,128)(2,1)S(1)}, u32[]{:S(2)}, u32[]{:S(2)}) collective-permute-start(bf16[32,1024]{1,0:T(8,128)(2,1)S(1)} %get-tuple-element.101.refs_4_), channel_id=1, source_target_pairs={{0,24},{1,25},{2,26},{3,27},{4,28},{5,29},{6,30},{7,31},{8,16},{9,... | collective-permute-start | bytes 196616 | tf_op jit(solution)/shard_map/ppermute | solution.py:67
  68.8 1.6 %collective-permute-done.7.refs_7_ = bf16[32,1024]{1,0:T(8,128)(2,1)S(1)} collective-permute-done((bf16[32,1024]{1,0:T(8,128)(2,1)S(1)}, bf16[32,1024]{1,0:T(8,128)(2,1)S(1)}, u32[]{:S(2)}, u32[]{:S(2)}) %collective-permute-start.7) | collective-permute-done | bytes 65568 | tf_op jit(solution)/shard_map/ppermute | solution.py:67
  71.0 2.5 %collective-permute-done.11.refs_5_ = bf16[32,1024]{1,0:T(8,128)(2,1)S(1)} collective-permute-done((bf16[32,1024]{1,0:T(8,128)(2,1)}, bf16[32,1024]{1,0:T(8,128)(2,1)S(1)}, u32[]{:S(2)}, u32[]{:S(2)}) %collective-permute-start.11) | collective-permute-done | bytes 65568 | tf_op jit(solution)/shard_map/ppermute | solution.py:67
  74.1 1.3 collective-permute-start.13
  75.4 0.8 copy-done.15
  76.2 0.8 copy-done.21
  77.0 0.8 copy-done.25
  77.9 0.8 copy-done.27
  78.7 0.8 copy-done.29
  79.8 1.6 %collective-permute-start.8 = (bf16[64,1024]{1,0:T(8,128)(2,1)S(1)}, bf16[64,1024]{1,0:T(8,128)(2,1)S(1)}, u32[]{:S(2)}, u32[]{:S(2)}) collective-permute-start(bf16[64,1024]{1,0:T(8,128)(2,1)S(1)} %get-tuple-element.103), channel_id=1, source_target_pairs={{0,2},{1,3},{2,0},{3,1},{4,6},{5,7},{6,4},{7,5},{8,10},{9,11},{10,... | collective-permute-start | bytes 393224 | tf_op jit(solution)/shard_map/ppermute | solution.py:67
  81.4 1.8 %collective-permute-start.9 = (bf16[64,1024]{1,0:T(8,128)(2,1)S(1)}, bf16[64,1024]{1,0:T(8,128)(2,1)S(1)}, u32[]{:S(2)}, u32[]{:S(2)}) collective-permute-start(bf16[64,1024]{1,0:T(8,128)(2,1)S(1)} %get-tuple-element.104), channel_id=1, source_target_pairs={{0,4},{1,5},{2,6},{3,7},{4,0},{5,1},{6,2},{7,3},{8,12},{9,13},{10,... | collective-permute-start | bytes 393224 | tf_op jit(solution)/shard_map/ppermute | solution.py:67
  83.2 0.8 copy-done.23
  84.0 1.2 gather.3
  85.2 1.6 %collective-permute-done.8.refs_1_ = bf16[64,1024]{1,0:T(8,128)(2,1)S(1)} collective-permute-done((bf16[64,1024]{1,0:T(8,128)(2,1)S(1)}, bf16[64,1024]{1,0:T(8,128)(2,1)S(1)}, u32[]{:S(2)}, u32[]{:S(2)}) %collective-permute-start.8) | collective-permute-done | bytes 131104 | tf_op jit(solution)/shard_map/ppermute | solution.py:67
  86.8 3.3 %collective-permute-start.10 = (bf16[64,1024]{1,0:T(8,128)(2,1)S(1)}, bf16[64,1024]{1,0:T(8,128)(2,1)S(1)}, u32[]{:S(2)}, u32[]{:S(2)}) collective-permute-start(bf16[64,1024]{1,0:T(8,128)(2,1)S(1)} %get-tuple-element.105), channel_id=1, source_target_pairs={{0,6},{1,7},{2,4},{3,5},{4,2},{5,3},{6,0},{7,1},{8,14},{9,15},{10,... | collective-permute-start | bytes 393224 | tf_op jit(solution)/shard_map/ppermute | solution.py:67
  90.1 0.8 collective-permute-start.14
  90.9 2.9 %collective-permute-done.10.refs_3_ = bf16[64,1024]{1,0:T(8,128)(2,1)S(1)} collective-permute-done((bf16[64,1024]{1,0:T(8,128)(2,1)S(1)}, bf16[64,1024]{1,0:T(8,128)(2,1)S(1)}, u32[]{:S(2)}, u32[]{:S(2)}) %collective-permute-start.10) | collective-permute-done | bytes 131104 | tf_op jit(solution)/shard_map/ppermute | solution.py:67
  93.8 2.2 %collective-permute-start.15 = (bf16[64,1024]{1,0:T(8,128)(2,1)S(1)}, bf16[64,1024]{1,0:T(8,128)(2,1)S(1)}, u32[]{:S(2)}, u32[]{:S(2)}) collective-permute-start(bf16[64,1024]{1,0:T(8,128)(2,1)S(1)} %get-tuple-element.109), channel_id=1, source_target_pairs={{0,4},{1,5},{2,6},{3,7},{4,0},{5,1},{6,2},{7,3},{8,12},{9,13},{10,... | collective-permute-start | bytes 393224 | tf_op jit(solution)/shard_map/ppermute | solution.py:67
  96.0 1.7 %collective-permute-start.16 = (bf16[64,1024]{1,0:T(8,128)(2,1)S(1)}, bf16[64,1024]{1,0:T(8,128)(2,1)S(1)}, u32[]{:S(2)}, u32[]{:S(2)}) collective-permute-start(bf16[64,1024]{1,0:T(8,128)(2,1)S(1)} %get-tuple-element.110), channel_id=1, source_target_pairs={{0,6},{1,7},{2,4},{3,5},{4,2},{5,3},{6,0},{7,1},{8,14},{9,15},{10,... | collective-permute-start | bytes 393224 | tf_op jit(solution)/shard_map/ppermute | solution.py:67
  97.7 1.6 %copy-done.7 = f32[256,2048]{1,0:T(8,128)S(1)} copy-done((f32[256,2048]{1,0:T(8,128)S(1)}, f32[256,2048]{1,0:T(8,128)}, u32[]{:S(2)}) %copy-start.7) | copy-done | bytes 2097176
  99.3 1.2 copy-done.10
  100.5 0.9 copy-done.12
  102.1 2.2 %mixed.1 = (bf16[256,2048]{1,0:T(8,128)(2,1)}, f32[48,2048]{1,0:T(8,128)S(1)}) custom-call(s32[1]{0:T(128)} %bitcast.1.k_ref, s32[1]{0:T(128)S(6)} %min.7.from_ref, bf16[256,2048]{1,0:T(8,128)(2,1)S(1)} %copy-done.10, f32[256,2048]{1,0:T(8,128)S(1)} %copy-done.7, bf16[256,2048]{1,0:T(8,128)(2,1)S(1)} %copy-done.2, bf16[1024,128]{1,0:T(8,128)(2,1)S(1)} %copy-done.12, ...), custom_call_target="tpu_custom_call" | custom-call | flops 134217728 | bytes 7340032 | tf_op jit(solution)/shard_map/mixed/pallas_call | solution.py:552
  104.4 5.5 %expert.1 = (bf16[64,1024]{1,0:T(8,128)(2,1)S(1)}, bf16[64,1024]{1,0:T(8,128)(2,1)S(1)}, bf16[64,1024]{1,0:T(8,128)(2,1)S(1)}, bf16[64,1024]{1,0:T(8,128)(2,1)S(1)}, bf16[2,256,512]{2,1,0:T(8,128)(2,1)S(1)}) custom-call(bf16[64,1024]{1,0:T(8,128)(2,1)S(1)} %get-tuple-element.113.refs_0_, bf16[64,1024]{1,0:T(8,128)(2,1)S(1)} %collective-permute-done.8.refs_1_, ...), custom_call_target="tpu_custom_call" | custom-call | flops 2684354560 | bytes 12582912 | tf_op jit(solution)/shard_map/expert/pallas_call | solution.py:569
  109.9 1.2 collective-permute-start.20
  111.1 0.7 collective-permute-start.21
  111.8 1.7 %collective-permute-start.22 = (bf16[64,1024]{1,0:T(8,128)(2,1)S(1)}, bf16[64,1024]{1,0:T(8,128)(2,1)S(1)}, u32[]{:S(2)}, u32[]{:S(2)}) collective-permute-start(bf16[64,1024]{1,0:T(8,128)(2,1)S(1)} %get-tuple-element.127), channel_id=1, source_target_pairs={{0,6},{1,7},{2,4},{3,5},{4,2},{5,3},{6,0},{7,1},{8,14},{9,15},{10,... | collective-permute-start | bytes 393224 | tf_op jit(solution)/shard_map/ppermute | solution.py:67
  113.5 2.2 %down.1 = (bf16[64,1024]{1,0:T(8,128)(2,1)S(1)}, bf16[64,1024]{1,0:T(8,128)(2,1)S(1)}, bf16[64,1024]{1,0:T(8,128)(2,1)S(1)}, bf16[64,1024]{1,0:T(8,128)(2,1)S(1)}) custom-call(bf16[2,256,512]{2,1,0:T(8,128)(2,1)S(1)} %get-tuple-element.132.hid_ref, bf16[512,2048]{1,0:T(8,128)(2,1)S(1)} %copy-done.1, bf16[512,2048]{1,0:T(8,128)(2,1)} %collective-permute-done.19.refs_13_.d1), custom_call_target="tpu_custom_call" | custom-call | flops 536870912 | bytes 2097152 | tf_op jit(solution)/shard_map/down/pallas_call | solution.py:585
  115.7 1.2 collective-permute-start.26
  116.8 0.7 collective-permute-start.27
  117.6 1.7 %collective-permute-start.28 = (bf16[64,1024]{1,0:T(8,128)(2,1)S(1)}, bf16[64,1024]{1,0:T(8,128)(2,1)S(1)}, u32[]{:S(2)}, u32[]{:S(2)}) collective-permute-start(bf16[64,1024]{1,0:T(8,128)(2,1)S(1)} %get-tuple-element.136), channel_id=1, source_target_pairs={{0,6},{1,7},{2,4},{3,5},{4,2},{5,3},{6,0},{7,1},{8,14},{9,15},{10,... | collective-permute-start | bytes 393224 | tf_op jit(solution)/shard_map/ppermute | solution.py:67
  120.2 2.4 %collective-permute-start.24 = (bf16[32,1024]{1,0:T(8,128)(2,1)S(1)}, bf16[32,1024]{1,0:T(8,128)(2,1)S(1)}, u32[]{:S(2)}, u32[]{:S(2)}) collective-permute-start(bf16[32,1024]{1,0:T(8,128)(2,1)S(1)} %get-tuple-element.130), channel_id=1, source_target_pairs={{0,16},{1,17},{2,18},{3,19},{4,20},{5,21},{6,22},{7,23},{8,24},{9,... | collective-permute-start | bytes 196616 | tf_op jit(solution)/shard_map/ppermute | solution.py:67
  122.6 1.4 %collective-permute-start.25 = (bf16[32,1024]{1,0:T(8,128)(2,1)S(1)}, bf16[32,1024]{1,0:T(8,128)(2,1)S(1)}, u32[]{:S(2)}, u32[]{:S(2)}) collective-permute-start(bf16[32,1024]{1,0:T(8,128)(2,1)S(1)} %get-tuple-element.131), channel_id=1, source_target_pairs={{0,24},{1,25},{2,26},{3,27},{4,28},{5,29},{6,30},{7,31},{8,16},{9,... | collective-permute-start | bytes 196616 | tf_op jit(solution)/shard_map/ppermute | solution.py:67
  124.5 2.9 %collective-permute-start.30 = (bf16[32,1024]{1,0:T(8,128)(2,1)S(1)}, bf16[32,1024]{1,0:T(8,128)(2,1)S(1)}, u32[]{:S(2)}, u32[]{:S(2)}) collective-permute-start(bf16[32,1024]{1,0:T(8,128)(2,1)S(1)} %get-tuple-element.139), channel_id=1, source_target_pairs={{0,16},{1,17},{2,18},{3,19},{4,20},{5,21},{6,22},{7,23},{8,24},{9,... | collective-permute-start | bytes 196616 | tf_op jit(solution)/shard_map/ppermute | solution.py:67
  127.4 1.4 %collective-permute-start.31 = (bf16[32,1024]{1,0:T(8,128)(2,1)S(1)}, bf16[32,1024]{1,0:T(8,128)(2,1)S(1)}, u32[]{:S(2)}, u32[]{:S(2)}) collective-permute-start(bf16[32,1024]{1,0:T(8,128)(2,1)S(1)} %get-tuple-element.140), channel_id=1, source_target_pairs={{0,24},{1,25},{2,26},{3,27},{4,28},{5,29},{6,30},{7,31},{8,16},{9,... | collective-permute-start | bytes 196616 | tf_op jit(solution)/shard_map/ppermute | solution.py:67
  128.8 1.2 collective-permute-done.29.refs_5_
  130.1 3.4 %collective-permute-done.31.refs_7_ = bf16[32,1024]{1,0:T(8,128)(2,1)S(1)} collective-permute-done((bf16[32,1024]{1,0:T(8,128)(2,1)S(1)}, bf16[32,1024]{1,0:T(8,128)(2,1)S(1)}, u32[]{:S(2)}, u32[]{:S(2)}) %collective-permute-start.31) | collective-permute-done | bytes 65568 | tf_op jit(solution)/shard_map/ppermute | solution.py:67
  133.5 1.0 final.1
  (88 shorter events, 10.9 us)
Async XLA Ops:
  0.0 7.0 %copy-start = (bf16[512,2048]{1,0:T(8,128)(2,1)S(1)}, bf16[512,2048]{1,0:T(8,128)(2,1)}, u32[]{:S(2)}) copy-start(bf16[512,2048]{1,0:T(8,128)(2,1)} %d0) | copy-start | bytes 6291460
  0.0 18.3 %copy-start.33 = (s32[256]{0:T(256)S(1)}, s32[256]{0:T(256)}, u32[]{:S(2)}) copy-start(s32[256]{0:T(256)} %param.22) | copy-start | bytes 3076
  4.3 2.3 %collective-permute-start = (f32[1032,128]{1,0:T(8,128)}, f32[1032,128]{1,0:T(8,128)S(1)}, u32[]{:S(2)}, u32[]{:S(2)}) collective-permute-start(f32[1032,128]{1,0:T(8,128)} %get-tuple-element.75), channel_id=1, source_target_pairs={{0,1},{1,0},{2,3},{3,2},{4,5},{5,4},{6,7},{7,6},{8,9},{9,8},{10,11... | collective-permute-start | bytes 1585160 | tf_op jit(solution)/shard_map/ppermute | solution.py:63
  6.5 97.8 %collective-permute-start.17 = (bf16[2048,512]{1,0:T(8,128)(2,1)}, bf16[2048,512]{1,0:T(8,128)(2,1)}, u32[]{:S(2)}, u32[]{:S(2)}) collective-permute-start(bf16[2048,512]{1,0:T(8,128)(2,1)} %refs_8_), channel_id=1, source_target_pairs={{0,1},{1,0},{2,3},{3,2},{4,5},{5,4},{6,7},{7,6},{8,9},{9,8},{10,11... | collective-permute-start | bytes 6291464 | tf_op jit(solution)/shard_map/ppermute | solution.py:63
  6.9 97.5 %collective-permute-start.18 = (bf16[2048,512]{1,0:T(8,128)(2,1)}, bf16[2048,512]{1,0:T(8,128)(2,1)}, u32[]{:S(2)}, u32[]{:S(2)}) collective-permute-start(bf16[2048,512]{1,0:T(8,128)(2,1)} %refs_9_), channel_id=1, source_target_pairs={{0,1},{1,0},{2,3},{3,2},{4,5},{5,4},{6,7},{7,6},{8,9},{9,8},{10,11... | collective-permute-start | bytes 6291464 | tf_op jit(solution)/shard_map/ppermute | solution.py:63
  7.0 97.3 %collective-permute-start.19 = (bf16[512,2048]{1,0:T(8,128)(2,1)S(1)}, bf16[512,2048]{1,0:T(8,128)(2,1)}, u32[]{:S(2)}, u32[]{:S(2)}) collective-permute-start(bf16[512,2048]{1,0:T(8,128)(2,1)S(1)} %copy-done), channel_id=1, source_target_pairs={{0,1},{1,0},{2,3},{3,2},{4,5},{5,4},{6,7},{7,6},{8,9},{9,8},{10,11... | collective-permute-start | bytes 6291464 | tf_op jit(solution)/shard_map/ppermute | solution.py:63
  7.4 1.0 copy-start.3
  9.5 0.8 copy-start.5
  10.2 19.9 %all-to-all-start = ((bf16[16,80,128]{2,1,0:T(8,128)(2,1)}), bf16[16,80,128]{2,1,0:T(8,128)(2,1)S(1)}, u32[]{:S(2)}, u32[]{:S(2)}) async-start(bf16[16,80,128]{2,1,0:T(8,128)(2,1)} %pair.1), calls=%async_computation | async-start | bytes 655360 | tf_op jit(solution)/shard_map/all_to_all | solution.py:73
  30.2 0.7 copy-start.9
  30.9 66.8 %copy-start.2 = (bf16[256,2048]{1,0:T(8,128)(2,1)S(1)}, bf16[256,2048]{1,0:T(8,128)(2,1)}, u32[]{:S(2)}) copy-start(bf16[256,2048]{1,0:T(8,128)(2,1)} %stream_ref.3) | copy-start | bytes 3145732
  30.9 17.5 %all-to-all-start.1 = ((bf16[16,64,128]{2,1,0:T(8,128)(2,1)}), bf16[16,64,128]{2,1,0:T(8,128)(2,1)S(1)}, u32[]{:S(2)}, u32[]{:S(2)}) async-start(bf16[16,64,128]{2,1,0:T(8,128)(2,1)} %copy-done.9), calls=%async_computation.1 | async-start | bytes 524288 | tf_op jit(solution)/shard_map/all_to_all | solution.py:73
  36.5 5.2 %collective-permute-start.1 = (bf16[192,32]{1,0:T(8,128)(2,1)}, bf16[192,32]{1,0:T(8,128)(2,1)S(1)}, u32[]{:S(2)}, u32[]{:S(2)}) collective-permute-start(bf16[192,32]{1,0:T(8,128)(2,1)} %get-tuple-element.86), channel_id=1, source_target_pairs={{0,8},{1,9},{2,10},{3,11},{4,12},{5,13},{6,14},{7,15},{8,0},{9,1},... | collective-permute-start | bytes 36872 | tf_op jit(solution)/shard_map/ppermute | solution.py:67
  38.4 7.1 %collective-permute-start.2 = (bf16[192,32]{1,0:T(8,128)(2,1)}, bf16[192,32]{1,0:T(8,128)(2,1)S(1)}, u32[]{:S(2)}, u32[]{:S(2)}) collective-permute-start(bf16[192,32]{1,0:T(8,128)(2,1)} %get-tuple-element.87), channel_id=1, source_target_pairs={{0,16},{1,17},{2,18},{3,19},{4,20},{5,21},{6,22},{7,23},{8,24},{9,... | collective-permute-start | bytes 36872 | tf_op jit(solution)/shard_map/ppermute | solution.py:67
  41.7 6.1 %collective-permute-start.3 = (bf16[192,32]{1,0:T(8,128)(2,1)}, bf16[192,32]{1,0:T(8,128)(2,1)S(1)}, u32[]{:S(2)}, u32[]{:S(2)}) collective-permute-start(bf16[192,32]{1,0:T(8,128)(2,1)} %get-tuple-element.88), channel_id=1, source_target_pairs={{0,24},{1,25},{2,26},{3,27},{4,28},{5,29},{6,30},{7,31},{8,16},{9,... | collective-permute-start | bytes 36872 | tf_op jit(solution)/shard_map/ppermute | solution.py:67
  47.8 0.6 copy-start.14
  48.4 1.0 copy-start.4
  49.5 1.0 copy-start.6
  50.5 24.9 %copy-start.13 = (bf16[192,32]{1,0:T(8,128)(2,1)S(1)}, bf16[192,32]{1,0:T(8,128)(2,1)}, u32[]{:S(2)}) copy-start(bf16[192,32]{1,0:T(8,128)(2,1)} %get-tuple-element.94.refs_0_) | copy-start | bytes 36868
  51.0 1.6 %collective-permute-start.4 = (bf16[1024,128]{1,0:T(8,128)(2,1)S(1)}, bf16[1024,128]{1,0:T(8,128)(2,1)S(1)}, u32[]{:S(2)}, u32[]{:S(2)}) collective-permute-start(bf16[1024,128]{1,0:T(8,128)(2,1)S(1)} %get-tuple-element.91), channel_id=1, source_target_pairs={{0,1},{1,0},{2,3},{3,2},{4,5},{5,4},{6,7},{7,6},{8,9},{9,8},{10,11... | collective-permute-start | bytes 786440 | tf_op jit(solution)/shard_map/ppermute | solution.py:63
  52.6 1.0 copy-start.17
  53.6 0.9 copy-start.18
  54.5 0.9 copy-start.19
  55.4 0.7 copy-start.30
  56.1 0.7 copy-start.32
  57.9 0.7 copy-start.11
  58.5 4.3 %collective-permute-start.5 = (bf16[32,1024]{1,0:T(8,128)(2,1)S(1)}, bf16[32,1024]{1,0:T(8,128)(2,1)S(1)}, u32[]{:S(2)}, u32[]{:S(2)}) collective-permute-start(bf16[32,1024]{1,0:T(8,128)(2,1)S(1)} %get-tuple-element.101.refs_4_), channel_id=1, source_target_pairs={{0,8},{1,9},{2,10},{3,11},{4,12},{5,13},{6,14},{7,15},{8,0},{9,1},... | collective-permute-start | bytes 196616 | tf_op jit(solution)/shard_map/ppermute | solution.py:67
  58.5 9.6 %collective-permute-start.6 = (bf16[32,1024]{1,0:T(8,128)(2,1)S(1)}, bf16[32,1024]{1,0:T(8,128)(2,1)S(1)}, u32[]{:S(2)}, u32[]{:S(2)}) collective-permute-start(bf16[32,1024]{1,0:T(8,128)(2,1)S(1)} %get-tuple-element.101.refs_4_), channel_id=1, source_target_pairs={{0,16},{1,17},{2,18},{3,19},{4,20},{5,21},{6,22},{7,23},{8,24},{9,... | collective-permute-start | bytes 196616 | tf_op jit(solution)/shard_map/ppermute | solution.py:67
  63.4 7.0 %collective-permute-start.7 = (bf16[32,1024]{1,0:T(8,128)(2,1)S(1)}, bf16[32,1024]{1,0:T(8,128)(2,1)S(1)}, u32[]{:S(2)}, u32[]{:S(2)}) collective-permute-start(bf16[32,1024]{1,0:T(8,128)(2,1)S(1)} %get-tuple-element.101.refs_4_), channel_id=1, source_target_pairs={{0,24},{1,25},{2,26},{3,27},{4,28},{5,29},{6,30},{7,31},{8,16},{9,... | collective-permute-start | bytes 196616 | tf_op jit(solution)/shard_map/ppermute | solution.py:67
  67.5 0.6 copy-start.20
  68.8 4.7 %collective-permute-start.11 = (bf16[32,1024]{1,0:T(8,128)(2,1)}, bf16[32,1024]{1,0:T(8,128)(2,1)S(1)}, u32[]{:S(2)}, u32[]{:S(2)}) collective-permute-start(bf16[32,1024]{1,0:T(8,128)(2,1)} %get-tuple-element.106.refs_4_), channel_id=1, source_target_pairs={{0,8},{1,9},{2,10},{3,11},{4,12},{5,13},{6,14},{7,15},{8,0},{9,1},... | collective-permute-start | bytes 196616 | tf_op jit(solution)/shard_map/ppermute | solution.py:67
  71.0 8.8 %collective-permute-start.12 = (bf16[32,1024]{1,0:T(8,128)(2,1)}, bf16[32,1024]{1,0:T(8,128)(2,1)}, u32[]{:S(2)}, u32[]{:S(2)}) collective-permute-start(bf16[32,1024]{1,0:T(8,128)(2,1)} %get-tuple-element.106.refs_4_), channel_id=1, source_target_pairs={{0,16},{1,17},{2,18},{3,19},{4,20},{5,21},{6,22},{7,23},{8,24},{9,... | collective-permute-start | bytes 196616 | tf_op jit(solution)/shard_map/ppermute | solution.py:67
  74.1 7.3 %collective-permute-start.13 = (bf16[32,1024]{1,0:T(8,128)(2,1)}, bf16[32,1024]{1,0:T(8,128)(2,1)}, u32[]{:S(2)}, u32[]{:S(2)}) collective-permute-start(bf16[32,1024]{1,0:T(8,128)(2,1)} %get-tuple-element.106.refs_4_), channel_id=1, source_target_pairs={{0,24},{1,25},{2,26},{3,27},{4,28},{5,29},{6,30},{7,31},{8,16},{9,... | collective-permute-start | bytes 196616 | tf_op jit(solution)/shard_map/ppermute | solution.py:67
  75.4 0.8 copy-start.15
  76.2 0.8 copy-start.21
  77.0 0.8 copy-start.25
  77.9 0.8 copy-start.27
  78.7 0.8 copy-start.29
  79.8 7.0 %collective-permute-start.8 = (bf16[64,1024]{1,0:T(8,128)(2,1)S(1)}, bf16[64,1024]{1,0:T(8,128)(2,1)S(1)}, u32[]{:S(2)}, u32[]{:S(2)}) collective-permute-start(bf16[64,1024]{1,0:T(8,128)(2,1)S(1)} %get-tuple-element.103), channel_id=1, source_target_pairs={{0,2},{1,3},{2,0},{3,1},{4,6},{5,7},{6,4},{7,5},{8,10},{9,11},{10,... | collective-permute-start | bytes 393224 | tf_op jit(solution)/shard_map/ppermute | solution.py:67
  81.4 8.7 %collective-permute-start.9 = (bf16[64,1024]{1,0:T(8,128)(2,1)S(1)}, bf16[64,1024]{1,0:T(8,128)(2,1)S(1)}, u32[]{:S(2)}, u32[]{:S(2)}) collective-permute-start(bf16[64,1024]{1,0:T(8,128)(2,1)S(1)} %get-tuple-element.104), channel_id=1, source_target_pairs={{0,4},{1,5},{2,6},{3,7},{4,0},{5,1},{6,2},{7,3},{8,12},{9,13},{10,... | collective-permute-start | bytes 393224 | tf_op jit(solution)/shard_map/ppermute | solution.py:67
  83.2 0.8 copy-start.23
  86.8 7.0 %collective-permute-start.10 = (bf16[64,1024]{1,0:T(8,128)(2,1)S(1)}, bf16[64,1024]{1,0:T(8,128)(2,1)S(1)}, u32[]{:S(2)}, u32[]{:S(2)}) collective-permute-start(bf16[64,1024]{1,0:T(8,128)(2,1)S(1)} %get-tuple-element.105), channel_id=1, source_target_pairs={{0,6},{1,7},{2,4},{3,5},{4,2},{5,3},{6,0},{7,1},{8,14},{9,15},{10,... | collective-permute-start | bytes 393224 | tf_op jit(solution)/shard_map/ppermute | solution.py:67
  90.1 5.9 %collective-permute-start.14 = (bf16[64,1024]{1,0:T(8,128)(2,1)S(1)}, bf16[64,1024]{1,0:T(8,128)(2,1)S(1)}, u32[]{:S(2)}, u32[]{:S(2)}) collective-permute-start(bf16[64,1024]{1,0:T(8,128)(2,1)S(1)} %get-tuple-element.108), channel_id=1, source_target_pairs={{0,2},{1,3},{2,0},{3,1},{4,6},{5,7},{6,4},{7,5},{8,10},{9,11},{10,... | collective-permute-start | bytes 393224 | tf_op jit(solution)/shard_map/ppermute | solution.py:67
  93.8 10.5 %collective-permute-start.15 = (bf16[64,1024]{1,0:T(8,128)(2,1)S(1)}, bf16[64,1024]{1,0:T(8,128)(2,1)S(1)}, u32[]{:S(2)}, u32[]{:S(2)}) collective-permute-start(bf16[64,1024]{1,0:T(8,128)(2,1)S(1)} %get-tuple-element.109), channel_id=1, source_target_pairs={{0,4},{1,5},{2,6},{3,7},{4,0},{5,1},{6,2},{7,3},{8,12},{9,13},{10,... | collective-permute-start | bytes 393224 | tf_op jit(solution)/shard_map/ppermute | solution.py:67
  96.0 8.4 %collective-permute-start.16 = (bf16[64,1024]{1,0:T(8,128)(2,1)S(1)}, bf16[64,1024]{1,0:T(8,128)(2,1)S(1)}, u32[]{:S(2)}, u32[]{:S(2)}) collective-permute-start(bf16[64,1024]{1,0:T(8,128)(2,1)S(1)} %get-tuple-element.110), channel_id=1, source_target_pairs={{0,6},{1,7},{2,4},{3,5},{4,2},{5,3},{6,0},{7,1},{8,14},{9,15},{10,... | collective-permute-start | bytes 393224 | tf_op jit(solution)/shard_map/ppermute | solution.py:67
  97.7 1.6 %copy-start.7 = (f32[256,2048]{1,0:T(8,128)S(1)}, f32[256,2048]{1,0:T(8,128)}, u32[]{:S(2)}) copy-start(f32[256,2048]{1,0:T(8,128)} %get-tuple-element.83.inside_ref) | copy-start | bytes 6291460
  99.3 1.2 copy-start.10
  100.5 0.9 copy-start.12
  101.4 0.7 copy-start.31
  102.1 2.3 %copy-start.8 = (bf16[2048,512]{1,0:T(8,128)(2,1)S(1)}, bf16[2048,512]{1,0:T(8,128)(2,1)}, u32[]{:S(2)}) copy-start(bf16[2048,512]{1,0:T(8,128)(2,1)} %refs_8_) | copy-start | bytes 6291460
  104.4 9.1 %copy-start.1 = (bf16[512,2048]{1,0:T(8,128)(2,1)S(1)}, bf16[512,2048]{1,0:T(8,128)(2,1)}, u32[]{:S(2)}) copy-start(bf16[512,2048]{1,0:T(8,128)(2,1)} %d0) | copy-start | bytes 6291460
  109.9 7.6 %collective-permute-start.20 = (bf16[64,1024]{1,0:T(8,128)(2,1)S(1)}, bf16[64,1024]{1,0:T(8,128)(2,1)S(1)}, u32[]{:S(2)}, u32[]{:S(2)}) collective-permute-start(bf16[64,1024]{1,0:T(8,128)(2,1)S(1)} %get-tuple-element.125), channel_id=1, source_target_pairs={{0,2},{1,3},{2,0},{3,1},{4,6},{5,7},{6,4},{7,5},{8,10},{9,11},{10,... | collective-permute-start | bytes 393224 | tf_op jit(solution)/shard_map/ppermute | solution.py:67
  111.1 8.1 %collective-permute-start.21 = (bf16[64,1024]{1,0:T(8,128)(2,1)S(1)}, bf16[64,1024]{1,0:T(8,128)(2,1)S(1)}, u32[]{:S(2)}, u32[]{:S(2)}) collective-permute-start(bf16[64,1024]{1,0:T(8,128)(2,1)S(1)} %get-tuple-element.126), channel_id=1, source_target_pairs={{0,4},{1,5},{2,6},{3,7},{4,0},{5,1},{6,2},{7,3},{8,12},{9,13},{10,... | collective-permute-start | bytes 393224 | tf_op jit(solution)/shard_map/ppermute | solution.py:67
  111.8 7.4 %collective-permute-start.22 = (bf16[64,1024]{1,0:T(8,128)(2,1)S(1)}, bf16[64,1024]{1,0:T(8,128)(2,1)S(1)}, u32[]{:S(2)}, u32[]{:S(2)}) collective-permute-start(bf16[64,1024]{1,0:T(8,128)(2,1)S(1)} %get-tuple-element.127), channel_id=1, source_target_pairs={{0,6},{1,7},{2,4},{3,5},{4,2},{5,3},{6,0},{7,1},{8,14},{9,15},{10,... | collective-permute-start | bytes 393224 | tf_op jit(solution)/shard_map/ppermute | solution.py:67
  113.5 5.7 %copy-start.16 = (bf16[192,32]{1,0:T(8,128)(2,1)S(1)}, bf16[192,32]{1,0:T(8,128)(2,1)}, u32[]{:S(2)}) copy-start(bf16[192,32]{1,0:T(8,128)(2,1)} %copy-done.14) | copy-start | bytes 36868
  115.7 6.9 %collective-permute-start.26 = (bf16[64,1024]{1,0:T(8,128)(2,1)S(1)}, bf16[64,1024]{1,0:T(8,128)(2,1)S(1)}, u32[]{:S(2)}, u32[]{:S(2)}) collective-permute-start(bf16[64,1024]{1,0:T(8,128)(2,1)S(1)} %get-tuple-element.134), channel_id=1, source_target_pairs={{0,2},{1,3},{2,0},{3,1},{4,6},{5,7},{6,4},{7,5},{8,10},{9,11},{10,... | collective-permute-start | bytes 393224 | tf_op jit(solution)/shard_map/ppermute | solution.py:67
  116.8 7.2 %collective-permute-start.27 = (bf16[64,1024]{1,0:T(8,128)(2,1)S(1)}, bf16[64,1024]{1,0:T(8,128)(2,1)S(1)}, u32[]{:S(2)}, u32[]{:S(2)}) collective-permute-start(bf16[64,1024]{1,0:T(8,128)(2,1)S(1)} %get-tuple-element.135), channel_id=1, source_target_pairs={{0,4},{1,5},{2,6},{3,7},{4,0},{5,1},{6,2},{7,3},{8,12},{9,13},{10,... | collective-permute-start | bytes 393224 | tf_op jit(solution)/shard_map/ppermute | solution.py:67
  117.6 6.5 %collective-permute-start.28 = (bf16[64,1024]{1,0:T(8,128)(2,1)S(1)}, bf16[64,1024]{1,0:T(8,128)(2,1)S(1)}, u32[]{:S(2)}, u32[]{:S(2)}) collective-permute-start(bf16[64,1024]{1,0:T(8,128)(2,1)S(1)} %get-tuple-element.136), channel_id=1, source_target_pairs={{0,6},{1,7},{2,4},{3,5},{4,2},{5,3},{6,0},{7,1},{8,14},{9,15},{10,... | collective-permute-start | bytes 393224 | tf_op jit(solution)/shard_map/ppermute | solution.py:67
  119.6 7.8 %collective-permute-start.23 = (bf16[32,1024]{1,0:T(8,128)(2,1)S(1)}, bf16[32,1024]{1,0:T(8,128)(2,1)S(1)}, u32[]{:S(2)}, u32[]{:S(2)}) collective-permute-start(bf16[32,1024]{1,0:T(8,128)(2,1)S(1)} %get-tuple-element.129), channel_id=1, source_target_pairs={{0,8},{1,9},{2,10},{3,11},{4,12},{5,13},{6,14},{7,15},{8,0},{9,1},... | collective-permute-start | bytes 196616 | tf_op jit(solution)/shard_map/ppermute | solution.py:67
  120.2 8.7 %collective-permute-start.24 = (bf16[32,1024]{1,0:T(8,128)(2,1)S(1)}, bf16[32,1024]{1,0:T(8,128)(2,1)S(1)}, u32[]{:S(2)}, u32[]{:S(2)}) collective-permute-start(bf16[32,1024]{1,0:T(8,128)(2,1)S(1)} %get-tuple-element.130), channel_id=1, source_target_pairs={{0,16},{1,17},{2,18},{3,19},{4,20},{5,21},{6,22},{7,23},{8,24},{9,... | collective-permute-start | bytes 196616 | tf_op jit(solution)/shard_map/ppermute | solution.py:67
  122.6 6.2 %collective-permute-start.25 = (bf16[32,1024]{1,0:T(8,128)(2,1)S(1)}, bf16[32,1024]{1,0:T(8,128)(2,1)S(1)}, u32[]{:S(2)}, u32[]{:S(2)}) collective-permute-start(bf16[32,1024]{1,0:T(8,128)(2,1)S(1)} %get-tuple-element.131), channel_id=1, source_target_pairs={{0,24},{1,25},{2,26},{3,27},{4,28},{5,29},{6,30},{7,31},{8,16},{9,... | collective-permute-start | bytes 196616 | tf_op jit(solution)/shard_map/ppermute | solution.py:67
  124.4 5.7 %collective-permute-start.29 = (bf16[32,1024]{1,0:T(8,128)(2,1)S(1)}, bf16[32,1024]{1,0:T(8,128)(2,1)S(1)}, u32[]{:S(2)}, u32[]{:S(2)}) collective-permute-start(bf16[32,1024]{1,0:T(8,128)(2,1)S(1)} %get-tuple-element.138), channel_id=1, source_target_pairs={{0,8},{1,9},{2,10},{3,11},{4,12},{5,13},{6,14},{7,15},{8,0},{9,1},... | collective-permute-start | bytes 196616 | tf_op jit(solution)/shard_map/ppermute | solution.py:67
  124.5 5.6 %collective-permute-start.30 = (bf16[32,1024]{1,0:T(8,128)(2,1)S(1)}, bf16[32,1024]{1,0:T(8,128)(2,1)S(1)}, u32[]{:S(2)}, u32[]{:S(2)}) collective-permute-start(bf16[32,1024]{1,0:T(8,128)(2,1)S(1)} %get-tuple-element.139), channel_id=1, source_target_pairs={{0,16},{1,17},{2,18},{3,19},{4,20},{5,21},{6,22},{7,23},{8,24},{9,... | collective-permute-start | bytes 196616 | tf_op jit(solution)/shard_map/ppermute | solution.py:67
  127.4 6.1 %collective-permute-start.31 = (bf16[32,1024]{1,0:T(8,128)(2,1)S(1)}, bf16[32,1024]{1,0:T(8,128)(2,1)S(1)}, u32[]{:S(2)}, u32[]{:S(2)}) collective-permute-start(bf16[32,1024]{1,0:T(8,128)(2,1)S(1)} %get-tuple-element.140), channel_id=1, source_target_pairs={{0,24},{1,25},{2,26},{3,27},{4,28},{5,29},{6,30},{7,31},{8,16},{9,... | collective-permute-start | bytes 196616 | tf_op jit(solution)/shard_map/ppermute | solution.py:67
  (4 other events, 2.5 us)

commit v4 on v3

--- a/solution.py
+++ b/solution.py
@@ -9,7 +9,7 @@
 
 CAP = 16
 TAIL = 8
-TAIL16 = 16
+DECAYS = 3
 ATTN_EPS = 1e-05
 NORM_EPS = 1e-06
 PLANES = 4
@@ -23,7 +23,7 @@
 
 
 def params(mb=60):
-    return pltpu.CompilerParams(vmem_limit_bytes=mb * 1024 * 1024)
+    return pltpu.CompilerParams(vmem_limit_bytes=int(mb * 1024 * 1024))
 
 
 def full(x):
@@ -112,14 +112,15 @@
         c.wait()
 
 
-def pair_kernel(k_ref, own_ref, recv_ref, out_ref, *, half, rows):
+def pair_kernel(k_ref, own_ref, recv_ref, notes_ref, out_ref, first_ref, *, half, rows):
     hd = own_ref.shape[1]
     first = k_ref[0] == 0
     base = half * hd
     mine = own_ref[base : base + 1, :]
     theirs = recv_ref[base : base + 1, :]
     pieces = out_ref.shape[0]
-    tail_row = lax.broadcasted_iota(jnp.int32, (TAIL16, hd), 0)
+    planes, tail_rows = notes_ref.shape[:2]
+    tail_row = lax.broadcasted_iota(jnp.int32, (tail_rows, hd), 0)
     for p in range(pieces):
         j = p * rows // hd
         mt = mine[:, j : j + 1]
@@ -130,12 +131,16 @@
         lo = p * rows
         chip = own_ref[lo : lo + rows, :] * a + recv_ref[lo : lo + rows, :] * b
         out_ref[p, 0:rows, :] = chip.astype(BF16)
-        d = jnp.broadcast_to(jnp.exp(mt + pt), (TAIL16, hd))
+        d = jnp.broadcast_to(jnp.exp(mt + pt), (tail_rows, hd))
+        notes = notes_ref[p * planes // pieces].astype(F32)
         d0 = d.astype(BF16).astype(F32)
         d1 = (d - d0).astype(BF16).astype(F32)
         d2 = d - d0 - d1
-        tail = jnp.where(tail_row == 0, d0, jnp.where(tail_row == 1, d1, jnp.where(tail_row == 2, d2, 0.0)))
-        out_ref[p, rows : rows + TAIL16, :] = tail.astype(BF16)
+        first_ref[lo : lo + rows, :] = jnp.where(first, own_ref[lo : lo + rows, :], recv_ref[lo : lo + rows, :])
+        tail = jnp.where(tail_row == 0, d0, jnp.where(tail_row == 1, d1, jnp.where(tail_row == 2, d2, notes)))
+        out_ref[p, rows:, :] = tail.astype(BF16)
+    rolled = pltpu.roll(theirs, hd - half, 1)
+    first_ref[base:, :] = jnp.broadcast_to(jnp.where(first, mine, rolled), (TAIL, hd))
 
 
 def scan_kernel(in_ref, out_ref):
@@ -143,36 +148,24 @@
     state = jnp.zeros((rows, hd), F32)
     for c in range(count):
         out_ref[c, :, :] = state.astype(BF16)
-        tail = in_ref[c, rows : rows + TAIL16, :].astype(F32)
+        tail = in_ref[c, rows:, :].astype(F32)
         d = tail[0:1, :] + tail[1:2, :] + tail[2:3, :]
         state = state * d + in_ref[c, 0:rows, :].astype(F32)
 
 
-def split_kernel(k_ref, pref_ref, own_hbm, recv_hbm, keep_ref, give_ref, first_ref, sem, *, half):
+def split_kernel(k_ref, pref_ref, first_ref, keep_ref, give_ref, *, half):
     hd = first_ref.shape[1]
     even = k_ref[0] == 0
-    base = half * hd
-
-    @pl.when(even)
-    def _():
-        pltpu.make_async_copy(own_hbm, first_ref, sem).start()
-
-    @pl.when(jnp.logical_not(even))
-    def _():
-        pltpu.make_async_copy(recv_hbm, first_ref, sem).start()
-
-    pltpu.make_async_copy(own_hbm, first_ref, sem).wait()
-    logs = first_ref[base : base + 1, :]
+    logs = first_ref[half * hd : half * hd + 1, :]
     for j in range(half):
         sl = slice(j * hd, (j + 1) * hd)
-        d0 = jnp.exp(jnp.where(even, logs[:, j : j + 1], logs[:, half + j : half + j + 1]))
         before = pref_ref[sl, :].astype(F32)
-        after = before * d0 + first_ref[sl, :]
+        after = before * jnp.exp(logs[:, j : j + 1]) + first_ref[sl, :]
         keep_ref[sl, :] = jnp.where(even, before, after).astype(BF16)
         give_ref[sl, :] = jnp.where(even, after, before).astype(BF16)
 
 
-def inside_kernel(start_ref, dec_ref, q_ref, key_ref, val_ref, stream_ref, inside_ref, lifted_ref, ir_ref, lr_ref, sr_ref):
+def inside_kernel(start_ref, dec_ref, q_ref, key_ref, val_ref, stream_ref, inside_ref, lifted_ref, near_ref):
     heads, tok = dec_ref.shape
     hd = q_ref.shape[1] // heads
     dec = dec_ref[...]
@@ -181,7 +174,7 @@
     lift = jnp.exp(run_c)
     cut = tok // 2
     tri = lower_tri(cut)
-    resp = ir_ref.shape[0]
+    resp = near_ref.shape[0] // 3
     start = start_ref[0]
     picked = lax.broadcasted_iota(jnp.int32, (resp, tok), 0) + start
     pick = jnp.where(lax.broadcasted_iota(jnp.int32, (resp, tok), 1) == picked, 1.0, 0.0).astype(BF16)
@@ -202,38 +195,37 @@
         w_b = (s_b * jnp.concatenate([f_ba, f_bb], axis=1)).astype(BF16)
         inside_ref[:cut, cols] = mm(w_aa, v[:cut])
         inside_ref[cut:, cols] = mm(w_b, v)
-    lr_ref[...] = mm(pick, lifted_ref[...]).astype(BF16)
-    sr_ref[...] = mm(pick, stream_ref[...]).astype(BF16)
+    near_ref[resp : 2 * resp, :] = mm(pick, lifted_ref[...])
+    near_ref[2 * resp :, :] = mm(pick, stream_ref[...])
     rest = inside_ref[...]
     high = rest.astype(BF16)
     rest = rest - high.astype(F32)
     mid = rest.astype(BF16)
     low = (rest - mid.astype(F32)).astype(BF16)
-    ir_ref[...] = mm(pick, high) + mm(pick, mid) + mm(pick, low)
+    near_ref[:resp, :] = mm(pick, high) + mm(pick, mid) + mm(pick, low)
 
 
 def head_norm(att):
     return att * lax.rsqrt(jnp.mean(att * att, axis=-1, keepdims=True) + ATTN_EPS)
 
 
-def rows_kernel(k_ref, lifted_ref, inside_ref, stream_ref, keep_ref, other_ref, again_ref, fgain_ref, *refs):
-    *out_refs, mixed_ref = refs
+def rows_kernel(k_ref, near_ref, keep_ref, other_ref, again_ref, fgain_ref, disp_ref, sent_ref, mixed_ref):
     hd = keep_ref.shape[1]
     half = keep_ref.shape[0] // hd
     k = k_ref[0]
+    resp = near_ref.shape[0] // 3
     for r in range(2 * half):
         side = r // half
         off = pl.multiple_of((side ^ k) * (half * hd) + (r % half) * hd, hd)
         cols = pl.ds(off, hd)
         src = keep_ref if side == 0 else other_ref
-        att = inside_ref[:, cols] + mm(lifted_ref[:, cols], src[(r % half) * hd : (r % half + 1) * hd, :])
-        mixed_ref[:, cols] = stream_ref[:, cols].astype(F32) + head_norm(att) * again_ref[:, cols]
+        lifted = near_ref[resp : 2 * resp, cols].astype(BF16)
+        att = near_ref[:resp, cols] + mm(lifted, src[(r % half) * hd : (r % half + 1) * hd, :])
+        mixed_ref[:, cols] = near_ref[2 * resp :, cols] + head_norm(att) * again_ref[:, cols]
     mixed = mixed_ref[...]
     scale = lax.rsqrt(jnp.mean(mixed * mixed, axis=-1, keepdims=True) + NORM_EPS)
     ffn = (mixed * scale * fgain_ref[...]).astype(BF16)
-    part = ffn.shape[1] // len(out_refs)
-    for c, out_ref in enumerate(out_refs):
-        out_ref[...] = ffn[:, c * part : (c + 1) * part]
+    sent_ref[...] = mm(disp_ref[...], ffn).astype(BF16)
 
 
 def mixed_kernel(k_ref, from_ref, lifted_ref, inside_ref, stream_ref, keep_ref, other_ref, again_ref, base_ref, near_ref, mixed_ref):
@@ -249,13 +241,22 @@
     near_ref[...] = mixed_ref[pl.ds(pl.multiple_of(from_ref[0], 16), near_ref.shape[0]), :]
 
 
-def route_kernel(start_ref, plane_ref, ids_ref, wts_ref, live_ref, *refs, experts):
-    *out_refs, tab_ref = refs
+def noted(experts, resp, lanes):
+    side = max(1, lanes // resp)
+    return side, -(-experts // side)
+
+
+def shift_table(resp, lanes, g, rows):
+    j = lax.broadcasted_iota(jnp.int32, (resp, lanes) if rows else (lanes, resp), 0 if rows else 1)
+    lane = lax.broadcasted_iota(jnp.int32, (resp, lanes) if rows else (lanes, resp), 1 if rows else 0)
+    return jnp.where(lane == j + g * resp, 1.0, 0.0).astype(BF16)
+
+
+def route_kernel(ids_ref, wts_ref, live_ref, disp_ref, notes_ref, *, experts):
     top, tok = ids_ref.shape
-    slots = experts * CAP
-    planes = len(out_refs)
-    span = slots // planes
-    resp = tab_ref.shape[2]
+    slots, resp = disp_ref.shape
+    planes, tail_rows, lanes = notes_ref.shape
+    count = experts // planes
     live = live_ref[...] == 1
     e_row = lax.broadcasted_iota(jnp.int32, (experts, tok), 0)
     chosen = jnp.zeros((experts, tok), F32)
@@ -276,16 +277,56 @@
     hit = mm(spread, place.astype(BF16)) == slot_of.astype(F32)
     w_hi = weight.astype(BF16)
     w_lo = (weight - w_hi.astype(F32)).astype(BF16)
-    picked = lax.broadcasted_iota(jnp.int32, (tok, resp), 1) + start_ref[0]
+    token = lax.broadcasted_iota(jnp.int32, (1, tok), 1)
+    start = jnp.min(jnp.where(live, token, tok - resp), axis=1, keepdims=True)
+    start = jnp.minimum(start, tok - resp)
+    picked = lax.broadcasted_iota(jnp.int32, (tok, resp), 1) + start
     pick = jnp.where(lax.broadcasted_iota(jnp.int32, (tok, resp), 0) == picked, 1.0, 0.0).astype(BF16)
-    zero = jnp.zeros((slots, tok), F32)
-    tables = (jnp.where(hit, 1.0, zero), jnp.where(hit, mm(spread, w_hi), zero), jnp.where(hit, mm(spread, w_lo), zero))
-    for n, table in enumerate(tables):
-        table = mm(table.astype(BF16), pick).astype(BF16)
-        for p in range(planes):
-            tab_ref[p, n * span : (n + 1) * span, :] = table[p * span : (p + 1) * span, :]
-    for m, out_ref in enumerate(out_refs):
-        out_ref[...] = tab_ref[plane_ref[0] ^ m, :, :]
+    disp_ref[...] = mm(jnp.where(hit, 1.0, 0.0).astype(BF16), pick).astype(BF16)
+    side, each = noted(count, resp, lanes)
+    tail_row = lax.broadcasted_iota(jnp.int32, (tail_rows, lanes), 0)
+    notes = [jnp.zeros((tail_rows, lanes), F32)] * planes
+    for n, part in enumerate((w_hi, w_lo)):
+        part = mm(part, pick).astype(BF16)
+        placed = [mm(part, shift_table(resp, lanes, g, True)) for g in range(side)]
+        for e in range(experts):
+            at = e % count
+            line = placed[at % side][e : e + 1, :]
+            here = tail_row == DECAYS + n * each + at // side
+            notes[e // count] = notes[e // count] + jnp.where(here, line, 0.0)
+    for p in range(planes):
+        notes_ref[p, :, :] = notes[p].astype(BF16)
+
+
+def plan_kernel(at_ref, plane_ref, in_ref, *outs, planes, rows):
+    lanes = in_ref.shape[2]
+    resp = outs[0].shape[1]
+    span = outs[0].shape[0] // 2
+    count = span // CAP
+    side, each = noted(count, resp, lanes)
+    e_row = lax.broadcasted_iota(jnp.int32, (count, resp), 0)
+    before = lax.broadcasted_iota(jnp.int32, (resp, resp), 0) < lax.broadcasted_iota(jnp.int32, (resp, resp), 1)
+    before = jnp.where(before, 1.0, 0.0).astype(BF16)
+    s_row = lax.broadcasted_iota(jnp.int32, (span, count), 0)
+    e_col = lax.broadcasted_iota(jnp.int32, (span, count), 1)
+    spread = jnp.where(s_row // CAP == e_col, 1.0, 0.0).astype(BF16)
+    slot_of = (lax.broadcasted_iota(jnp.int32, (span, resp), 0) % CAP).astype(F32)
+    for m in range(planes):
+        pair = (plane_ref[0] ^ m) * count + at_ref[0]
+        tail = in_ref[pair, rows:, :]
+        moved = [mm(tail, shift_table(resp, lanes, g, False)) for g in range(side)]
+        parts = []
+        for n in range(2):
+            part = jnp.zeros((count, resp), F32)
+            for e in range(count):
+                r = DECAYS + n * each + e // side
+                part = part + jnp.where(e_row == e, moved[e % side][r : r + 1, :], 0.0)
+            parts.append(part.astype(BF16))
+        chosen = parts[0].astype(F32) > 0.0
+        place = mm(jnp.where(chosen, 1.0, 0.0).astype(BF16), before)
+        hit = mm(spread, jnp.where(chosen, place, -1.0).astype(BF16)) == slot_of
+        for n in range(2):
+            outs[m][n * span : (n + 1) * span, :] = jnp.where(hit, mm(spread, parts[n]), 0.0).astype(BF16)
 
 
 def table_rows(tab_ref, n, at, count):
@@ -294,36 +335,25 @@
     return jnp.concatenate(rows, axis=0)
 
 
-def gather_kernel(at_ref, *refs, planes, count):
-    tabs, rows, outs = refs[:planes], refs[planes : 2 * planes], refs[2 * planes :]
-    for m in range(planes):
-        got = mm(table_rows(tabs[m], 0, at_ref[0], count), rows[m][...]).astype(BF16)
-        for q in range(count):
-            outs[q][m * CAP : (m + 1) * CAP, :] = got[q * CAP : (q + 1) * CAP, :]
-
-
 def combine_kernel(at_ref, *refs, planes, count):
     tabs, results, outs = refs[:planes], refs[planes : planes + count], refs[planes + count :]
     for m in range(planes):
         got = jnp.concatenate([results[q][m * CAP : (m + 1) * CAP, :] for q in range(count)], axis=0)
-        hi = table_rows(tabs[m], 1, at_ref[0], count)
-        lo = table_rows(tabs[m], 2, at_ref[0], count)
+        hi = table_rows(tabs[m], 0, at_ref[0], count)
+        lo = table_rows(tabs[m], 1, at_ref[0], count)
         outs[m][...] = (mm(hi, got, 0, 0) + mm(lo, got, 0, 0)).astype(outs[m].dtype)
 
 
-def expert_kernel(*refs, count, parts, step):
-    xs, refs = refs[: count * parts], refs[count * parts :]
-    (g0, u0, d0, g1, u1, d1), refs = refs[:6], refs[6:]
-    outs, refs = refs[:count], refs[count:]
-    hid_out, gv, uv, dv, hid_ref, x_ref, sems = refs
+def expert_kernel(at_ref, plane_ref, x_hbm, g0, u0, d0, g1, u1, d1, *refs, count, parts, step):
+    outs, (gv, uv, dv, hid_ref, x_ref, sems) = refs[: count * parts], refs[count * parts :]
     units = g0.shape[1]
-    rows, part = xs[0].shape
+    rows, part = outs[0].shape
     cuts = range(0, units, step)
     gets = []
     for q in range(count):
-        for c in range(parts):
-            dst = x_ref.at[pl.ds(q * rows, rows), pl.ds(c * part, part)]
-            gets.append(copy(xs[c * count + q], dst, sems, len(gets)))
+        for m in range(rows // CAP):
+            pair = (plane_ref[0] ^ m) * count + (at_ref[0] ^ q)
+            gets.append(copy(x_hbm.at[pair], x_ref.at[pl.ds(q * rows + m * CAP, CAP)], sems, len(gets)))
     at = len(gets)
     for n, (g, u) in enumerate(((g0, u0), (g1, u1))):
         for c in cuts:
@@ -331,7 +361,7 @@
             gets.append(copy(g.at[:, cols], gv.at[n, :, cols], sems, len(gets)))
             gets.append(copy(u.at[:, cols], uv.at[n, :, cols], sems, len(gets)))
     for n, d in enumerate((d0, d1)):
-        gets.append(copy(d.at[:, pl.ds(0, part)], dv.at[n], sems, len(gets)))
+        gets.append(copy(d, dv.at[n], sems, len(gets)))
     for c in gets[:at]:
         c.wait()
     many = count * rows
@@ -346,32 +376,16 @@
                 gate = mm(x, gv[n, :, c : c + step])
                 up = mm(x, uv[n, :, c : c + step])
                 hid_ref[n, r : r + block, c : c + step] = (gate / (1.0 + jnp.exp(-gate)) * up).astype(BF16)
-    put = copy(hid_ref, hid_out, sems, len(gets))
     gets[at].wait()
     gets[at + 1].wait()
-    down(hid_ref, dv, outs, block)
-    put.wait()
-
-
-def down(hid_ref, down_ref, outs, block):
-    rows, part = outs[0].shape
-    for r in range(0, rows * len(outs), block):
-        for c in range(0, part, 256):
-            cols = slice(c, c + 256)
-            p0 = mm(hid_ref[0, r : r + block, :], down_ref[0, :, cols]).astype(BF16).astype(F32)
-            p1 = mm(hid_ref[1, r : r + block, :], down_ref[1, :, cols]).astype(BF16).astype(F32)
+    for r in range(0, many, block):
+        for c in range(0, part * parts, 256):
+            p0 = mm(hid_ref[0, r : r + block, :], dv[0, :, c : c + 256]).astype(BF16).astype(F32)
+            p1 = mm(hid_ref[1, r : r + block, :], dv[1, :, c : c + 256]).astype(BF16).astype(F32)
             p = (p0 + p1).astype(BF16)
             for q in range(r // rows, (r + block) // rows):
-                outs[q][:, cols] = p[q * rows - r : (q + 1) * rows - r, :]
-
-
-def down_kernel(hid_ref, d0, d1, *refs, count, first):
-    outs, (dv, sems) = refs[:count], refs[count:]
-    part = outs[0].shape[1]
-    gets = [copy(d.at[:, pl.ds(first, part)], dv.at[n], sems, n) for n, d in enumerate((d0, d1))]
-    for c in gets:
-        c.wait()
-    down(hid_ref, dv, outs, min(256, hid_ref.shape[1]))
+                out_ref = outs[c // part * count + q]
+                out_ref[:, c % part : c % part + 256] = p[q * rows - r : (q + 1) * rows - r, :]
 
 
 def final_kernel(start_ref, from_ref, base_hbm, near_ref, *refs, parts, planes):
@@ -442,56 +456,66 @@
         name="states",
     )(bit, key_rows, value_rows, log_decay)
     recv = partner(send)
-    recv, gate_own, up_own, down_own = lax.optimization_barrier((recv, gate_weight, up_weight, down_weight))
-    gate_other, up_other, down_other = partner(gate_own), partner(up_own), partner(down_own)
-    packed = pl.pallas_call(
-        functools.partial(pair_kernel, half=half, rows=rows),
-        grid=(1,),
-        out_shape=sds((pairs, rows + TAIL16, hd), BF16),
-        in_specs=[SMEM, full(own), full(recv)],
-        out_specs=full(sds((pairs, rows + TAIL16, hd), BF16)),
-        compiler_params=params(8),
-        name="pair",
-    )(bit, own, recv)
-    gathered = across_pairs(packed)
-    col = pl.BlockSpec((tok, width // 2), lambda i: (0, i))
-    wcol = pl.BlockSpec((resp, width // 2), lambda i: (0, i))
     start = jnp.minimum(jnp.argmax(response_mask), tok - resp).astype(jnp.int32).reshape(1)
     plane = lax.shift_right_logical(me, (2 * count).bit_length() - 1).reshape(1).astype(jnp.int32)
     at = (lax.shift_right_logical(me, 1) & (count - 1)).reshape(1).astype(jnp.int32)
     routing = (expert_ids.T, route_weights.T, response_mask.reshape(1, tok))
-    table = sds((3 * count * CAP, resp), BF16)
-    tables = pl.pallas_call(
+    table = sds((2 * count * CAP, resp), BF16)
+    slot_rows = sds((slots, resp), BF16)
+    tail = -(-(DECAYS + 2 * noted(count, resp, hd)[1]) // 16) * 16
+    note = sds((planes, tail, hd), BF16)
+    disp, notes = pl.pallas_call(
         functools.partial(route_kernel, experts=experts),
         grid=(1,),
-        out_shape=[table] * planes,
-        in_specs=[SMEM, SMEM] + [full(a) for a in routing],
-        out_specs=[full(table)] * planes,
-        scratch_shapes=[pltpu.VMEM((planes,) + table.shape, BF16)],
+        out_shape=[slot_rows, note],
+        in_specs=[full(a) for a in routing],
+        out_specs=[full(slot_rows), full(note)],
         compiler_params=params(),
         cost_estimate=cost(8 * tok * tok * slots, 1 << 20),
         name="route",
-    )(start, plane, *routing)
-    tables = [tables[0]] + [apart(tables[m], 2 * count * m) for m in range(1, planes)]
-    inside, lifted, inside_r, lifted_r, stream_r = pl.pallas_call(
+    )(*routing)
+    recv, gate_own, up_own, down_own, disp, notes = lax.optimization_barrier(
+        (recv, gate_weight, up_weight, down_weight, disp, notes)
+    )
+    gate_other, up_other, down_other = partner(gate_own), partner(up_own), partner(down_own)
+    payload = sds((pairs, rows + tail, hd), BF16)
+    packed, earlier = pl.pallas_call(
+        functools.partial(pair_kernel, half=half, rows=rows),
+        grid=(1,),
+        out_shape=[payload, sds(own.shape, F32)],
+        in_specs=[SMEM, full(own), full(recv), full(note)],
+        out_specs=[full(payload), full(own)],
+        compiler_params=params(63.4),
+        name="pair",
+    )(bit, own, recv, notes)
+    gathered = across_pairs(packed)
+    col = pl.BlockSpec((tok, width // 2), lambda i: (0, i))
+    wcol = pl.BlockSpec((3 * resp, width // 2), lambda i: (0, i))
+    inside, lifted, nearby = pl.pallas_call(
         inside_kernel,
         grid=(2,),
         out_shape=[
             sds((tok, width), F32),
             sds((tok, width), BF16),
-            sds((resp, width), F32),
-            sds((resp, width), BF16),
-            sds((resp, width), BF16),
+            sds((3 * resp, width), F32),
         ],
         in_specs=[SMEM, pl.BlockSpec((half, tok), lambda i: (i, 0)), col, col, col, col],
-        out_specs=[col, col, wcol, wcol, wcol],
+        out_specs=[col, col, wcol],
         compiler_params=params(),
         cost_estimate=cost(4 * tok * tok * width, 6 << 20),
         name="inside",
     )(start, log_decay, query_rows, key_rows, value_rows, stream_in)
-    gathered, inside, lifted, inside_r, lifted_r, stream_r = lax.optimization_barrier(
-        (gathered, inside, lifted, inside_r, lifted_r, stream_r)
-    )
+    gathered, inside, lifted, nearby = lax.optimization_barrier((gathered, inside, lifted, nearby))
+    tables = pl.pallas_call(
+        functools.partial(plan_kernel, planes=planes, rows=rows),
+        grid=(1,),
+        out_shape=[table] * planes,
+        in_specs=[SMEM, SMEM, full(gathered)],
+        out_specs=[full(table)] * planes,
+        compiler_params=params(),
+        cost_estimate=cost(1 << 24, 1 << 20),
+        name="plan",
+    )(at, plane, gathered)
     scanned = pl.pallas_call(
         scan_kernel,
         grid=(1,),
@@ -502,47 +526,31 @@
         name="scan",
     )(gathered)
     pref = across_pairs(scanned).reshape(half * hd, hd)
-    pref, *tables = lax.optimization_barrier((pref, *tables))
+    pref, gate_other, up_other, down_other = lax.optimization_barrier((pref, gate_other, up_other, down_other))
     keep, give = pl.pallas_call(
         functools.partial(split_kernel, half=half),
         grid=(1,),
         out_shape=[sds((half * hd, hd), BF16)] * 2,
-        in_specs=[SMEM, full(pref), HBM, HBM],
+        in_specs=[SMEM, full(pref), full(earlier)],
         out_specs=[full(pref)] * 2,
-        scratch_shapes=[pltpu.VMEM((span + TAIL, hd), F32), DMA],
         compiler_params=params(8),
         name="split",
-    )(bit, pref, own, recv)
+    )(bit, pref, earlier)
     other = partner(give)
 
     again = attn_gain.reshape(1, width)
-    window = (lifted_r, inside_r, stream_r, keep, other, again, ffn_gain.reshape(1, width))
-    row_part = sds((resp, part), BF16)
-    ready = pl.pallas_call(
+    window = (nearby, keep, other, again, ffn_gain.reshape(1, width), disp)
+    sent = pl.pallas_call(
         rows_kernel,
         grid=(1,),
-        out_shape=[row_part] * PARTS,
+        out_shape=sds((slots, width), BF16),
         in_specs=[SMEM] + [full(a) for a in window],
-        out_specs=[full(row_part)] * PARTS,
+        out_specs=full(sds((slots, width), BF16)),
         scratch_shapes=[pltpu.VMEM((resp, width), F32)],
         compiler_params=params(8),
         name="rows",
     )(bit, *window)
-    lines = [[ready[c]] + [apart(ready[c], 2 * count * m) for m in range(1, planes)] for c in range(PARTS)]
-    chunk = sds((planes * CAP, part), BF16)
-    arrived = []
-    for c in range(PARTS):
-        operands = (*tables, *lines[c])
-        chunks = pl.pallas_call(
-            functools.partial(gather_kernel, planes=planes, count=count),
-            grid=(1,),
-            out_shape=[chunk] * count,
-            in_specs=[SMEM] + [full(a) for a in operands],
-            out_specs=[full(chunk)] * count,
-            compiler_params=params(8),
-            name="gather",
-        )(at, *operands)
-        arrived += [chunks[0]] + [apart(chunks[m], 2 * m) for m in range(1, count)]
+    arrived = across_pairs(sent.reshape(pairs, CAP, width))
 
     gain_col = pl.BlockSpec((1, width // 2), lambda i: (0, i))
     state_all = pl.BlockSpec((half * hd, hd), lambda i: (0, 0))
@@ -556,45 +564,37 @@
         in_specs=[SMEM, SMEM, col, col, col, state_all, state_all, gain_col],
         out_specs=[col, near_col],
         scratch_shapes=[pltpu.VMEM((tok, width // 2), F32)],
-        compiler_params=params(32),
+        compiler_params=params(60),
         cost_estimate=cost(2 * tok * width * hd, 7 << 20),
         name="mixed",
     )(bit, first, lifted, inside, stream_in, keep, other, again)
-    base, around, *arrived = lax.optimization_barrier((base, around, *arrived))
-
+    arrived, base, around, *tables = lax.optimization_barrier((arrived, base, around, *tables))
+
+    row_part = sds((resp, part), BF16)
+    chunk = sds((planes * CAP, part), BF16)
     units = gate_weight.shape[1]
     step = min(256, units)
     many = count * chunk.shape[0]
-    hidden = sds((2, many, units), BF16)
-    *results, hid = pl.pallas_call(
+    results = pl.pallas_call(
         functools.partial(expert_kernel, count=count, parts=PARTS, step=step),
         grid=(1,),
-        out_shape=[chunk] * count + [hidden],
-        in_specs=[HBM] * (count * PARTS + 6),
-        out_specs=[full(chunk)] * count + [HBM],
+        out_shape=[chunk] * (count * PARTS),
+        in_specs=[SMEM, SMEM] + [HBM] * 7,
+        out_specs=[full(chunk)] * (count * PARTS),
         scratch_shapes=[pltpu.VMEM((2, width, units), BF16)] * 2
-        + [pltpu.VMEM((2, units, part), BF16), pltpu.VMEM(hidden.shape, BF16), pltpu.VMEM((many, width), BF16)]
-        + [DMA((count * PARTS + 4 * (units // step) + 3,))],
+        + [pltpu.VMEM((2, units, width), BF16), pltpu.VMEM((2, many, units), BF16), pltpu.VMEM((many, width), BF16)]
+        + [DMA((pairs + 4 * (units // step) + 2,))],
         compiler_params=params(48),
-        cost_estimate=cost(10 * many * width * units, 12 << 20),
+        cost_estimate=cost(12 * many * width * units, 14 << 20),
         name="expert",
-    )(*arrived, gate_own, up_own, down_own, gate_other, up_other, down_other)
+    )(at, plane, arrived, gate_own, up_own, down_own, gate_other, up_other, down_other)
+    backs = []
+    for c in range(PARTS):
+        mine = results[c * count : (c + 1) * count]
+        backs.append([mine[0]] + [apart(mine[m], 2 * m) for m in range(1, count)])
     shares = []
     for c in range(PARTS):
-        if c:
-            results = pl.pallas_call(
-                functools.partial(down_kernel, count=count, first=c * part),
-                grid=(1,),
-                out_shape=[chunk] * count,
-                in_specs=[full(hid), HBM, HBM],
-                out_specs=[full(chunk)] * count,
-                scratch_shapes=[pltpu.VMEM((2, units, part), BF16), DMA((2,))],
-                compiler_params=params(48),
-                cost_estimate=cost(2 * many * width * units, 2 << 20),
-                name="down",
-            )(hid, down_own, down_other)
-        back = [results[0]] + [apart(results[m], 2 * m) for m in range(1, count)]
-        operands = (*tables, *back)
+        operands = (*tables, *backs[c])
         kinds = [sds((resp, part), F32)] + [row_part] * (planes - 1)
         sums = pl.pallas_call(
             functools.partial(combine_kernel, planes=planes, count=count),

time: 136 us -> 110 us (0.81)
  starting transfers between devices: 56.5 us -> 31.7 us
  local copies, waits for them, and re-layouts: 22.6 us -> 0.17 us
  blocking collectives: 0 us -> 12.9 us
  Pallas kernels: 28.5 us -> 33.4 us
  waiting for transfers between devices: 25.2 us -> 29.6 us
    ppermute x27 -> x12, starting transfers between devices: 43.4 us -> 18.5 us  [apart(): lax.ppermute(x, BOTH, [(i, i ^ distance) for i in range(lax.axis_size(BOT...]
    unnamed x68 -> x30, local copies, waits for them, and re-layouts: 22.6 us -> 0.17 us
    all_to_all x2, waiting for transfers between devices: 3.85 us -> 21.2 us  [across_pairs(): return lax.all_to_all(x, BOTH, 0, 0, tiled=True, axis_index_groups=groups)]
    all_to_all x0 -> x1, blocking collectives: none -> 12.9 us  [across_pairs(): return lax.all_to_all(x, BOTH, 0, 0, tiled=True, axis_index_groups=groups)]
    ppermute x27 -> x12, waiting for transfers between devices: 18.1 us -> 6.88 us  [apart(): lax.ppermute(x, BOTH, [(i, i ^ distance) for i in range(lax.axis_size(BOT...]
    pallas_call x1, Pallas kernels: 5.51 us -> 7.63 us  [shards(): pl.pallas_call(functools.partial(expert_kernel, count=count, parts=PARTS,...]
    pallas_call x1, Pallas kernels: 2.23 us -> 4.02 us  [shards(): pl.pallas_call(mixed_kernel, grid=(2,), out_shape=[sds((tok, width), BF16...]
    ppermute x5, waiting for transfers between devices: 3.28 us -> 1.53 us  [partner(): return lax.ppermute(x, 'grp', [(i, i ^ 1) for i in range(count)])]
  transfers between devices with their start and end apart: 34 -> 19, of which waited for: 13 -> 9; matrix products, arithmetic and copies ran while one was open for 1% -> 1% of each run, Pallas kernels for 13% -> 17%
where the time goes in v4:
time: 110 us
  Pallas kernels  33.4 us (30%)
  starting transfers between devices  31.7 us (29%)
  waiting for transfers between devices  29.6 us (27%)
  blocking collectives  12.9 us (12%)
    all_to_all x2, waiting for transfers between devices, across_pairs(): return lax.all_to_all(x, BOTH, 0, 0, tiled=True, axis_index_groups=groups)  21.2 us
    ppermute x12, starting transfers between devices, apart(): lax.ppermute(x, BOTH, [(i, i ^ distance) for i in range(lax.axis_size(BOT...  18.5 us
    all_to_all x1, blocking collectives, across_pairs(): return lax.all_to_all(x, BOTH, 0, 0, tiled=True, axis_index_groups=groups)  12.9 us
    all_to_all x2, starting transfers between devices, across_pairs(): return lax.all_to_all(x, BOTH, 0, 0, tiled=True, axis_index_groups=groups)  11.9 us
    pallas_call x1, Pallas kernels, shards(): pl.pallas_call(functools.partial(expert_kernel, count=count, parts=PARTS,...  7.63 us
    ppermute x12, waiting for transfers between devices, apart(): lax.ppermute(x, BOTH, [(i, i ^ distance) for i in range(lax.axis_size(BOT...  6.88 us
    pallas_call x1, Pallas kernels, shards(): pl.pallas_call(inside_kernel, grid=(2,), out_shape=[sds((tok, width), F32...  6.73 us
    pallas_call x1, Pallas kernels, shards(): pl.pallas_call(states_kernel, out_shape=[sds((span + TAIL, hd), F32)] * 2...  4.12 us
  transfers between devices with their start and end apart: 19, of which 9 were waited for; matrix products, arithmetic and copies ran while one was open for 1% of the time, Pallas kernels for 17%

profile of v4, /device:TPU:0, one launch (start us, length us, event | category | flops | bytes accessed | tf_op | source)
XLA Modules:
  0.0 109.5 jit_solution(9185687744608281007)
XLA Ops:
  0.0 4.1 %states.1 = (f32[1032,128]{1,0:T(8,128)}, f32[1032,128]{1,0:T(8,128)}) custom-call(s32[1]{0:T(128)} %bitcast.1.k_ref, bf16[256,2048]{1,0:T(8,128)(2,1)} %key_ref.1, bf16[256,2048]{1,0:T(8,128)(2,1)} %val_ref.1, f32[16,256]{1,0:T(8,128)} %dec_ref.1), custom_call_target="tpu_custom_call" | custom-call | flops 134217728 | bytes 3145728 | tf_op jit(solution)/shard_map/states/pallas_call | solution.py:445
  4.1 0.5 collective-permute-start
  4.6 1.9 %route.1 = (bf16[256,32]{1,0:T(8,128)(2,1)}, bf16[4,16,128]{2,1,0:T(8,128)(2,1)}) custom-call(s32[8,256]{1,0:T(8,128)} %bitcast.16, f32[8,256]{1,0:T(8,128)} %bitcast.17, s32[1,256]{1,0:T(1,128)} %bitcast.15), custom_call_target="tpu_custom_call" | custom-call | flops 134217728 | bytes 1048576 | tf_op jit(solution)/shard_map/route/pallas_call | solution.py:467
  6.6 0.0 collective-permute-done.recv_ref
  6.6 0.2 collective-permute-start.1
  6.8 0.3 collective-permute-start.2
  7.1 0.2 collective-permute-start.3
  7.3 0.1 copy-done.13
  7.4 2.4 %pair.1 = (bf16[16,80,128]{2,1,0:T(8,128)(2,1)}, f32[1032,128]{1,0:T(8,128)}) custom-call(s32[1]{0:T(128)} %bitcast.1.k_ref, f32[1032,128]{1,0:T(8,128)} %get-tuple-element.61.own_ref, f32[1032,128]{1,0:T(8,128)} %copy-done.13, bf16[4,16,128]{2,1,0:T(8,128)(2,1)} %get-tuple-element.66.notes_ref), custom_call_target="tpu_custom_call" | custom-call | tf_op jit(solution)/shard_map/pair/pallas_call | solution.py:482
  9.8 8.1 %all-to-all-start = ((bf16[16,80,128]{2,1,0:T(8,128)(2,1)}), bf16[16,80,128]{2,1,0:T(8,128)(2,1)S(1)}, u32[]{:S(2)}, u32[]{:S(2)}) async-start(bf16[16,80,128]{2,1,0:T(8,128)(2,1)} %get-tuple-element.67), calls=%async_computation | async-start | bytes 655360 | tf_op jit(solution)/shard_map/all_to_all | solution.py:73
  17.9 0.0 copy-done.14
  17.9 0.7 iota_reduce_fusion
  19.2 0.0 copy-start.4
  19.2 0.0 copy-start.10
  19.2 0.0 copy-start.11
  19.2 0.0 copy-start.12
  19.2 6.7 %inside.1 = (f32[256,2048]{1,0:T(8,128)}, bf16[256,2048]{1,0:T(8,128)(2,1)}, f32[96,2048]{1,0:T(8,128)}) custom-call(s32[1]{0:T(128)} %bitcast.start_ref, f32[16,256]{1,0:T(8,128)} %dec_ref.1, bf16[256,2048]{1,0:T(8,128)(2,1)} %q_ref.1, bf16[256,2048]{1,0:T(8,128)(2,1)} %key_ref.1, bf16[256,2048]{1,0:T(8,128)(2,1)} %val_ref.1, bf16[256,2048]{1,0:T(8,128)(2,1)} %stream_ref.3), custom_call_target="tpu_custom_call" | custom-call | flops 536870912 | bytes 6291456 | tf_op jit(solution)/shard_map/inside/pallas_call | solution.py:494
  26.0 3.7 %all-to-all-done.in_ref = bf16[16,80,128]{2,1,0:T(8,128)(2,1)S(1)} async-done(((bf16[16,80,128]{2,1,0:T(8,128)(2,1)}), bf16[16,80,128]{2,1,0:T(8,128)(2,1)S(1)}, u32[]{:S(2)}, u32[]{:S(2)}) %all-to-all-start) | async-done | bytes 327712 | tf_op jit(solution)/shard_map/all_to_all | solution.py:73
  29.6 0.1 scan.1
  29.7 12.9 %all_to_all.15 = bf16[16,64,128]{2,1,0:T(8,128)(2,1)S(1)} all-to-all(bf16[16,64,128]{2,1,0:T(8,128)(2,1)S(1)} %scan.1), channel_id=1, replica_groups={{0,2,4,6,8,10,12,14,16,18,20,22,24,26,28,30},{1,3,5,7,9,11,13,15,17,19,..., dimensions={0} | all-to-all | bytes 524288 | tf_op jit(solution)/shard_map/all_to_all | solution.py:73
  42.7 0.0 collective-permute-done.1.g1
  42.7 0.0 collective-permute-done.2.u1
  42.7 0.0 collective-permute-done.3.d1
  42.7 0.0 copy-done.4
  42.7 0.2 split.1
  42.9 0.1 collective-permute-start.4
  43.0 1.5 %collective-permute-done.4.other_ref = bf16[1024,128]{1,0:T(8,128)(2,1)S(1)} collective-permute-done((bf16[1024,128]{1,0:T(8,128)(2,1)S(1)}, bf16[1024,128]{1,0:T(8,128)(2,1)S(1)}, u32[]{:S(2)}, u32[]{:S(2)}) %collective-permute-start.4) | collective-permute-done | bytes 262176 | tf_op jit(solution)/shard_map/ppermute | solution.py:63
  44.5 0.0 copy-done.10
  44.5 0.0 copy-done.12
  44.5 1.9 %rows.1 = bf16[256,2048]{1,0:T(8,128)(2,1)} custom-call(s32[1]{0:T(128)} %bitcast.1.k_ref, f32[96,2048]{1,0:T(8,128)S(1)} %copy-done.3, bf16[1024,128]{1,0:T(8,128)(2,1)S(1)} %get-tuple-element.78.keep_ref, bf16[1024,128]{1,0:T(8,128)(2,1)S(1)} %collective-permute-done.4.other_ref, f32[1,2048]{1,0:T(1,128)S(1)} %bitcast.13, f32[1,2048]{1,0:T(1,128)S(1)} %bitcast.14, ...), custom_call_target="tpu_custom_call" | custom-call | tf_op jit(solution)/shard_map/rows/pallas_call | solution.py:543
  46.4 0.0 copy-done
  46.4 0.0 copy-done.2
  46.4 3.8 %all-to-all-start.2 = ((bf16[16,16,2048]{2,1,0:T(8,128)(2,1)}), bf16[16,16,2048]{2,1,0:T(8,128)(2,1)S(1)}, u32[]{:S(2)}, u32[]{:S(2)}) async-start(bf16[16,16,2048]{2,1,0:T(8,128)(2,1)} %bitcast.8), calls=%async_computation.2 | async-start | bytes 2097152 | tf_op jit(solution)/shard_map/all_to_all | solution.py:73
  50.3 2.8 %plan.1 = (bf16[128,32]{1,0:T(8,128)(2,1)}, bf16[128,32]{1,0:T(8,128)(2,1)}, bf16[128,32]{1,0:T(8,128)(2,1)}, bf16[128,32]{1,0:T(8,128)(2,1)}) custom-call(s32[1]{0:T(128)} %bitcast.9.at_ref, s32[1]{0:T(128)} %bitcast.10.plane_ref, bf16[16,80,128]{2,1,0:T(8,128)(2,1)} %copy-done), custom_call_target="tpu_custom_call" | custom-call | flops 16777216 | bytes 1048576 | tf_op jit(solution)/shard_map/plan/pallas_call | solution.py:509
  53.1 4.0 %mixed.1 = (bf16[256,2048]{1,0:T(8,128)(2,1)}, f32[48,2048]{1,0:T(8,128)}) custom-call(s32[1]{0:T(128)} %bitcast.1.k_ref, s32[1]{0:T(128)S(6)} %min.7.from_ref, bf16[256,2048]{1,0:T(8,128)(2,1)} %get-tuple-element.81.lifted_ref, f32[256,2048]{1,0:T(8,128)} %get-tuple-element.82.inside_ref, bf16[256,2048]{1,0:T(8,128)(2,1)} %stream_ref.3, ...), custom_call_target="tpu_custom_call" | custom-call | flops 134217728 | bytes 7340032 | tf_op jit(solution)/shard_map/mixed/pallas_call | solution.py:560
  57.1 17.5 %all-to-all-done.2.x_hbm = bf16[16,16,2048]{2,1,0:T(8,128)(2,1)S(1)} async-done(((bf16[16,16,2048]{2,1,0:T(8,128)(2,1)}), bf16[16,16,2048]{2,1,0:T(8,128)(2,1)S(1)}, u32[]{:S(2)}, u32[]{:S(2)}) %all-to-all-start.2) | async-done | bytes 1048608 | tf_op jit(solution)/shard_map/all_to_all | solution.py:73
  74.7 7.6 %expert.1 = (bf16[64,1024]{1,0:T(8,128)(2,1)S(1)}, bf16[64,1024]{1,0:T(8,128)(2,1)S(1)}, bf16[64,1024]{1,0:T(8,128)(2,1)S(1)}, bf16[64,1024]{1,0:T(8,128)(2,1)S(...) custom-call(s32[1]{0:T(128)} %bitcast.9.at_ref, ...), custom_call_target="tpu_custom_call" | custom-call | flops 3221225472 | bytes 14680064 | tf_op jit(solution)/shard_map/expert/pallas_call | solution.py:578
  82.3 0.6 collective-permute-start.5
  82.9 2.0 %collective-permute-start.6 = (bf16[64,1024]{1,0:T(8,128)(2,1)S(1)}, bf16[64,1024]{1,0:T(8,128)(2,1)S(1)}, u32[]{:S(2)}, u32[]{:S(2)}) collective-permute-start(bf16[64,1024]{1,0:T(8,128)(2,1)S(1)} %get-tuple-element.101), channel_id=1, source_target_pairs={{0,4},{1,5},{2,6},{3,7},{4,0},{5,1},{6,2},{7,3},{8,12},{9,13},{10,... | collective-permute-start | bytes 393224 | tf_op jit(solution)/shard_map/ppermute | solution.py:67
  84.9 1.0 collective-permute-start.7
  85.9 0.6 collective-permute-start.11
  86.4 2.0 %collective-permute-start.12 = (bf16[64,1024]{1,0:T(8,128)(2,1)S(1)}, bf16[64,1024]{1,0:T(8,128)(2,1)S(1)}, u32[]{:S(2)}, u32[]{:S(2)}) collective-permute-start(bf16[64,1024]{1,0:T(8,128)(2,1)S(1)} %get-tuple-element.109), channel_id=1, source_target_pairs={{0,4},{1,5},{2,6},{3,7},{4,0},{5,1},{6,2},{7,3},{8,12},{9,13},{10,... | collective-permute-start | bytes 393224 | tf_op jit(solution)/shard_map/ppermute | solution.py:67
  88.4 1.6 %collective-permute-done.5.refs_5_ = bf16[64,1024]{1,0:T(8,128)(2,1)S(1)} collective-permute-done((bf16[64,1024]{1,0:T(8,128)(2,1)S(1)}, bf16[64,1024]{1,0:T(8,128)(2,1)S(1)}, u32[]{:S(2)}, u32[]{:S(2)}) %collective-permute-start.5) | collective-permute-done | bytes 131104 | tf_op jit(solution)/shard_map/ppermute | solution.py:67
  90.0 2.2 %collective-permute-start.13 = (bf16[64,1024]{1,0:T(8,128)(2,1)S(1)}, bf16[64,1024]{1,0:T(8,128)(2,1)S(1)}, u32[]{:S(2)}, u32[]{:S(2)}) collective-permute-start(bf16[64,1024]{1,0:T(8,128)(2,1)S(1)} %get-tuple-element.110), channel_id=1, source_target_pairs={{0,6},{1,7},{2,4},{3,5},{4,2},{5,3},{6,0},{7,1},{8,14},{9,15},{10,... | collective-permute-start | bytes 393224 | tf_op jit(solution)/shard_map/ppermute | solution.py:67
  92.2 0.0 collective-permute-done.6.refs_6_
  92.2 0.9 collective-permute-done.7.refs_7_
  93.2 0.3 combine.2
  93.5 3.3 %collective-permute-start.8 = (bf16[32,1024]{1,0:T(8,128)(2,1)S(1)}, bf16[32,1024]{1,0:T(8,128)(2,1)S(1)}, u32[]{:S(2)}, u32[]{:S(2)}) collective-permute-start(bf16[32,1024]{1,0:T(8,128)(2,1)S(1)} %get-tuple-element.104), channel_id=1, source_target_pairs={{0,8},{1,9},{2,10},{3,11},{4,12},{5,13},{6,14},{7,15},{8,0},{9,1},... | collective-permute-start | bytes 196616 | tf_op jit(solution)/shard_map/ppermute | solution.py:67
  96.9 0.6 collective-permute-start.9
  97.4 0.0 collective-permute-done.11.refs_5_
  97.4 1.9 %collective-permute-start.10 = (bf16[32,1024]{1,0:T(8,128)(2,1)S(1)}, bf16[32,1024]{1,0:T(8,128)(2,1)S(1)}, u32[]{:S(2)}, u32[]{:S(2)}) collective-permute-start(bf16[32,1024]{1,0:T(8,128)(2,1)S(1)} %get-tuple-element.106), channel_id=1, source_target_pairs={{0,24},{1,25},{2,26},{3,27},{4,28},{5,29},{6,30},{7,31},{8,16},{9,... | collective-permute-start | bytes 196616 | tf_op jit(solution)/shard_map/ppermute | solution.py:67
  99.3 0.0 collective-permute-done.12.refs_6_
  99.3 0.0 collective-permute-done.13.refs_7_
  99.3 0.3 combine.3
  99.7 1.1 %collective-permute-start.14 = (bf16[32,1024]{1,0:T(8,128)(2,1)S(1)}, bf16[32,1024]{1,0:T(8,128)(2,1)S(1)}, u32[]{:S(2)}, u32[]{:S(2)}) collective-permute-start(bf16[32,1024]{1,0:T(8,128)(2,1)S(1)} %get-tuple-element.112), channel_id=1, source_target_pairs={{0,8},{1,9},{2,10},{3,11},{4,12},{5,13},{6,14},{7,15},{8,0},{9,1},... | collective-permute-start | bytes 196616 | tf_op jit(solution)/shard_map/ppermute | solution.py:67
  100.8 1.5 %collective-permute-start.15 = (bf16[32,1024]{1,0:T(8,128)(2,1)S(1)}, bf16[32,1024]{1,0:T(8,128)(2,1)S(1)}, u32[]{:S(2)}, u32[]{:S(2)}) collective-permute-start(bf16[32,1024]{1,0:T(8,128)(2,1)S(1)} %get-tuple-element.113), channel_id=1, source_target_pairs={{0,16},{1,17},{2,18},{3,19},{4,20},{5,21},{6,22},{7,23},{8,24},{9,... | collective-permute-start | bytes 196616 | tf_op jit(solution)/shard_map/ppermute | solution.py:67
  102.2 0.0 collective-permute-done.8.refs_1_
  102.2 1.9 %collective-permute-start.16 = (bf16[32,1024]{1,0:T(8,128)(2,1)S(1)}, bf16[32,1024]{1,0:T(8,128)(2,1)S(1)}, u32[]{:S(2)}, u32[]{:S(2)}) collective-permute-start(bf16[32,1024]{1,0:T(8,128)(2,1)S(1)} %get-tuple-element.114), channel_id=1, source_target_pairs={{0,24},{1,25},{2,26},{3,27},{4,28},{5,29},{6,30},{7,31},{8,16},{9,... | collective-permute-start | bytes 196616 | tf_op jit(solution)/shard_map/ppermute | solution.py:67
  104.1 1.1 collective-permute-done.9.refs_2_
  105.2 0.0 collective-permute-done.10.refs_3_
  105.2 0.3 collective-permute-done.14.refs_5_
  105.4 1.8 %collective-permute-done.15.refs_6_ = bf16[32,1024]{1,0:T(8,128)(2,1)S(1)} collective-permute-done((bf16[32,1024]{1,0:T(8,128)(2,1)S(1)}, bf16[32,1024]{1,0:T(8,128)(2,1)S(1)}, u32[]{:S(2)}, u32[]{:S(2)}) %collective-permute-start.15) | collective-permute-done | bytes 65568 | tf_op jit(solution)/shard_map/ppermute | solution.py:67
  107.3 1.2 %collective-permute-done.16.refs_7_ = bf16[32,1024]{1,0:T(8,128)(2,1)S(1)} collective-permute-done((bf16[32,1024]{1,0:T(8,128)(2,1)S(1)}, bf16[32,1024]{1,0:T(8,128)(2,1)S(1)}, u32[]{:S(2)}, u32[]{:S(2)}) %collective-permute-start.16) | collective-permute-done | bytes 65568 | tf_op jit(solution)/shard_map/ppermute | solution.py:67
  108.4 1.0 final.1
  (19 shorter events, 0.0 us)
Async XLA Ops:
  0.0 17.9 %copy-start.14 = (s32[256]{0:T(256)S(1)}, s32[256]{0:T(256)}, u32[]{:S(2)}) copy-start(s32[256]{0:T(256)} %param.22) | copy-start | bytes 3076
  4.1 2.5 %collective-permute-start = (f32[1032,128]{1,0:T(8,128)}, f32[1032,128]{1,0:T(8,128)S(1)}, u32[]{:S(2)}, u32[]{:S(2)}) collective-permute-start(f32[1032,128]{1,0:T(8,128)} %get-tuple-element.62), channel_id=1, source_target_pairs={{0,1},{1,0},{2,3},{3,2},{4,5},{5,4},{6,7},{7,6},{8,9},{9,8},{10,11... | collective-permute-start | bytes 1585160 | tf_op jit(solution)/shard_map/ppermute | solution.py:63
  6.6 0.8 copy-start.13
  6.6 36.1 %collective-permute-start.1 = (bf16[2048,512]{1,0:T(8,128)(2,1)}, bf16[2048,512]{1,0:T(8,128)(2,1)}, u32[]{:S(2)}, u32[]{:S(2)}) collective-permute-start(bf16[2048,512]{1,0:T(8,128)(2,1)} %g0), channel_id=1, source_target_pairs={{0,1},{1,0},{2,3},{3,2},{4,5},{5,4},{6,7},{7,6},{8,9},{9,8},{10,11... | collective-permute-start | bytes 6291464 | tf_op jit(solution)/shard_map/ppermute | solution.py:63
  6.8 35.9 %collective-permute-start.2 = (bf16[2048,512]{1,0:T(8,128)(2,1)}, bf16[2048,512]{1,0:T(8,128)(2,1)}, u32[]{:S(2)}, u32[]{:S(2)}) collective-permute-start(bf16[2048,512]{1,0:T(8,128)(2,1)} %u0), channel_id=1, source_target_pairs={{0,1},{1,0},{2,3},{3,2},{4,5},{5,4},{6,7},{7,6},{8,9},{9,8},{10,11... | collective-permute-start | bytes 6291464 | tf_op jit(solution)/shard_map/ppermute | solution.py:63
  7.1 35.6 %collective-permute-start.3 = (bf16[512,2048]{1,0:T(8,128)(2,1)}, bf16[512,2048]{1,0:T(8,128)(2,1)}, u32[]{:S(2)}, u32[]{:S(2)}) collective-permute-start(bf16[512,2048]{1,0:T(8,128)(2,1)} %d0), channel_id=1, source_target_pairs={{0,1},{1,0},{2,3},{3,2},{4,5},{5,4},{6,7},{7,6},{8,9},{9,8},{10,11... | collective-permute-start | bytes 6291464 | tf_op jit(solution)/shard_map/ppermute | solution.py:63
  9.8 19.9 %all-to-all-start = ((bf16[16,80,128]{2,1,0:T(8,128)(2,1)}), bf16[16,80,128]{2,1,0:T(8,128)(2,1)S(1)}, u32[]{:S(2)}, u32[]{:S(2)}) async-start(bf16[16,80,128]{2,1,0:T(8,128)(2,1)} %get-tuple-element.67), calls=%async_computation | async-start | bytes 655360 | tf_op jit(solution)/shard_map/all_to_all | solution.py:73
  19.2 23.5 %copy-start.4 = (f32[1032,128]{1,0:T(8,128)S(1)}, f32[1032,128]{1,0:T(8,128)}, u32[]{:S(2)}) copy-start(f32[1032,128]{1,0:T(8,128)} %get-tuple-element.77.first_ref) | copy-start | bytes 1585156
  19.2 25.3 %copy-start.10 = (bf16[256,32]{1,0:T(8,128)(2,1)S(1)}, bf16[256,32]{1,0:T(8,128)(2,1)}, u32[]{:S(2)}) copy-start(bf16[256,32]{1,0:T(8,128)(2,1)} %get-tuple-element.80.disp_ref) | copy-start | bytes 49156
  19.2 25.3 %copy-start.11 = (f32[2048]{0:T(1024)S(1)}, f32[2048]{0:T(1024)}, u32[]{:S(2)}) copy-start(f32[2048]{0:T(1024)} %param.18) | copy-start | bytes 24580
  19.2 25.3 %copy-start.12 = (f32[2048]{0:T(1024)S(1)}, f32[2048]{0:T(1024)}, u32[]{:S(2)}) copy-start(f32[2048]{0:T(1024)} %param.19) | copy-start | bytes 24580
  26.0 18.6 %copy-start.3 = (f32[96,2048]{1,0:T(8,128)S(1)}, f32[96,2048]{1,0:T(8,128)}, u32[]{:S(2)}) copy-start(f32[96,2048]{1,0:T(8,128)} %get-tuple-element.71.near_ref) | copy-start | bytes 2359300
  29.6 16.8 %copy-start = (bf16[16,80,128]{2,1,0:T(8,128)(2,1)}, bf16[16,80,128]{2,1,0:T(8,128)(2,1)S(1)}, u32[]{:S(2)}) copy-start(bf16[16,80,128]{2,1,0:T(8,128)(2,1)S(1)} %all-to-all-done.in_ref) | copy-start | bytes 983044
  42.9 3.5 %copy-start.1 = (bf16[1024,128]{1,0:T(8,128)(2,1)}, bf16[1024,128]{1,0:T(8,128)(2,1)S(1)}, u32[]{:S(2)}) copy-start(bf16[1024,128]{1,0:T(8,128)(2,1)S(1)} %get-tuple-element.78.keep_ref) | copy-start | bytes 786436
  42.9 1.6 %collective-permute-start.4 = (bf16[1024,128]{1,0:T(8,128)(2,1)S(1)}, bf16[1024,128]{1,0:T(8,128)(2,1)S(1)}, u32[]{:S(2)}, u32[]{:S(2)}) collective-permute-start(bf16[1024,128]{1,0:T(8,128)(2,1)S(1)} %get-tuple-element.79), channel_id=1, source_target_pairs={{0,1},{1,0},{2,3},{3,2},{4,5},{5,4},{6,7},{7,6},{8,9},{9,8},{10,11... | collective-permute-start | bytes 786440 | tf_op jit(solution)/shard_map/ppermute | solution.py:63
  44.5 1.9 %copy-start.2 = (bf16[1024,128]{1,0:T(8,128)(2,1)}, bf16[1024,128]{1,0:T(8,128)(2,1)S(1)}, u32[]{:S(2)}) copy-start(bf16[1024,128]{1,0:T(8,128)(2,1)S(1)} %collective-permute-done.4.other_ref) | copy-start | bytes 786436
  46.4 28.3 %all-to-all-start.2 = ((bf16[16,16,2048]{2,1,0:T(8,128)(2,1)}), bf16[16,16,2048]{2,1,0:T(8,128)(2,1)S(1)}, u32[]{:S(2)}, u32[]{:S(2)}) async-start(bf16[16,16,2048]{2,1,0:T(8,128)(2,1)} %bitcast.8), calls=%async_computation.2 | async-start | bytes 2097152 | tf_op jit(solution)/shard_map/all_to_all | solution.py:73
  74.7 18.5 %copy-start.6 = (bf16[128,32]{1,0:T(8,128)(2,1)S(1)}, bf16[128,32]{1,0:T(8,128)(2,1)}, u32[]{:S(2)}) copy-start(bf16[128,32]{1,0:T(8,128)(2,1)} %get-tuple-element.91.refs_0_) | copy-start | bytes 24580
  74.7 18.5 %copy-start.7 = (bf16[128,32]{1,0:T(8,128)(2,1)S(1)}, bf16[128,32]{1,0:T(8,128)(2,1)}, u32[]{:S(2)}) copy-start(bf16[128,32]{1,0:T(8,128)(2,1)} %get-tuple-element.92.refs_1_) | copy-start | bytes 24580
  74.7 18.5 %copy-start.8 = (bf16[128,32]{1,0:T(8,128)(2,1)S(1)}, bf16[128,32]{1,0:T(8,128)(2,1)}, u32[]{:S(2)}) copy-start(bf16[128,32]{1,0:T(8,128)(2,1)} %get-tuple-element.93.refs_2_) | copy-start | bytes 24580
  74.7 18.5 %copy-start.9 = (bf16[128,32]{1,0:T(8,128)(2,1)S(1)}, bf16[128,32]{1,0:T(8,128)(2,1)}, u32[]{:S(2)}) copy-start(bf16[128,32]{1,0:T(8,128)(2,1)} %get-tuple-element.94.refs_3_) | copy-start | bytes 24580
  74.7 33.7 %copy-start.5 = (f32[48,2048]{1,0:T(8,128)S(1)}, f32[48,2048]{1,0:T(8,128)}, u32[]{:S(2)}) copy-start(f32[48,2048]{1,0:T(8,128)} %get-tuple-element.90.near_ref) | copy-start | bytes 1179652
  82.3 7.7 %collective-permute-start.5 = (bf16[64,1024]{1,0:T(8,128)(2,1)S(1)}, bf16[64,1024]{1,0:T(8,128)(2,1)S(1)}, u32[]{:S(2)}, u32[]{:S(2)}) collective-permute-start(bf16[64,1024]{1,0:T(8,128)(2,1)S(1)} %get-tuple-element.100), channel_id=1, source_target_pairs={{0,2},{1,3},{2,0},{3,1},{4,6},{5,7},{6,4},{7,5},{8,10},{9,11},{10,... | collective-permute-start | bytes 393224 | tf_op jit(solution)/shard_map/ppermute | solution.py:67
  82.9 9.3 %collective-permute-start.6 = (bf16[64,1024]{1,0:T(8,128)(2,1)S(1)}, bf16[64,1024]{1,0:T(8,128)(2,1)S(1)}, u32[]{:S(2)}, u32[]{:S(2)}) collective-permute-start(bf16[64,1024]{1,0:T(8,128)(2,1)S(1)} %get-tuple-element.101), channel_id=1, source_target_pairs={{0,4},{1,5},{2,6},{3,7},{4,0},{5,1},{6,2},{7,3},{8,12},{9,13},{10,... | collective-permute-start | bytes 393224 | tf_op jit(solution)/shard_map/ppermute | solution.py:67
  84.9 8.3 %collective-permute-start.7 = (bf16[64,1024]{1,0:T(8,128)(2,1)S(1)}, bf16[64,1024]{1,0:T(8,128)(2,1)S(1)}, u32[]{:S(2)}, u32[]{:S(2)}) collective-permute-start(bf16[64,1024]{1,0:T(8,128)(2,1)S(1)} %get-tuple-element.102), channel_id=1, source_target_pairs={{0,6},{1,7},{2,4},{3,5},{4,2},{5,3},{6,0},{7,1},{8,14},{9,15},{10,... | collective-permute-start | bytes 393224 | tf_op jit(solution)/shard_map/ppermute | solution.py:67
  85.9 11.6 %collective-permute-start.11 = (bf16[64,1024]{1,0:T(8,128)(2,1)S(1)}, bf16[64,1024]{1,0:T(8,128)(2,1)S(1)}, u32[]{:S(2)}, u32[]{:S(2)}) collective-permute-start(bf16[64,1024]{1,0:T(8,128)(2,1)S(1)} %get-tuple-element.108), channel_id=1, source_target_pairs={{0,2},{1,3},{2,0},{3,1},{4,6},{5,7},{6,4},{7,5},{8,10},{9,11},{10,... | collective-permute-start | bytes 393224 | tf_op jit(solution)/shard_map/ppermute | solution.py:67
  86.4 12.9 %collective-permute-start.12 = (bf16[64,1024]{1,0:T(8,128)(2,1)S(1)}, bf16[64,1024]{1,0:T(8,128)(2,1)S(1)}, u32[]{:S(2)}, u32[]{:S(2)}) collective-permute-start(bf16[64,1024]{1,0:T(8,128)(2,1)S(1)} %get-tuple-element.109), channel_id=1, source_target_pairs={{0,4},{1,5},{2,6},{3,7},{4,0},{5,1},{6,2},{7,3},{8,12},{9,13},{10,... | collective-permute-start | bytes 393224 | tf_op jit(solution)/shard_map/ppermute | solution.py:67
  90.0 9.3 %collective-permute-start.13 = (bf16[64,1024]{1,0:T(8,128)(2,1)S(1)}, bf16[64,1024]{1,0:T(8,128)(2,1)S(1)}, u32[]{:S(2)}, u32[]{:S(2)}) collective-permute-start(bf16[64,1024]{1,0:T(8,128)(2,1)S(1)} %get-tuple-element.110), channel_id=1, source_target_pairs={{0,6},{1,7},{2,4},{3,5},{4,2},{5,3},{6,0},{7,1},{8,14},{9,15},{10,... | collective-permute-start | bytes 393224 | tf_op jit(solution)/shard_map/ppermute | solution.py:67
  93.5 8.7 %collective-permute-start.8 = (bf16[32,1024]{1,0:T(8,128)(2,1)S(1)}, bf16[32,1024]{1,0:T(8,128)(2,1)S(1)}, u32[]{:S(2)}, u32[]{:S(2)}) collective-permute-start(bf16[32,1024]{1,0:T(8,128)(2,1)S(1)} %get-tuple-element.104), channel_id=1, source_target_pairs={{0,8},{1,9},{2,10},{3,11},{4,12},{5,13},{6,14},{7,15},{8,0},{9,1},... | collective-permute-start | bytes 196616 | tf_op jit(solution)/shard_map/ppermute | solution.py:67
  96.9 8.3 %collective-permute-start.9 = (bf16[32,1024]{1,0:T(8,128)(2,1)S(1)}, bf16[32,1024]{1,0:T(8,128)(2,1)S(1)}, u32[]{:S(2)}, u32[]{:S(2)}) collective-permute-start(bf16[32,1024]{1,0:T(8,128)(2,1)S(1)} %get-tuple-element.105), channel_id=1, source_target_pairs={{0,16},{1,17},{2,18},{3,19},{4,20},{5,21},{6,22},{7,23},{8,24},{9,... | collective-permute-start | bytes 196616 | tf_op jit(solution)/shard_map/ppermute | solution.py:67
  97.4 7.7 %collective-permute-start.10 = (bf16[32,1024]{1,0:T(8,128)(2,1)S(1)}, bf16[32,1024]{1,0:T(8,128)(2,1)S(1)}, u32[]{:S(2)}, u32[]{:S(2)}) collective-permute-start(bf16[32,1024]{1,0:T(8,128)(2,1)S(1)} %get-tuple-element.106), channel_id=1, source_target_pairs={{0,24},{1,25},{2,26},{3,27},{4,28},{5,29},{6,30},{7,31},{8,16},{9,... | collective-permute-start | bytes 196616 | tf_op jit(solution)/shard_map/ppermute | solution.py:67
  99.7 5.8 %collective-permute-start.14 = (bf16[32,1024]{1,0:T(8,128)(2,1)S(1)}, bf16[32,1024]{1,0:T(8,128)(2,1)S(1)}, u32[]{:S(2)}, u32[]{:S(2)}) collective-permute-start(bf16[32,1024]{1,0:T(8,128)(2,1)S(1)} %get-tuple-element.112), channel_id=1, source_target_pairs={{0,8},{1,9},{2,10},{3,11},{4,12},{5,13},{6,14},{7,15},{8,0},{9,1},... | collective-permute-start | bytes 196616 | tf_op jit(solution)/shard_map/ppermute | solution.py:67
  100.8 6.5 %collective-permute-start.15 = (bf16[32,1024]{1,0:T(8,128)(2,1)S(1)}, bf16[32,1024]{1,0:T(8,128)(2,1)S(1)}, u32[]{:S(2)}, u32[]{:S(2)}) collective-permute-start(bf16[32,1024]{1,0:T(8,128)(2,1)S(1)} %get-tuple-element.113), channel_id=1, source_target_pairs={{0,16},{1,17},{2,18},{3,19},{4,20},{5,21},{6,22},{7,23},{8,24},{9,... | collective-permute-start | bytes 196616 | tf_op jit(solution)/shard_map/ppermute | solution.py:67
  102.2 6.2 %collective-permute-start.16 = (bf16[32,1024]{1,0:T(8,128)(2,1)S(1)}, bf16[32,1024]{1,0:T(8,128)(2,1)S(1)}, u32[]{:S(2)}, u32[]{:S(2)}) collective-permute-start(bf16[32,1024]{1,0:T(8,128)(2,1)S(1)} %get-tuple-element.114), channel_id=1, source_target_pairs={{0,24},{1,25},{2,26},{3,27},{4,28},{5,29},{6,30},{7,31},{8,16},{9,... | collective-permute-start | bytes 196616 | tf_op jit(solution)/shard_map/ppermute | solution.py:67

commit v5 on v4

--- a/solution.py
+++ b/solution.py
@@ -105,7 +105,7 @@
         for j in range(half):
             cols = slice(j * hd, (j + 1) * hd)
             scaled = (key_ref[n, :, cols].astype(F32) * fac[:, first + j : first + j + 1]).astype(BF16)
-            dst[cols, :] = mm(scaled, val_ref[n, :, cols], 0, 0)
+            dst[cols, :] = mm(val_ref[n, :, cols], scaled, 0, 0)
         dst[span:, :] = tail
         puts.append(copy(dst, out, sems, 5 + n))
     for c in puts:
@@ -165,7 +165,13 @@
         give_ref[sl, :] = jnp.where(even, after, before).astype(BF16)
 
 
-def inside_kernel(start_ref, dec_ref, q_ref, key_ref, val_ref, stream_ref, inside_ref, lifted_ref, near_ref):
+def window_start(live, resp):
+    tok = live.shape[1]
+    token = lax.broadcasted_iota(jnp.int32, (1, tok), 1)
+    return jnp.min(jnp.where(live, token, tok - resp), axis=1, keepdims=True).clip(0, tok - resp)
+
+
+def inside_kernel(live_ref, dec_ref, q_ref, key_ref, val_ref, stream_ref, inside_ref, lifted_ref, near_ref):
     heads, tok = dec_ref.shape
     hd = q_ref.shape[1] // heads
     dec = dec_ref[...]
@@ -175,8 +181,7 @@
     cut = tok // 2
     tri = lower_tri(cut)
     resp = near_ref.shape[0] // 3
-    start = start_ref[0]
-    picked = lax.broadcasted_iota(jnp.int32, (resp, tok), 0) + start
+    picked = lax.broadcasted_iota(jnp.int32, (resp, tok), 0) + window_start(live_ref[...] == 1, resp)
     pick = jnp.where(lax.broadcasted_iota(jnp.int32, (resp, tok), 1) == picked, 1.0, 0.0).astype(BF16)
     for h in range(heads):
         cols = slice(h * hd, (h + 1) * hd)
@@ -220,7 +225,7 @@
         cols = pl.ds(off, hd)
         src = keep_ref if side == 0 else other_ref
         lifted = near_ref[resp : 2 * resp, cols].astype(BF16)
-        att = near_ref[:resp, cols] + mm(lifted, src[(r % half) * hd : (r % half + 1) * hd, :])
+        att = near_ref[:resp, cols] + mm(lifted, src[(r % half) * hd : (r % half + 1) * hd, :], 1, 1)
         mixed_ref[:, cols] = near_ref[2 * resp :, cols] + head_norm(att) * again_ref[:, cols]
     mixed = mixed_ref[...]
     scale = lax.rsqrt(jnp.mean(mixed * mixed, axis=-1, keepdims=True) + NORM_EPS)
@@ -235,7 +240,7 @@
     for j in range(half):
         cols = slice(j * hd, (j + 1) * hd)
         st = jnp.where(mine, keep_ref[cols, :].astype(F32), other_ref[cols, :].astype(F32)).astype(BF16)
-        att = inside_ref[:, cols] + mm(lifted_ref[:, cols], st)
+        att = inside_ref[:, cols] + mm(lifted_ref[:, cols], st, 1, 1)
         mixed_ref[:, cols] = stream_ref[:, cols].astype(F32) + head_norm(att) * again_ref[:, cols]
     base_ref[...] = mixed_ref[...].astype(BF16)
     near_ref[...] = mixed_ref[pl.ds(pl.multiple_of(from_ref[0], 16), near_ref.shape[0]), :]
@@ -277,10 +282,7 @@
     hit = mm(spread, place.astype(BF16)) == slot_of.astype(F32)
     w_hi = weight.astype(BF16)
     w_lo = (weight - w_hi.astype(F32)).astype(BF16)
-    token = lax.broadcasted_iota(jnp.int32, (1, tok), 1)
-    start = jnp.min(jnp.where(live, token, tok - resp), axis=1, keepdims=True)
-    start = jnp.minimum(start, tok - resp)
-    picked = lax.broadcasted_iota(jnp.int32, (tok, resp), 1) + start
+    picked = lax.broadcasted_iota(jnp.int32, (tok, resp), 1) + window_start(live, resp)
     pick = jnp.where(lax.broadcasted_iota(jnp.int32, (tok, resp), 0) == picked, 1.0, 0.0).astype(BF16)
     disp_ref[...] = mm(jnp.where(hit, 1.0, 0.0).astype(BF16), pick).astype(BF16)
     side, each = noted(count, resp, lanes)
@@ -456,7 +458,6 @@
         name="states",
     )(bit, key_rows, value_rows, log_decay)
     recv = partner(send)
-    start = jnp.minimum(jnp.argmax(response_mask), tok - resp).astype(jnp.int32).reshape(1)
     plane = lax.shift_right_logical(me, (2 * count).bit_length() - 1).reshape(1).astype(jnp.int32)
     at = (lax.shift_right_logical(me, 1) & (count - 1)).reshape(1).astype(jnp.int32)
     routing = (expert_ids.T, route_weights.T, response_mask.reshape(1, tok))
@@ -499,12 +500,12 @@
             sds((tok, width), BF16),
             sds((3 * resp, width), F32),
         ],
-        in_specs=[SMEM, pl.BlockSpec((half, tok), lambda i: (i, 0)), col, col, col, col],
+        in_specs=[full(routing[2]), pl.BlockSpec((half, tok), lambda i: (i, 0)), col, col, col, col],
         out_specs=[col, col, wcol],
         compiler_params=params(),
         cost_estimate=cost(4 * tok * tok * width, 6 << 20),
         name="inside",
-    )(start, log_decay, query_rows, key_rows, value_rows, stream_in)
+    )(routing[2], log_decay, query_rows, key_rows, value_rows, stream_in)
     gathered, inside, lifted, nearby = lax.optimization_barrier((gathered, inside, lifted, nearby))
     tables = pl.pallas_call(
         functools.partial(plan_kernel, planes=planes, rows=rows),
@@ -554,6 +555,9 @@
 
     gain_col = pl.BlockSpec((1, width // 2), lambda i: (0, i))
     state_all = pl.BlockSpec((half * hd, hd), lambda i: (0, 0))
+    keep, mask = lax.optimization_barrier((keep, response_mask))
+    start = jnp.where(mask == 1, jnp.arange(tok, dtype=jnp.int32), tok - resp).min()
+    start = jnp.minimum(start, tok - resp).astype(jnp.int32).reshape(1)
     near = min(tok, resp + 16)
     first = jnp.minimum(start & -16, tok - near)
     near_col = pl.BlockSpec((near, width // 2), lambda i: (0, i))

time: 110 us -> 109 us (level)
  no operation moved by 1% of the time
where the time goes in v5:
time: 109 us
  Pallas kernels  32.9 us (30%)
  starting transfers between devices  31.7 us (29%)
  waiting for transfers between devices  29.5 us (27%)
  blocking collectives  12.7 us (12%)
    all_to_all x2, waiting for transfers between devices, across_pairs(): return lax.all_to_all(x, BOTH, 0, 0, tiled=True, axis_index_groups=groups)  21.1 us
    ppermute x12, starting transfers between devices, apart(): lax.ppermute(x, BOTH, [(i, i ^ distance) for i in range(lax.axis_size(BOT...  18.5 us
    all_to_all x1, blocking collectives, across_pairs(): return lax.all_to_all(x, BOTH, 0, 0, tiled=True, axis_index_groups=groups)  12.7 us
    all_to_all x2, starting transfers between devices, across_pairs(): return lax.all_to_all(x, BOTH, 0, 0, tiled=True, axis_index_groups=groups)  11.9 us
    pallas_call x1, Pallas kernels, shards(): pl.pallas_call(functools.partial(expert_kernel, count=count, parts=PARTS,...  7.63 us
    ppermute x12, waiting for transfers between devices, apart(): lax.ppermute(x, BOTH, [(i, i ^ distance) for i in range(lax.axis_size(BOT...  6.89 us
    pallas_call x1, Pallas kernels, shards(): pl.pallas_call(inside_kernel, grid=(2,), out_shape=[sds((tok, width), F32...  6.84 us
    pallas_call x1, Pallas kernels, shards(): pl.pallas_call(mixed_kernel, grid=(2,), out_shape=[sds((tok, width), BF16...  4.05 us
  transfers between devices with their start and end apart: 19, of which 9 were waited for; matrix products, arithmetic and copies ran while one was open for 1% of the time, Pallas kernels for 17%

profile of v5, /device:TPU:0, one launch (start us, length us, event | category | flops | bytes accessed | tf_op | source)
XLA Modules:
  0.0 108.6 jit_solution(1475058811627498042)
XLA Ops:
  0.0 3.4 %states.1 = (f32[1032,128]{1,0:T(8,128)}, f32[1032,128]{1,0:T(8,128)}) custom-call(s32[1]{0:T(128)} %bitcast.k_ref, bf16[256,2048]{1,0:T(8,128)(2,1)} %key_ref.1, bf16[256,2048]{1,0:T(8,128)(2,1)} %val_ref.1, f32[16,256]{1,0:T(8,128)} %dec_ref.1), custom_call_target="tpu_custom_call" | custom-call | flops 134217728 | bytes 3145728 | tf_op jit(solution)/shard_map/states/pallas_call | solution.py:447
  3.4 0.5 collective-permute-start
  3.9 1.9 %route.1 = (bf16[256,32]{1,0:T(8,128)(2,1)}, bf16[4,16,128]{2,1,0:T(8,128)(2,1)}) custom-call(s32[8,256]{1,0:T(8,128)} %bitcast.17, f32[8,256]{1,0:T(8,128)} %bitcast.18, s32[1,256]{1,0:T(1,128)} %bitcast.15), custom_call_target="tpu_custom_call" | custom-call | flops 134217728 | bytes 1048576 | tf_op jit(solution)/shard_map/route/pallas_call | solution.py:468
  5.9 0.0 collective-permute-done.recv_ref
  5.9 0.2 collective-permute-start.1
  6.1 0.3 collective-permute-start.2
  6.4 0.2 collective-permute-start.3
  6.6 0.1 copy-done.13
  6.7 2.4 %pair.1 = (bf16[16,80,128]{2,1,0:T(8,128)(2,1)}, f32[1032,128]{1,0:T(8,128)}) custom-call(s32[1]{0:T(128)} %bitcast.k_ref, f32[1032,128]{1,0:T(8,128)} %get-tuple-element.61.own_ref, f32[1032,128]{1,0:T(8,128)} %copy-done.13, bf16[4,16,128]{2,1,0:T(8,128)(2,1)} %get-tuple-element.66.notes_ref), custom_call_target="tpu_custom_call" | custom-call | tf_op jit(solution)/shard_map/pair/pallas_call | solution.py:483
  9.0 8.1 %all-to-all-start = ((bf16[16,80,128]{2,1,0:T(8,128)(2,1)}), bf16[16,80,128]{2,1,0:T(8,128)(2,1)S(1)}, u32[]{:S(2)}, u32[]{:S(2)}) async-start(bf16[16,80,128]{2,1,0:T(8,128)(2,1)} %get-tuple-element.67), calls=%async_computation | async-start | bytes 655360 | tf_op jit(solution)/shard_map/all_to_all | solution.py:73
  17.1 0.0 copy-start.4
  17.1 0.0 copy-start.11
  17.2 0.0 copy-start.12
  17.2 6.8 %inside.1 = (f32[256,2048]{1,0:T(8,128)}, bf16[256,2048]{1,0:T(8,128)(2,1)}, f32[96,2048]{1,0:T(8,128)}) custom-call(s32[1,256]{1,0:T(1,128)} %bitcast.16, f32[16,256]{1,0:T(8,128)} %dec_ref.1, bf16[256,2048]{1,0:T(8,128)(2,1)} %q_ref.1, bf16[256,2048]{1,0:T(8,128)(2,1)} %key_ref.1, bf16[256,2048]{1,0:T(8,128)(2,1)} %val_ref.1, bf16[256,2048]{1,0:T(8,128)(2,1)} %stream_ref.3), custom_call_target="tpu_custom_call" | custom-call | flops 536870912 | bytes 6291456 | tf_op jit(solution)/shard_map/inside/pallas_call | solution.py:495
  24.0 4.9 %all-to-all-done.in_ref = bf16[16,80,128]{2,1,0:T(8,128)(2,1)S(1)} async-done(((bf16[16,80,128]{2,1,0:T(8,128)(2,1)}), bf16[16,80,128]{2,1,0:T(8,128)(2,1)S(1)}, u32[]{:S(2)}, u32[]{:S(2)}) %all-to-all-start) | async-done | bytes 327712 | tf_op jit(solution)/shard_map/all_to_all | solution.py:73
  28.9 0.1 scan.1
  29.0 12.7 %all_to_all.15 = bf16[16,64,128]{2,1,0:T(8,128)(2,1)S(1)} all-to-all(bf16[16,64,128]{2,1,0:T(8,128)(2,1)S(1)} %scan.1), channel_id=1, replica_groups={{0,2,4,6,8,10,12,14,16,18,20,22,24,26,28,30},{1,3,5,7,9,11,13,15,17,19,..., dimensions={0} | all-to-all | bytes 524288 | tf_op jit(solution)/shard_map/all_to_all | solution.py:73
  41.7 0.0 collective-permute-done.1.g1
  41.7 0.0 collective-permute-done.2.u1
  41.7 0.0 collective-permute-done.3.d1
  41.7 0.2 split.1
  41.9 0.1 collective-permute-start.4
  42.0 1.5 %collective-permute-done.4.other_ref = bf16[1024,128]{1,0:T(8,128)(2,1)S(1)} collective-permute-done((bf16[1024,128]{1,0:T(8,128)(2,1)S(1)}, bf16[1024,128]{1,0:T(8,128)(2,1)S(1)}, u32[]{:S(2)}, u32[]{:S(2)}) %collective-permute-start.4) | collective-permute-done | bytes 262176 | tf_op jit(solution)/shard_map/ppermute | solution.py:63
  43.5 0.0 copy-done.11
  43.5 0.0 copy-done.3
  43.5 0.0 copy-start.14
  43.5 2.0 %rows.1 = bf16[256,2048]{1,0:T(8,128)(2,1)} custom-call(s32[1]{0:T(128)} %bitcast.k_ref, f32[96,2048]{1,0:T(8,128)S(1)} %copy-done.3, bf16[1024,128]{1,0:T(8,128)(2,1)S(1)} %get-tuple-element.84.keep_ref, bf16[1024,128]{1,0:T(8,128)(2,1)S(1)} %collective-permute-done.4.other_ref, f32[1,2048]{1,0:T(1,128)S(1)} %bitcast.13, f32[1,2048]{1,0:T(1,128)S(1)} %bitcast.14, ...), custom_call_target="tpu_custom_call" | custom-call | tf_op jit(solution)/shard_map/rows/pallas_call | solution.py:544
  45.5 3.8 %all-to-all-start.2 = ((bf16[16,16,2048]{2,1,0:T(8,128)(2,1)}), bf16[16,16,2048]{2,1,0:T(8,128)(2,1)S(1)}, u32[]{:S(2)}, u32[]{:S(2)}) async-start(bf16[16,16,2048]{2,1,0:T(8,128)(2,1)} %bitcast.8), calls=%async_computation.2 | async-start | bytes 2097152 | tf_op jit(solution)/shard_map/all_to_all | solution.py:73
  49.4 2.8 %plan.1 = (bf16[128,32]{1,0:T(8,128)(2,1)}, bf16[128,32]{1,0:T(8,128)(2,1)}, bf16[128,32]{1,0:T(8,128)(2,1)}, bf16[128,32]{1,0:T(8,128)(2,1)}) custom-call(s32[1]{0:T(128)} %bitcast.9.at_ref, s32[1]{0:T(128)} %bitcast.10.plane_ref, bf16[16,80,128]{2,1,0:T(8,128)(2,1)} %copy-done), custom_call_target="tpu_custom_call" | custom-call | flops 16777216 | bytes 1048576 | tf_op jit(solution)/shard_map/plan/pallas_call | solution.py:510
  52.2 0.0 copy-done.14
  52.2 0.6 fusion
  53.5 4.0 %mixed.1 = (bf16[256,2048]{1,0:T(8,128)(2,1)}, f32[48,2048]{1,0:T(8,128)}) custom-call(s32[1]{0:T(128)} %bitcast.k_ref, s32[1]{0:T(128)S(6)} %min.7.from_ref, bf16[256,2048]{1,0:T(8,128)(2,1)} %get-tuple-element.82.lifted_ref, f32[256,2048]{1,0:T(8,128)} %get-tuple-element.83.inside_ref, bf16[256,2048]{1,0:T(8,128)(2,1)} %stream_ref.3, ...), custom_call_target="tpu_custom_call" | custom-call | flops 134217728 | bytes 7340032 | tf_op jit(solution)/shard_map/mixed/pallas_call | solution.py:564
  57.6 16.2 %all-to-all-done.2.x_hbm = bf16[16,16,2048]{2,1,0:T(8,128)(2,1)S(1)} async-done(((bf16[16,16,2048]{2,1,0:T(8,128)(2,1)}), bf16[16,16,2048]{2,1,0:T(8,128)(2,1)S(1)}, u32[]{:S(2)}, u32[]{:S(2)}) %all-to-all-start.2) | async-done | bytes 1048608 | tf_op jit(solution)/shard_map/all_to_all | solution.py:73
  73.8 7.6 %expert.1 = (bf16[64,1024]{1,0:T(8,128)(2,1)S(1)}, bf16[64,1024]{1,0:T(8,128)(2,1)S(1)}, bf16[64,1024]{1,0:T(8,128)(2,1)S(1)}, bf16[64,1024]{1,0:T(8,128)(2,1)S(...) custom-call(s32[1]{0:T(128)} %bitcast.9.at_ref, ...), custom_call_target="tpu_custom_call" | custom-call | flops 3221225472 | bytes 14680064 | tf_op jit(solution)/shard_map/expert/pallas_call | solution.py:582
  81.4 0.6 collective-permute-start.5
  82.1 2.0 %collective-permute-start.6 = (bf16[64,1024]{1,0:T(8,128)(2,1)S(1)}, bf16[64,1024]{1,0:T(8,128)(2,1)S(1)}, u32[]{:S(2)}, u32[]{:S(2)}) collective-permute-start(bf16[64,1024]{1,0:T(8,128)(2,1)S(1)} %get-tuple-element.103), channel_id=1, source_target_pairs={{0,4},{1,5},{2,6},{3,7},{4,0},{5,1},{6,2},{7,3},{8,12},{9,13},{10,... | collective-permute-start | bytes 393224 | tf_op jit(solution)/shard_map/ppermute | solution.py:67
  84.0 1.0 collective-permute-start.7
  85.0 0.6 collective-permute-start.11
  85.5 2.0 %collective-permute-start.12 = (bf16[64,1024]{1,0:T(8,128)(2,1)S(1)}, bf16[64,1024]{1,0:T(8,128)(2,1)S(1)}, u32[]{:S(2)}, u32[]{:S(2)}) collective-permute-start(bf16[64,1024]{1,0:T(8,128)(2,1)S(1)} %get-tuple-element.111), channel_id=1, source_target_pairs={{0,4},{1,5},{2,6},{3,7},{4,0},{5,1},{6,2},{7,3},{8,12},{9,13},{10,... | collective-permute-start | bytes 393224 | tf_op jit(solution)/shard_map/ppermute | solution.py:67
  87.5 1.7 %collective-permute-done.5.refs_5_ = bf16[64,1024]{1,0:T(8,128)(2,1)S(1)} collective-permute-done((bf16[64,1024]{1,0:T(8,128)(2,1)S(1)}, bf16[64,1024]{1,0:T(8,128)(2,1)S(1)}, u32[]{:S(2)}, u32[]{:S(2)}) %collective-permute-start.5) | collective-permute-done | bytes 131104 | tf_op jit(solution)/shard_map/ppermute | solution.py:67
  89.2 2.2 %collective-permute-start.13 = (bf16[64,1024]{1,0:T(8,128)(2,1)S(1)}, bf16[64,1024]{1,0:T(8,128)(2,1)S(1)}, u32[]{:S(2)}, u32[]{:S(2)}) collective-permute-start(bf16[64,1024]{1,0:T(8,128)(2,1)S(1)} %get-tuple-element.112), channel_id=1, source_target_pairs={{0,6},{1,7},{2,4},{3,5},{4,2},{5,3},{6,0},{7,1},{8,14},{9,15},{10,... | collective-permute-start | bytes 393224 | tf_op jit(solution)/shard_map/ppermute | solution.py:67
  91.4 0.0 collective-permute-done.6.refs_6_
  91.4 0.9 collective-permute-done.7.refs_7_
  92.3 0.0 copy-done.8
  92.3 0.0 copy-done.9
  92.3 0.3 combine.2
  92.7 3.3 %collective-permute-start.8 = (bf16[32,1024]{1,0:T(8,128)(2,1)S(1)}, bf16[32,1024]{1,0:T(8,128)(2,1)S(1)}, u32[]{:S(2)}, u32[]{:S(2)}) collective-permute-start(bf16[32,1024]{1,0:T(8,128)(2,1)S(1)} %get-tuple-element.106), channel_id=1, source_target_pairs={{0,8},{1,9},{2,10},{3,11},{4,12},{5,13},{6,14},{7,15},{8,0},{9,1},... | collective-permute-start | bytes 196616 | tf_op jit(solution)/shard_map/ppermute | solution.py:67
  96.0 0.6 collective-permute-start.9
  96.5 0.0 collective-permute-done.11.refs_5_
  96.6 1.9 %collective-permute-start.10 = (bf16[32,1024]{1,0:T(8,128)(2,1)S(1)}, bf16[32,1024]{1,0:T(8,128)(2,1)S(1)}, u32[]{:S(2)}, u32[]{:S(2)}) collective-permute-start(bf16[32,1024]{1,0:T(8,128)(2,1)S(1)} %get-tuple-element.108), channel_id=1, source_target_pairs={{0,24},{1,25},{2,26},{3,27},{4,28},{5,29},{6,30},{7,31},{8,16},{9,... | collective-permute-start | bytes 196616 | tf_op jit(solution)/shard_map/ppermute | solution.py:67
  98.4 0.0 collective-permute-done.12.refs_6_
  98.4 0.0 collective-permute-done.13.refs_7_
  98.4 0.3 combine.3
  98.8 1.1 %collective-permute-start.14 = (bf16[32,1024]{1,0:T(8,128)(2,1)S(1)}, bf16[32,1024]{1,0:T(8,128)(2,1)S(1)}, u32[]{:S(2)}, u32[]{:S(2)}) collective-permute-start(bf16[32,1024]{1,0:T(8,128)(2,1)S(1)} %get-tuple-element.114), channel_id=1, source_target_pairs={{0,8},{1,9},{2,10},{3,11},{4,12},{5,13},{6,14},{7,15},{8,0},{9,1},... | collective-permute-start | bytes 196616 | tf_op jit(solution)/shard_map/ppermute | solution.py:67
  99.9 1.5 %collective-permute-start.15 = (bf16[32,1024]{1,0:T(8,128)(2,1)S(1)}, bf16[32,1024]{1,0:T(8,128)(2,1)S(1)}, u32[]{:S(2)}, u32[]{:S(2)}) collective-permute-start(bf16[32,1024]{1,0:T(8,128)(2,1)S(1)} %get-tuple-element.115), channel_id=1, source_target_pairs={{0,16},{1,17},{2,18},{3,19},{4,20},{5,21},{6,22},{7,23},{8,24},{9,... | collective-permute-start | bytes 196616 | tf_op jit(solution)/shard_map/ppermute | solution.py:67
  101.4 0.0 collective-permute-done.8.refs_1_
  101.4 1.9 %collective-permute-start.16 = (bf16[32,1024]{1,0:T(8,128)(2,1)S(1)}, bf16[32,1024]{1,0:T(8,128)(2,1)S(1)}, u32[]{:S(2)}, u32[]{:S(2)}) collective-permute-start(bf16[32,1024]{1,0:T(8,128)(2,1)S(1)} %get-tuple-element.116), channel_id=1, source_target_pairs={{0,24},{1,25},{2,26},{3,27},{4,28},{5,29},{6,30},{7,31},{8,16},{9,... | collective-permute-start | bytes 196616 | tf_op jit(solution)/shard_map/ppermute | solution.py:67
  103.2 1.1 collective-permute-done.9.refs_2_
  104.3 0.0 collective-permute-done.10.refs_3_
  104.3 0.3 collective-permute-done.14.refs_5_
  104.6 1.8 %collective-permute-done.15.refs_6_ = bf16[32,1024]{1,0:T(8,128)(2,1)S(1)} collective-permute-done((bf16[32,1024]{1,0:T(8,128)(2,1)S(1)}, bf16[32,1024]{1,0:T(8,128)(2,1)S(1)}, u32[]{:S(2)}, u32[]{:S(2)}) %collective-permute-start.15) | collective-permute-done | bytes 65568 | tf_op jit(solution)/shard_map/ppermute | solution.py:67
  106.4 1.1 %collective-permute-done.16.refs_7_ = bf16[32,1024]{1,0:T(8,128)(2,1)S(1)} collective-permute-done((bf16[32,1024]{1,0:T(8,128)(2,1)S(1)}, bf16[32,1024]{1,0:T(8,128)(2,1)S(1)}, u32[]{:S(2)}, u32[]{:S(2)}) %collective-permute-start.16) | collective-permute-done | bytes 65568 | tf_op jit(solution)/shard_map/ppermute | solution.py:67
  107.5 0.0 copy-done.5
  107.5 1.0 final.1
  (19 shorter events, 0.0 us)
Async XLA Ops:
  3.4 2.5 %collective-permute-start = (f32[1032,128]{1,0:T(8,128)}, f32[1032,128]{1,0:T(8,128)S(1)}, u32[]{:S(2)}, u32[]{:S(2)}) collective-permute-start(f32[1032,128]{1,0:T(8,128)} %get-tuple-element.62), channel_id=1, source_target_pairs={{0,1},{1,0},{2,3},{3,2},{4,5},{5,4},{6,7},{7,6},{8,9},{9,8},{10,11... | collective-permute-start | bytes 1585160 | tf_op jit(solution)/shard_map/ppermute | solution.py:63
  5.9 0.8 copy-start.13
  5.9 35.8 %collective-permute-start.1 = (bf16[2048,512]{1,0:T(8,128)(2,1)}, bf16[2048,512]{1,0:T(8,128)(2,1)}, u32[]{:S(2)}, u32[]{:S(2)}) collective-permute-start(bf16[2048,512]{1,0:T(8,128)(2,1)} %g0), channel_id=1, source_target_pairs={{0,1},{1,0},{2,3},{3,2},{4,5},{5,4},{6,7},{7,6},{8,9},{9,8},{10,11... | collective-permute-start | bytes 6291464 | tf_op jit(solution)/shard_map/ppermute | solution.py:63
  6.1 35.6 %collective-permute-start.2 = (bf16[2048,512]{1,0:T(8,128)(2,1)}, bf16[2048,512]{1,0:T(8,128)(2,1)}, u32[]{:S(2)}, u32[]{:S(2)}) collective-permute-start(bf16[2048,512]{1,0:T(8,128)(2,1)} %u0), channel_id=1, source_target_pairs={{0,1},{1,0},{2,3},{3,2},{4,5},{5,4},{6,7},{7,6},{8,9},{9,8},{10,11... | collective-permute-start | bytes 6291464 | tf_op jit(solution)/shard_map/ppermute | solution.py:63
  6.4 35.3 %collective-permute-start.3 = (bf16[512,2048]{1,0:T(8,128)(2,1)}, bf16[512,2048]{1,0:T(8,128)(2,1)}, u32[]{:S(2)}, u32[]{:S(2)}) collective-permute-start(bf16[512,2048]{1,0:T(8,128)(2,1)} %d0), channel_id=1, source_target_pairs={{0,1},{1,0},{2,3},{3,2},{4,5},{5,4},{6,7},{7,6},{8,9},{9,8},{10,11... | collective-permute-start | bytes 6291464 | tf_op jit(solution)/shard_map/ppermute | solution.py:63
  9.0 19.9 %all-to-all-start = ((bf16[16,80,128]{2,1,0:T(8,128)(2,1)}), bf16[16,80,128]{2,1,0:T(8,128)(2,1)S(1)}, u32[]{:S(2)}, u32[]{:S(2)}) async-start(bf16[16,80,128]{2,1,0:T(8,128)(2,1)} %get-tuple-element.67), calls=%async_computation | async-start | bytes 655360 | tf_op jit(solution)/shard_map/all_to_all | solution.py:73
  17.1 24.5 %copy-start.4 = (f32[1032,128]{1,0:T(8,128)S(1)}, f32[1032,128]{1,0:T(8,128)}, u32[]{:S(2)}) copy-start(f32[1032,128]{1,0:T(8,128)} %get-tuple-element.76.first_ref) | copy-start | bytes 1585156
  17.1 26.4 %copy-start.10 = (bf16[256,32]{1,0:T(8,128)(2,1)S(1)}, bf16[256,32]{1,0:T(8,128)(2,1)}, u32[]{:S(2)}) copy-start(bf16[256,32]{1,0:T(8,128)(2,1)} %get-tuple-element.81.disp_ref) | copy-start | bytes 49156
  17.1 26.4 %copy-start.11 = (f32[2048]{0:T(1024)S(1)}, f32[2048]{0:T(1024)}, u32[]{:S(2)}) copy-start(f32[2048]{0:T(1024)} %param.18) | copy-start | bytes 24580
  17.2 26.3 %copy-start.12 = (f32[2048]{0:T(1024)S(1)}, f32[2048]{0:T(1024)}, u32[]{:S(2)}) copy-start(f32[2048]{0:T(1024)} %param.19) | copy-start | bytes 24580
  24.0 19.5 %copy-start.3 = (f32[96,2048]{1,0:T(8,128)S(1)}, f32[96,2048]{1,0:T(8,128)}, u32[]{:S(2)}) copy-start(f32[96,2048]{1,0:T(8,128)} %get-tuple-element.79.near_ref) | copy-start | bytes 2359300
  28.9 16.6 %copy-start = (bf16[16,80,128]{2,1,0:T(8,128)(2,1)}, bf16[16,80,128]{2,1,0:T(8,128)(2,1)S(1)}, u32[]{:S(2)}) copy-start(bf16[16,80,128]{2,1,0:T(8,128)(2,1)S(1)} %all-to-all-done.in_ref) | copy-start | bytes 983044
  41.9 3.6 %copy-start.1 = (bf16[1024,128]{1,0:T(8,128)(2,1)}, bf16[1024,128]{1,0:T(8,128)(2,1)S(1)}, u32[]{:S(2)}) copy-start(bf16[1024,128]{1,0:T(8,128)(2,1)S(1)} %get-tuple-element.84.keep_ref) | copy-start | bytes 786436
  41.9 1.6 %collective-permute-start.4 = (bf16[1024,128]{1,0:T(8,128)(2,1)S(1)}, bf16[1024,128]{1,0:T(8,128)(2,1)S(1)}, u32[]{:S(2)}, u32[]{:S(2)}) collective-permute-start(bf16[1024,128]{1,0:T(8,128)(2,1)S(1)} %get-tuple-element.80), channel_id=1, source_target_pairs={{0,1},{1,0},{2,3},{3,2},{4,5},{5,4},{6,7},{7,6},{8,9},{9,8},{10,11... | collective-permute-start | bytes 786440 | tf_op jit(solution)/shard_map/ppermute | solution.py:63
  43.5 2.0 %copy-start.2 = (bf16[1024,128]{1,0:T(8,128)(2,1)}, bf16[1024,128]{1,0:T(8,128)(2,1)S(1)}, u32[]{:S(2)}) copy-start(bf16[1024,128]{1,0:T(8,128)(2,1)S(1)} %collective-permute-done.4.other_ref) | copy-start | bytes 786436
  43.5 8.7 %copy-start.14 = (s32[256]{0:T(256)S(1)}, s32[256]{0:T(256)}, u32[]{:S(2)}) copy-start(s32[256]{0:T(256)} %param.22) | copy-start | bytes 3076
  45.5 28.3 %all-to-all-start.2 = ((bf16[16,16,2048]{2,1,0:T(8,128)(2,1)}), bf16[16,16,2048]{2,1,0:T(8,128)(2,1)S(1)}, u32[]{:S(2)}, u32[]{:S(2)}) async-start(bf16[16,16,2048]{2,1,0:T(8,128)(2,1)} %bitcast.8), calls=%async_computation.2 | async-start | bytes 2097152 | tf_op jit(solution)/shard_map/all_to_all | solution.py:73
  73.8 18.5 %copy-start.6 = (bf16[128,32]{1,0:T(8,128)(2,1)S(1)}, bf16[128,32]{1,0:T(8,128)(2,1)}, u32[]{:S(2)}) copy-start(bf16[128,32]{1,0:T(8,128)(2,1)} %get-tuple-element.93.refs_0_) | copy-start | bytes 24580
  73.8 18.5 %copy-start.7 = (bf16[128,32]{1,0:T(8,128)(2,1)S(1)}, bf16[128,32]{1,0:T(8,128)(2,1)}, u32[]{:S(2)}) copy-start(bf16[128,32]{1,0:T(8,128)(2,1)} %get-tuple-element.94.refs_1_) | copy-start | bytes 24580
  73.8 18.5 %copy-start.8 = (bf16[128,32]{1,0:T(8,128)(2,1)S(1)}, bf16[128,32]{1,0:T(8,128)(2,1)}, u32[]{:S(2)}) copy-start(bf16[128,32]{1,0:T(8,128)(2,1)} %get-tuple-element.95.refs_2_) | copy-start | bytes 24580
  73.8 18.5 %copy-start.9 = (bf16[128,32]{1,0:T(8,128)(2,1)S(1)}, bf16[128,32]{1,0:T(8,128)(2,1)}, u32[]{:S(2)}) copy-start(bf16[128,32]{1,0:T(8,128)(2,1)} %get-tuple-element.96.refs_3_) | copy-start | bytes 24580
  73.8 33.7 %copy-start.5 = (f32[48,2048]{1,0:T(8,128)S(1)}, f32[48,2048]{1,0:T(8,128)}, u32[]{:S(2)}) copy-start(f32[48,2048]{1,0:T(8,128)} %get-tuple-element.92.near_ref) | copy-start | bytes 1179652
  81.4 7.7 %collective-permute-start.5 = (bf16[64,1024]{1,0:T(8,128)(2,1)S(1)}, bf16[64,1024]{1,0:T(8,128)(2,1)S(1)}, u32[]{:S(2)}, u32[]{:S(2)}) collective-permute-start(bf16[64,1024]{1,0:T(8,128)(2,1)S(1)} %get-tuple-element.102), channel_id=1, source_target_pairs={{0,2},{1,3},{2,0},{3,1},{4,6},{5,7},{6,4},{7,5},{8,10},{9,11},{10,... | collective-permute-start | bytes 393224 | tf_op jit(solution)/shard_map/ppermute | solution.py:67
  82.1 9.3 %collective-permute-start.6 = (bf16[64,1024]{1,0:T(8,128)(2,1)S(1)}, bf16[64,1024]{1,0:T(8,128)(2,1)S(1)}, u32[]{:S(2)}, u32[]{:S(2)}) collective-permute-start(bf16[64,1024]{1,0:T(8,128)(2,1)S(1)} %get-tuple-element.103), channel_id=1, source_target_pairs={{0,4},{1,5},{2,6},{3,7},{4,0},{5,1},{6,2},{7,3},{8,12},{9,13},{10,... | collective-permute-start | bytes 393224 | tf_op jit(solution)/shard_map/ppermute | solution.py:67
  84.0 8.3 %collective-permute-start.7 = (bf16[64,1024]{1,0:T(8,128)(2,1)S(1)}, bf16[64,1024]{1,0:T(8,128)(2,1)S(1)}, u32[]{:S(2)}, u32[]{:S(2)}) collective-permute-start(bf16[64,1024]{1,0:T(8,128)(2,1)S(1)} %get-tuple-element.104), channel_id=1, source_target_pairs={{0,6},{1,7},{2,4},{3,5},{4,2},{5,3},{6,0},{7,1},{8,14},{9,15},{10,... | collective-permute-start | bytes 393224 | tf_op jit(solution)/shard_map/ppermute | solution.py:67
  85.0 11.6 %collective-permute-start.11 = (bf16[64,1024]{1,0:T(8,128)(2,1)S(1)}, bf16[64,1024]{1,0:T(8,128)(2,1)S(1)}, u32[]{:S(2)}, u32[]{:S(2)}) collective-permute-start(bf16[64,1024]{1,0:T(8,128)(2,1)S(1)} %get-tuple-element.110), channel_id=1, source_target_pairs={{0,2},{1,3},{2,0},{3,1},{4,6},{5,7},{6,4},{7,5},{8,10},{9,11},{10,... | collective-permute-start | bytes 393224 | tf_op jit(solution)/shard_map/ppermute | solution.py:67
  85.5 12.9 %collective-permute-start.12 = (bf16[64,1024]{1,0:T(8,128)(2,1)S(1)}, bf16[64,1024]{1,0:T(8,128)(2,1)S(1)}, u32[]{:S(2)}, u32[]{:S(2)}) collective-permute-start(bf16[64,1024]{1,0:T(8,128)(2,1)S(1)} %get-tuple-element.111), channel_id=1, source_target_pairs={{0,4},{1,5},{2,6},{3,7},{4,0},{5,1},{6,2},{7,3},{8,12},{9,13},{10,... | collective-permute-start | bytes 393224 | tf_op jit(solution)/shard_map/ppermute | solution.py:67
  89.2 9.2 %collective-permute-start.13 = (bf16[64,1024]{1,0:T(8,128)(2,1)S(1)}, bf16[64,1024]{1,0:T(8,128)(2,1)S(1)}, u32[]{:S(2)}, u32[]{:S(2)}) collective-permute-start(bf16[64,1024]{1,0:T(8,128)(2,1)S(1)} %get-tuple-element.112), channel_id=1, source_target_pairs={{0,6},{1,7},{2,4},{3,5},{4,2},{5,3},{6,0},{7,1},{8,14},{9,15},{10,... | collective-permute-start | bytes 393224 | tf_op jit(solution)/shard_map/ppermute | solution.py:67
  92.7 8.7 %collective-permute-start.8 = (bf16[32,1024]{1,0:T(8,128)(2,1)S(1)}, bf16[32,1024]{1,0:T(8,128)(2,1)S(1)}, u32[]{:S(2)}, u32[]{:S(2)}) collective-permute-start(bf16[32,1024]{1,0:T(8,128)(2,1)S(1)} %get-tuple-element.106), channel_id=1, source_target_pairs={{0,8},{1,9},{2,10},{3,11},{4,12},{5,13},{6,14},{7,15},{8,0},{9,1},... | collective-permute-start | bytes 196616 | tf_op jit(solution)/shard_map/ppermute | solution.py:67
  96.0 8.3 %collective-permute-start.9 = (bf16[32,1024]{1,0:T(8,128)(2,1)S(1)}, bf16[32,1024]{1,0:T(8,128)(2,1)S(1)}, u32[]{:S(2)}, u32[]{:S(2)}) collective-permute-start(bf16[32,1024]{1,0:T(8,128)(2,1)S(1)} %get-tuple-element.107), channel_id=1, source_target_pairs={{0,16},{1,17},{2,18},{3,19},{4,20},{5,21},{6,22},{7,23},{8,24},{9,... | collective-permute-start | bytes 196616 | tf_op jit(solution)/shard_map/ppermute | solution.py:67
  96.6 7.7 %collective-permute-start.10 = (bf16[32,1024]{1,0:T(8,128)(2,1)S(1)}, bf16[32,1024]{1,0:T(8,128)(2,1)S(1)}, u32[]{:S(2)}, u32[]{:S(2)}) collective-permute-start(bf16[32,1024]{1,0:T(8,128)(2,1)S(1)} %get-tuple-element.108), channel_id=1, source_target_pairs={{0,24},{1,25},{2,26},{3,27},{4,28},{5,29},{6,30},{7,31},{8,16},{9,... | collective-permute-start | bytes 196616 | tf_op jit(solution)/shard_map/ppermute | solution.py:67
  98.8 5.8 %collective-permute-start.14 = (bf16[32,1024]{1,0:T(8,128)(2,1)S(1)}, bf16[32,1024]{1,0:T(8,128)(2,1)S(1)}, u32[]{:S(2)}, u32[]{:S(2)}) collective-permute-start(bf16[32,1024]{1,0:T(8,128)(2,1)S(1)} %get-tuple-element.114), channel_id=1, source_target_pairs={{0,8},{1,9},{2,10},{3,11},{4,12},{5,13},{6,14},{7,15},{8,0},{9,1},... | collective-permute-start | bytes 196616 | tf_op jit(solution)/shard_map/ppermute | solution.py:67
  99.9 6.5 %collective-permute-start.15 = (bf16[32,1024]{1,0:T(8,128)(2,1)S(1)}, bf16[32,1024]{1,0:T(8,128)(2,1)S(1)}, u32[]{:S(2)}, u32[]{:S(2)}) collective-permute-start(bf16[32,1024]{1,0:T(8,128)(2,1)S(1)} %get-tuple-element.115), channel_id=1, source_target_pairs={{0,16},{1,17},{2,18},{3,19},{4,20},{5,21},{6,22},{7,23},{8,24},{9,... | collective-permute-start | bytes 196616 | tf_op jit(solution)/shard_map/ppermute | solution.py:67
  101.4 6.2 %collective-permute-start.16 = (bf16[32,1024]{1,0:T(8,128)(2,1)S(1)}, bf16[32,1024]{1,0:T(8,128)(2,1)S(1)}, u32[]{:S(2)}, u32[]{:S(2)}) collective-permute-start(bf16[32,1024]{1,0:T(8,128)(2,1)S(1)} %get-tuple-element.116), channel_id=1, source_target_pairs={{0,24},{1,25},{2,26},{3,27},{4,28},{5,29},{6,30},{7,31},{8,16},{9,... | collective-permute-start | bytes 196616 | tf_op jit(solution)/shard_map/ppermute | solution.py:67

commit v6 on v5

--- a/solution.py
+++ b/solution.py
@@ -346,8 +346,8 @@
         outs[m][...] = (mm(hi, got, 0, 0) + mm(lo, got, 0, 0)).astype(outs[m].dtype)
 
 
-def expert_kernel(at_ref, plane_ref, x_hbm, g0, u0, d0, g1, u1, d1, *refs, count, parts, step):
-    outs, (gv, uv, dv, hid_ref, x_ref, sems) = refs[: count * parts], refs[count * parts :]
+def expert_kernel(at_ref, plane_ref, x_hbm, g0, u0, d0, g1, u1, d1, *refs, count, step):
+    outs, (hid_out, gv, uv, dv, hid_ref, x_ref, sems) = refs[:count], refs[count:]
     units = g0.shape[1]
     rows, part = outs[0].shape
     cuts = range(0, units, step)
@@ -363,7 +363,7 @@
             gets.append(copy(g.at[:, cols], gv.at[n, :, cols], sems, len(gets)))
             gets.append(copy(u.at[:, cols], uv.at[n, :, cols], sems, len(gets)))
     for n, d in enumerate((d0, d1)):
-        gets.append(copy(d, dv.at[n], sems, len(gets)))
+        gets.append(copy(d.at[:, pl.ds(0, part)], dv.at[n], sems, len(gets)))
     for c in gets[:at]:
         c.wait()
     many = count * rows
@@ -378,16 +378,32 @@
                 gate = mm(x, gv[n, :, c : c + step])
                 up = mm(x, uv[n, :, c : c + step])
                 hid_ref[n, r : r + block, c : c + step] = (gate / (1.0 + jnp.exp(-gate)) * up).astype(BF16)
+    put = copy(hid_ref, hid_out, sems, len(gets))
     gets[at].wait()
     gets[at + 1].wait()
-    for r in range(0, many, block):
-        for c in range(0, part * parts, 256):
-            p0 = mm(hid_ref[0, r : r + block, :], dv[0, :, c : c + 256]).astype(BF16).astype(F32)
-            p1 = mm(hid_ref[1, r : r + block, :], dv[1, :, c : c + 256]).astype(BF16).astype(F32)
+    down(hid_ref, dv, outs, block)
+    put.wait()
+
+
+def down(hid_ref, down_ref, outs, block):
+    rows, part = outs[0].shape
+    for r in range(0, rows * len(outs), block):
+        for c in range(0, part, 256):
+            cols = slice(c, c + 256)
+            p0 = mm(hid_ref[0, r : r + block, :], down_ref[0, :, cols]).astype(BF16).astype(F32)
+            p1 = mm(hid_ref[1, r : r + block, :], down_ref[1, :, cols]).astype(BF16).astype(F32)
             p = (p0 + p1).astype(BF16)
             for q in range(r // rows, (r + block) // rows):
-                out_ref = outs[c // part * count + q]
-                out_ref[:, c % part : c % part + 256] = p[q * rows - r : (q + 1) * rows - r, :]
+                outs[q][:, cols] = p[q * rows - r : (q + 1) * rows - r, :]
+
+
+def down_kernel(hid_ref, d0, d1, *refs, count, first):
+    outs, (dv, sems) = refs[:count], refs[count:]
+    part = outs[0].shape[1]
+    gets = [copy(d.at[:, pl.ds(first, part)], dv.at[n], sems, n) for n, d in enumerate((d0, d1))]
+    for c in gets:
+        c.wait()
+    down(hid_ref, dv, outs, min(256, hid_ref.shape[1]))
 
 
 def final_kernel(start_ref, from_ref, base_hbm, near_ref, *refs, parts, planes):
@@ -579,26 +595,36 @@
     units = gate_weight.shape[1]
     step = min(256, units)
     many = count * chunk.shape[0]
-    results = pl.pallas_call(
-        functools.partial(expert_kernel, count=count, parts=PARTS, step=step),
-        grid=(1,),
-        out_shape=[chunk] * (count * PARTS),
+    hidden = sds((2, many, units), BF16)
+    *results, hid = pl.pallas_call(
+        functools.partial(expert_kernel, count=count, step=step),
+        grid=(1,),
+        out_shape=[chunk] * count + [hidden],
         in_specs=[SMEM, SMEM] + [HBM] * 7,
-        out_specs=[full(chunk)] * (count * PARTS),
+        out_specs=[full(chunk)] * count + [HBM],
         scratch_shapes=[pltpu.VMEM((2, width, units), BF16)] * 2
-        + [pltpu.VMEM((2, units, width), BF16), pltpu.VMEM((2, many, units), BF16), pltpu.VMEM((many, width), BF16)]
-        + [DMA((pairs + 4 * (units // step) + 2,))],
+        + [pltpu.VMEM((2, units, part), BF16), pltpu.VMEM(hidden.shape, BF16), pltpu.VMEM((many, width), BF16)]
+        + [DMA((pairs + 4 * (units // step) + 3,))],
         compiler_params=params(48),
-        cost_estimate=cost(12 * many * width * units, 14 << 20),
+        cost_estimate=cost(10 * many * width * units, 12 << 20),
         name="expert",
     )(at, plane, arrived, gate_own, up_own, down_own, gate_other, up_other, down_other)
-    backs = []
-    for c in range(PARTS):
-        mine = results[c * count : (c + 1) * count]
-        backs.append([mine[0]] + [apart(mine[m], 2 * m) for m in range(1, count)])
     shares = []
     for c in range(PARTS):
-        operands = (*tables, *backs[c])
+        if c:
+            results = pl.pallas_call(
+                functools.partial(down_kernel, count=count, first=c * part),
+                grid=(1,),
+                out_shape=[chunk] * count,
+                in_specs=[full(hid), HBM, HBM],
+                out_specs=[full(chunk)] * count,
+                scratch_shapes=[pltpu.VMEM((2, units, part), BF16), DMA((2,))],
+                compiler_params=params(48),
+                cost_estimate=cost(2 * many * width * units, 2 << 20),
+                name="down",
+            )(hid, down_own, down_other)
+        back = [results[0]] + [apart(results[m], 2 * m) for m in range(1, count)]
+        operands = (*tables, *back)
         kinds = [sds((resp, part), F32)] + [row_part] * (planes - 1)
         sums = pl.pallas_call(
             functools.partial(combine_kernel, planes=planes, count=count),

time: 109 us -> 107 us (0.982)
  waiting for transfers between devices: 29.5 us -> 27 us
  Pallas kernels: 32.9 us -> 34.5 us
    ppermute x12, waiting for transfers between devices: 6.89 us -> 4.43 us  [apart(): lax.ppermute(x, BOTH, [(i, i ^ distance) for i in range(lax.axis_size(BOT...]
    pallas_call x1 -> x2, Pallas kernels: 7.63 us -> 9.21 us  [the longest x1 6.87 us: shards(): pl.pallas_call(functools.partial(expert_kernel, count=count, step=step),...]
  transfers between devices with their start and end apart: 19 -> 19, of which waited for: 9 -> 7; matrix products, arithmetic and copies ran while one was open for 1% -> 1% of each run, Pallas kernels for 17% -> 20%
where the time goes in v6:
time: 107 us
  Pallas kernels  34.5 us (32%)
  starting transfers between devices  30.9 us (29%)
  waiting for transfers between devices  27 us (25%)
  blocking collectives  12.7 us (12%)
    all_to_all x2, waiting for transfers between devices, across_pairs(): return lax.all_to_all(x, BOTH, 0, 0, tiled=True, axis_index_groups=groups)  21.1 us
    ppermute x12, starting transfers between devices, apart(): lax.ppermute(x, BOTH, [(i, i ^ distance) for i in range(lax.axis_size(BOT...  17.7 us
    all_to_all x1, blocking collectives, across_pairs(): return lax.all_to_all(x, BOTH, 0, 0, tiled=True, axis_index_groups=groups)  12.7 us
    all_to_all x2, starting transfers between devices, across_pairs(): return lax.all_to_all(x, BOTH, 0, 0, tiled=True, axis_index_groups=groups)  11.9 us
    pallas_call x1, Pallas kernels, shards(): pl.pallas_call(functools.partial(expert_kernel, count=count, step=step),...  6.87 us
    pallas_call x1, Pallas kernels, shards(): pl.pallas_call(inside_kernel, grid=(2,), out_shape=[sds((tok, width), F32...  6.84 us
    ppermute x12, waiting for transfers between devices, apart(): lax.ppermute(x, BOTH, [(i, i ^ distance) for i in range(lax.axis_size(BOT...  4.43 us
    pallas_call x1, Pallas kernels, shards(): pl.pallas_call(mixed_kernel, grid=(2,), out_shape=[sds((tok, width), BF16...  4.07 us
  transfers between devices with their start and end apart: 19, of which 7 were waited for; matrix products, arithmetic and copies ran while one was open for 1% of the time, Pallas kernels for 20%

profile of v6, /device:TPU:0, one launch (start us, length us, event | category | flops | bytes accessed | tf_op | source)
XLA Modules:
  0.0 107.0 jit_solution(2493357195842255004)
XLA Ops:
  0.0 3.4 %states.1 = (f32[1032,128]{1,0:T(8,128)}, f32[1032,128]{1,0:T(8,128)}) custom-call(s32[1]{0:T(128)} %bitcast.k_ref, bf16[256,2048]{1,0:T(8,128)(2,1)} %key_ref.1, bf16[256,2048]{1,0:T(8,128)(2,1)} %val_ref.1, f32[16,256]{1,0:T(8,128)} %dec_ref.1), custom_call_target="tpu_custom_call" | custom-call | flops 134217728 | bytes 3145728 | tf_op jit(solution)/shard_map/states/pallas_call | solution.py:463
  3.4 0.5 collective-permute-start
  3.9 1.9 %route.1 = (bf16[256,32]{1,0:T(8,128)(2,1)}, bf16[4,16,128]{2,1,0:T(8,128)(2,1)}) custom-call(s32[8,256]{1,0:T(8,128)} %bitcast.17, f32[8,256]{1,0:T(8,128)} %bitcast.18, s32[1,256]{1,0:T(1,128)} %bitcast.15), custom_call_target="tpu_custom_call" | custom-call | flops 134217728 | bytes 1048576 | tf_op jit(solution)/shard_map/route/pallas_call | solution.py:484
  5.9 0.0 collective-permute-done.recv_ref
  5.9 0.2 collective-permute-start.1
  6.1 0.3 collective-permute-start.2
  6.4 0.2 collective-permute-start.3
  6.6 0.1 copy-done.13
  6.7 2.4 %pair.1 = (bf16[16,80,128]{2,1,0:T(8,128)(2,1)}, f32[1032,128]{1,0:T(8,128)}) custom-call(s32[1]{0:T(128)} %bitcast.k_ref, f32[1032,128]{1,0:T(8,128)} %get-tuple-element.62.own_ref, f32[1032,128]{1,0:T(8,128)} %copy-done.13, bf16[4,16,128]{2,1,0:T(8,128)(2,1)} %get-tuple-element.67.notes_ref), custom_call_target="tpu_custom_call" | custom-call | tf_op jit(solution)/shard_map/pair/pallas_call | solution.py:499
  9.0 8.1 %all-to-all-start = ((bf16[16,80,128]{2,1,0:T(8,128)(2,1)}), bf16[16,80,128]{2,1,0:T(8,128)(2,1)S(1)}, u32[]{:S(2)}, u32[]{:S(2)}) async-start(bf16[16,80,128]{2,1,0:T(8,128)(2,1)} %get-tuple-element.68), calls=%async_computation | async-start | bytes 655360 | tf_op jit(solution)/shard_map/all_to_all | solution.py:73
  17.1 0.0 copy-start.4
  17.2 0.0 copy-start.11
  17.2 0.0 copy-start.12
  17.2 6.8 %inside.1 = (f32[256,2048]{1,0:T(8,128)}, bf16[256,2048]{1,0:T(8,128)(2,1)}, f32[96,2048]{1,0:T(8,128)}) custom-call(s32[1,256]{1,0:T(1,128)} %bitcast.16, f32[16,256]{1,0:T(8,128)} %dec_ref.1, bf16[256,2048]{1,0:T(8,128)(2,1)} %q_ref.1, bf16[256,2048]{1,0:T(8,128)(2,1)} %key_ref.1, bf16[256,2048]{1,0:T(8,128)(2,1)} %val_ref.1, bf16[256,2048]{1,0:T(8,128)(2,1)} %stream_ref.3), custom_call_target="tpu_custom_call" | custom-call | flops 536870912 | bytes 6291456 | tf_op jit(solution)/shard_map/inside/pallas_call | solution.py:511
  24.0 4.9 %all-to-all-done.in_ref = bf16[16,80,128]{2,1,0:T(8,128)(2,1)S(1)} async-done(((bf16[16,80,128]{2,1,0:T(8,128)(2,1)}), bf16[16,80,128]{2,1,0:T(8,128)(2,1)S(1)}, u32[]{:S(2)}, u32[]{:S(2)}) %all-to-all-start) | async-done | bytes 327712 | tf_op jit(solution)/shard_map/all_to_all | solution.py:73
  28.9 0.1 scan.1
  29.0 12.7 %all_to_all.15 = bf16[16,64,128]{2,1,0:T(8,128)(2,1)S(1)} all-to-all(bf16[16,64,128]{2,1,0:T(8,128)(2,1)S(1)} %scan.1), channel_id=1, replica_groups={{0,2,4,6,8,10,12,14,16,18,20,22,24,26,28,30},{1,3,5,7,9,11,13,15,17,19,..., dimensions={0} | all-to-all | bytes 524288 | tf_op jit(solution)/shard_map/all_to_all | solution.py:73
  41.7 0.0 collective-permute-done.1.g1
  41.7 0.0 collective-permute-done.2.u1
  41.7 0.0 collective-permute-done.3.d1
  41.7 0.0 copy-done.4
  41.7 0.2 split.1
  41.9 0.0 copy-start.1
  41.9 0.1 collective-permute-start.4
  42.0 1.5 %collective-permute-done.4.other_ref = bf16[1024,128]{1,0:T(8,128)(2,1)S(1)} collective-permute-done((bf16[1024,128]{1,0:T(8,128)(2,1)S(1)}, bf16[1024,128]{1,0:T(8,128)(2,1)S(1)}, u32[]{:S(2)}, u32[]{:S(2)}) %collective-permute-start.4) | collective-permute-done | bytes 262176 | tf_op jit(solution)/shard_map/ppermute | solution.py:63
  43.5 0.0 copy-start.14
  43.5 2.0 %rows.1 = bf16[256,2048]{1,0:T(8,128)(2,1)} custom-call(s32[1]{0:T(128)} %bitcast.k_ref, f32[96,2048]{1,0:T(8,128)S(1)} %copy-done.3, bf16[1024,128]{1,0:T(8,128)(2,1)S(1)} %get-tuple-element.85.keep_ref, bf16[1024,128]{1,0:T(8,128)(2,1)S(1)} %collective-permute-done.4.other_ref, f32[1,2048]{1,0:T(1,128)S(1)} %bitcast.13, f32[1,2048]{1,0:T(1,128)S(1)} %bitcast.14, ...), custom_call_target="tpu_custom_call" | custom-call | tf_op jit(solution)/shard_map/rows/pallas_call | solution.py:560
  45.5 0.0 copy-done.2
  45.5 3.8 %all-to-all-start.2 = ((bf16[16,16,2048]{2,1,0:T(8,128)(2,1)}), bf16[16,16,2048]{2,1,0:T(8,128)(2,1)S(1)}, u32[]{:S(2)}, u32[]{:S(2)}) async-start(bf16[16,16,2048]{2,1,0:T(8,128)(2,1)} %bitcast.8), calls=%async_computation.2 | async-start | bytes 2097152 | tf_op jit(solution)/shard_map/all_to_all | solution.py:73
  49.4 2.8 %plan.1 = (bf16[128,32]{1,0:T(8,128)(2,1)}, bf16[128,32]{1,0:T(8,128)(2,1)}, bf16[128,32]{1,0:T(8,128)(2,1)}, bf16[128,32]{1,0:T(8,128)(2,1)}) custom-call(s32[1]{0:T(128)} %bitcast.9.at_ref, s32[1]{0:T(128)} %bitcast.10.plane_ref, bf16[16,80,128]{2,1,0:T(8,128)(2,1)} %copy-done), custom_call_target="tpu_custom_call" | custom-call | flops 16777216 | bytes 1048576 | tf_op jit(solution)/shard_map/plan/pallas_call | solution.py:526
  52.2 0.6 fusion
  53.5 4.1 %mixed.1 = (bf16[256,2048]{1,0:T(8,128)(2,1)}, f32[48,2048]{1,0:T(8,128)}) custom-call(s32[1]{0:T(128)} %bitcast.k_ref, s32[1]{0:T(128)S(6)} %min.7.from_ref, bf16[256,2048]{1,0:T(8,128)(2,1)} %get-tuple-element.83.lifted_ref, f32[256,2048]{1,0:T(8,128)} %get-tuple-element.84.inside_ref, bf16[256,2048]{1,0:T(8,128)(2,1)} %stream_ref.3, ...), custom_call_target="tpu_custom_call" | custom-call | flops 134217728 | bytes 7340032 | tf_op jit(solution)/shard_map/mixed/pallas_call | solution.py:580
  57.6 16.2 %all-to-all-done.2.x_hbm = bf16[16,16,2048]{2,1,0:T(8,128)(2,1)S(1)} async-done(((bf16[16,16,2048]{2,1,0:T(8,128)(2,1)}), bf16[16,16,2048]{2,1,0:T(8,128)(2,1)S(1)}, u32[]{:S(2)}, u32[]{:S(2)}) %all-to-all-start.2) | async-done | bytes 1048608 | tf_op jit(solution)/shard_map/all_to_all | solution.py:73
  73.8 6.9 %expert.1 = (bf16[64,1024]{1,0:T(8,128)(2,1)S(1)}, bf16[64,1024]{1,0:T(8,128)(2,1)S(1)}, bf16[64,1024]{1,0:T(8,128)(2,1)S(1)}, bf16[64,1024]{1,0:T(8,128)(2,1)S(1)}, bf16[2,256,512]{2,1,0:T(8,128)(2,1)S(1)}) custom-call(s32[1]{0:T(128)} %bitcast.9.at_ref, s32[1]{0:T(128)} %bitcast.10.plane_ref, bf16[16,16,2048]{2,1,0:T(8,128)(2,1)S(1)} %all-to-all-done.2.x_hbm, ...), custom_call_target="tpu_custom_call" | custom-call | flops 2684354560 | bytes 12582912 | tf_op jit(solution)/shard_map/expert/pallas_call | solution.py:599
  80.7 0.6 collective-permute-start.5
  81.3 2.0 %collective-permute-start.6 = (bf16[64,1024]{1,0:T(8,128)(2,1)S(1)}, bf16[64,1024]{1,0:T(8,128)(2,1)S(1)}, u32[]{:S(2)}, u32[]{:S(2)}) collective-permute-start(bf16[64,1024]{1,0:T(8,128)(2,1)S(1)} %get-tuple-element.104), channel_id=1, source_target_pairs={{0,4},{1,5},{2,6},{3,7},{4,0},{5,1},{6,2},{7,3},{8,12},{9,13},{10,... | collective-permute-start | bytes 393224 | tf_op jit(solution)/shard_map/ppermute | solution.py:67
  83.3 1.0 collective-permute-start.7
  84.2 2.3 %down.1 = (bf16[64,1024]{1,0:T(8,128)(2,1)S(1)}, bf16[64,1024]{1,0:T(8,128)(2,1)S(1)}, bf16[64,1024]{1,0:T(8,128)(2,1)S(1)}, bf16[64,1024]{1,0:T(8,128)(2,1)S(1)}) custom-call(bf16[2,256,512]{2,1,0:T(8,128)(2,1)S(1)} %get-tuple-element.110.hid_ref, bf16[512,2048]{1,0:T(8,128)(2,1)} %d0.1, bf16[512,2048]{1,0:T(8,128)(2,1)} %collective-permute-done.3.d1), custom_call_target="tpu_custom_call" | custom-call | flops 536870912 | bytes 2097152 | tf_op jit(solution)/shard_map/down/pallas_call | solution.py:615
  86.6 0.6 collective-permute-start.11
  87.2 2.0 %collective-permute-start.12 = (bf16[64,1024]{1,0:T(8,128)(2,1)S(1)}, bf16[64,1024]{1,0:T(8,128)(2,1)S(1)}, u32[]{:S(2)}, u32[]{:S(2)}) collective-permute-start(bf16[64,1024]{1,0:T(8,128)(2,1)S(1)} %get-tuple-element.113), channel_id=1, source_target_pairs={{0,4},{1,5},{2,6},{3,7},{4,0},{5,1},{6,2},{7,3},{8,12},{9,13},{10,... | collective-permute-start | bytes 393224 | tf_op jit(solution)/shard_map/ppermute | solution.py:67
  89.2 0.0 collective-permute-done.5.refs_5_
  89.2 1.0 collective-permute-start.13
  90.1 0.0 collective-permute-done.6.refs_6_
  90.1 0.1 collective-permute-done.7.refs_7_
  90.2 0.0 copy-done.8
  90.2 0.3 combine.2
  90.6 3.3 %collective-permute-start.8 = (bf16[32,1024]{1,0:T(8,128)(2,1)S(1)}, bf16[32,1024]{1,0:T(8,128)(2,1)S(1)}, u32[]{:S(2)}, u32[]{:S(2)}) collective-permute-start(bf16[32,1024]{1,0:T(8,128)(2,1)S(1)} %get-tuple-element.107), channel_id=1, source_target_pairs={{0,8},{1,9},{2,10},{3,11},{4,12},{5,13},{6,14},{7,15},{8,0},{9,1},... | collective-permute-start | bytes 196616 | tf_op jit(solution)/shard_map/ppermute | solution.py:67
  93.9 0.7 collective-permute-start.9
  94.5 0.0 collective-permute-done.11.refs_5_
  94.6 2.1 %collective-permute-start.10 = (bf16[32,1024]{1,0:T(8,128)(2,1)S(1)}, bf16[32,1024]{1,0:T(8,128)(2,1)S(1)}, u32[]{:S(2)}, u32[]{:S(2)}) collective-permute-start(bf16[32,1024]{1,0:T(8,128)(2,1)S(1)} %get-tuple-element.109), channel_id=1, source_target_pairs={{0,24},{1,25},{2,26},{3,27},{4,28},{5,29},{6,30},{7,31},{8,16},{9,... | collective-permute-start | bytes 196616 | tf_op jit(solution)/shard_map/ppermute | solution.py:67
  96.7 0.0 collective-permute-done.12.refs_6_
  96.7 0.0 collective-permute-done.13.refs_7_
  96.7 0.3 combine.3
  97.0 1.7 %collective-permute-start.14 = (bf16[32,1024]{1,0:T(8,128)(2,1)S(1)}, bf16[32,1024]{1,0:T(8,128)(2,1)S(1)}, u32[]{:S(2)}, u32[]{:S(2)}) collective-permute-start(bf16[32,1024]{1,0:T(8,128)(2,1)S(1)} %get-tuple-element.116), channel_id=1, source_target_pairs={{0,8},{1,9},{2,10},{3,11},{4,12},{5,13},{6,14},{7,15},{8,0},{9,1},... | collective-permute-start | bytes 196616 | tf_op jit(solution)/shard_map/ppermute | solution.py:67
  98.7 0.7 collective-permute-start.15
  99.5 0.0 collective-permute-done.8.refs_1_
  99.5 2.0 %collective-permute-start.16 = (bf16[32,1024]{1,0:T(8,128)(2,1)S(1)}, bf16[32,1024]{1,0:T(8,128)(2,1)S(1)}, u32[]{:S(2)}, u32[]{:S(2)}) collective-permute-start(bf16[32,1024]{1,0:T(8,128)(2,1)S(1)} %get-tuple-element.118), channel_id=1, source_target_pairs={{0,24},{1,25},{2,26},{3,27},{4,28},{5,29},{6,30},{7,31},{8,16},{9,... | collective-permute-start | bytes 196616 | tf_op jit(solution)/shard_map/ppermute | solution.py:67
  101.5 0.7 collective-permute-done.9.refs_2_
  102.2 0.0 collective-permute-done.10.refs_3_
  102.2 0.8 collective-permute-done.14.refs_5_
  103.0 2.8 %collective-permute-done.15.refs_6_ = bf16[32,1024]{1,0:T(8,128)(2,1)S(1)} collective-permute-done((bf16[32,1024]{1,0:T(8,128)(2,1)S(1)}, bf16[32,1024]{1,0:T(8,128)(2,1)S(1)}, u32[]{:S(2)}, u32[]{:S(2)}) %collective-permute-start.15) | collective-permute-done | bytes 65568 | tf_op jit(solution)/shard_map/ppermute | solution.py:67
  105.8 0.0 collective-permute-done.16.refs_7_
  105.8 0.0 copy-done.5
  105.8 1.0 final.1
  (20 shorter events, 0.0 us)
Async XLA Ops:
  3.4 2.5 %collective-permute-start = (f32[1032,128]{1,0:T(8,128)}, f32[1032,128]{1,0:T(8,128)S(1)}, u32[]{:S(2)}, u32[]{:S(2)}) collective-permute-start(f32[1032,128]{1,0:T(8,128)} %get-tuple-element.63), channel_id=1, source_target_pairs={{0,1},{1,0},{2,3},{3,2},{4,5},{5,4},{6,7},{7,6},{8,9},{9,8},{10,11... | collective-permute-start | bytes 1585160 | tf_op jit(solution)/shard_map/ppermute | solution.py:63
  5.9 0.8 copy-start.13
  5.9 35.8 %collective-permute-start.1 = (bf16[2048,512]{1,0:T(8,128)(2,1)}, bf16[2048,512]{1,0:T(8,128)(2,1)}, u32[]{:S(2)}, u32[]{:S(2)}) collective-permute-start(bf16[2048,512]{1,0:T(8,128)(2,1)} %g0), channel_id=1, source_target_pairs={{0,1},{1,0},{2,3},{3,2},{4,5},{5,4},{6,7},{7,6},{8,9},{9,8},{10,11... | collective-permute-start | bytes 6291464 | tf_op jit(solution)/shard_map/ppermute | solution.py:63
  6.1 35.6 %collective-permute-start.2 = (bf16[2048,512]{1,0:T(8,128)(2,1)}, bf16[2048,512]{1,0:T(8,128)(2,1)}, u32[]{:S(2)}, u32[]{:S(2)}) collective-permute-start(bf16[2048,512]{1,0:T(8,128)(2,1)} %u0), channel_id=1, source_target_pairs={{0,1},{1,0},{2,3},{3,2},{4,5},{5,4},{6,7},{7,6},{8,9},{9,8},{10,11... | collective-permute-start | bytes 6291464 | tf_op jit(solution)/shard_map/ppermute | solution.py:63
  6.4 35.3 %collective-permute-start.3 = (bf16[512,2048]{1,0:T(8,128)(2,1)}, bf16[512,2048]{1,0:T(8,128)(2,1)}, u32[]{:S(2)}, u32[]{:S(2)}) collective-permute-start(bf16[512,2048]{1,0:T(8,128)(2,1)} %d0.1), channel_id=1, source_target_pairs={{0,1},{1,0},{2,3},{3,2},{4,5},{5,4},{6,7},{7,6},{8,9},{9,8},{10,11... | collective-permute-start | bytes 6291464 | tf_op jit(solution)/shard_map/ppermute | solution.py:63
  9.0 19.9 %all-to-all-start = ((bf16[16,80,128]{2,1,0:T(8,128)(2,1)}), bf16[16,80,128]{2,1,0:T(8,128)(2,1)S(1)}, u32[]{:S(2)}, u32[]{:S(2)}) async-start(bf16[16,80,128]{2,1,0:T(8,128)(2,1)} %get-tuple-element.68), calls=%async_computation | async-start | bytes 655360 | tf_op jit(solution)/shard_map/all_to_all | solution.py:73
  17.1 24.5 %copy-start.4 = (f32[1032,128]{1,0:T(8,128)S(1)}, f32[1032,128]{1,0:T(8,128)}, u32[]{:S(2)}) copy-start(f32[1032,128]{1,0:T(8,128)} %get-tuple-element.77.first_ref) | copy-start | bytes 1585156
  17.2 26.4 %copy-start.10 = (bf16[256,32]{1,0:T(8,128)(2,1)S(1)}, bf16[256,32]{1,0:T(8,128)(2,1)}, u32[]{:S(2)}) copy-start(bf16[256,32]{1,0:T(8,128)(2,1)} %get-tuple-element.82.disp_ref) | copy-start | bytes 49156
  17.2 26.3 %copy-start.11 = (f32[2048]{0:T(1024)S(1)}, f32[2048]{0:T(1024)}, u32[]{:S(2)}) copy-start(f32[2048]{0:T(1024)} %param.18) | copy-start | bytes 24580
  17.2 26.3 %copy-start.12 = (f32[2048]{0:T(1024)S(1)}, f32[2048]{0:T(1024)}, u32[]{:S(2)}) copy-start(f32[2048]{0:T(1024)} %param.19) | copy-start | bytes 24580
  24.0 19.5 %copy-start.3 = (f32[96,2048]{1,0:T(8,128)S(1)}, f32[96,2048]{1,0:T(8,128)}, u32[]{:S(2)}) copy-start(f32[96,2048]{1,0:T(8,128)} %get-tuple-element.80.near_ref) | copy-start | bytes 2359300
  28.9 16.6 %copy-start = (bf16[16,80,128]{2,1,0:T(8,128)(2,1)}, bf16[16,80,128]{2,1,0:T(8,128)(2,1)S(1)}, u32[]{:S(2)}) copy-start(bf16[16,80,128]{2,1,0:T(8,128)(2,1)S(1)} %all-to-all-done.in_ref) | copy-start | bytes 983044
  41.9 3.6 %copy-start.1 = (bf16[1024,128]{1,0:T(8,128)(2,1)}, bf16[1024,128]{1,0:T(8,128)(2,1)S(1)}, u32[]{:S(2)}) copy-start(bf16[1024,128]{1,0:T(8,128)(2,1)S(1)} %get-tuple-element.85.keep_ref) | copy-start | bytes 786436
  41.9 1.6 %collective-permute-start.4 = (bf16[1024,128]{1,0:T(8,128)(2,1)S(1)}, bf16[1024,128]{1,0:T(8,128)(2,1)S(1)}, u32[]{:S(2)}, u32[]{:S(2)}) collective-permute-start(bf16[1024,128]{1,0:T(8,128)(2,1)S(1)} %get-tuple-element.81), channel_id=1, source_target_pairs={{0,1},{1,0},{2,3},{3,2},{4,5},{5,4},{6,7},{7,6},{8,9},{9,8},{10,11... | collective-permute-start | bytes 786440 | tf_op jit(solution)/shard_map/ppermute | solution.py:63
  43.5 2.0 %copy-start.2 = (bf16[1024,128]{1,0:T(8,128)(2,1)}, bf16[1024,128]{1,0:T(8,128)(2,1)S(1)}, u32[]{:S(2)}) copy-start(bf16[1024,128]{1,0:T(8,128)(2,1)S(1)} %collective-permute-done.4.other_ref) | copy-start | bytes 786436
  43.5 8.7 %copy-start.14 = (s32[256]{0:T(256)S(1)}, s32[256]{0:T(256)}, u32[]{:S(2)}) copy-start(s32[256]{0:T(256)} %param.22) | copy-start | bytes 3076
  45.5 28.3 %all-to-all-start.2 = ((bf16[16,16,2048]{2,1,0:T(8,128)(2,1)}), bf16[16,16,2048]{2,1,0:T(8,128)(2,1)S(1)}, u32[]{:S(2)}, u32[]{:S(2)}) async-start(bf16[16,16,2048]{2,1,0:T(8,128)(2,1)} %bitcast.8), calls=%async_computation.2 | async-start | bytes 2097152 | tf_op jit(solution)/shard_map/all_to_all | solution.py:73
  80.7 8.5 %collective-permute-start.5 = (bf16[64,1024]{1,0:T(8,128)(2,1)S(1)}, bf16[64,1024]{1,0:T(8,128)(2,1)S(1)}, u32[]{:S(2)}, u32[]{:S(2)}) collective-permute-start(bf16[64,1024]{1,0:T(8,128)(2,1)S(1)} %get-tuple-element.103), channel_id=1, source_target_pairs={{0,2},{1,3},{2,0},{3,1},{4,6},{5,7},{6,4},{7,5},{8,10},{9,11},{10,... | collective-permute-start | bytes 393224 | tf_op jit(solution)/shard_map/ppermute | solution.py:67
  81.3 8.9 %collective-permute-start.6 = (bf16[64,1024]{1,0:T(8,128)(2,1)S(1)}, bf16[64,1024]{1,0:T(8,128)(2,1)S(1)}, u32[]{:S(2)}, u32[]{:S(2)}) collective-permute-start(bf16[64,1024]{1,0:T(8,128)(2,1)S(1)} %get-tuple-element.104), channel_id=1, source_target_pairs={{0,4},{1,5},{2,6},{3,7},{4,0},{5,1},{6,2},{7,3},{8,12},{9,13},{10,... | collective-permute-start | bytes 393224 | tf_op jit(solution)/shard_map/ppermute | solution.py:67
  83.3 7.0 %collective-permute-start.7 = (bf16[64,1024]{1,0:T(8,128)(2,1)S(1)}, bf16[64,1024]{1,0:T(8,128)(2,1)S(1)}, u32[]{:S(2)}, u32[]{:S(2)}) collective-permute-start(bf16[64,1024]{1,0:T(8,128)(2,1)S(1)} %get-tuple-element.105), channel_id=1, source_target_pairs={{0,6},{1,7},{2,4},{3,5},{4,2},{5,3},{6,0},{7,1},{8,14},{9,15},{10,... | collective-permute-start | bytes 393224 | tf_op jit(solution)/shard_map/ppermute | solution.py:67
  84.2 6.0 %copy-start.6 = (bf16[128,32]{1,0:T(8,128)(2,1)S(1)}, bf16[128,32]{1,0:T(8,128)(2,1)}, u32[]{:S(2)}) copy-start(bf16[128,32]{1,0:T(8,128)(2,1)} %get-tuple-element.94.refs_0_) | copy-start | bytes 24580
  84.2 6.0 %copy-start.7 = (bf16[128,32]{1,0:T(8,128)(2,1)S(1)}, bf16[128,32]{1,0:T(8,128)(2,1)}, u32[]{:S(2)}) copy-start(bf16[128,32]{1,0:T(8,128)(2,1)} %get-tuple-element.95.refs_1_) | copy-start | bytes 24580
  84.2 6.0 %copy-start.8 = (bf16[128,32]{1,0:T(8,128)(2,1)S(1)}, bf16[128,32]{1,0:T(8,128)(2,1)}, u32[]{:S(2)}) copy-start(bf16[128,32]{1,0:T(8,128)(2,1)} %get-tuple-element.96.refs_2_) | copy-start | bytes 24580
  84.2 6.0 %copy-start.9 = (bf16[128,32]{1,0:T(8,128)(2,1)S(1)}, bf16[128,32]{1,0:T(8,128)(2,1)}, u32[]{:S(2)}) copy-start(bf16[128,32]{1,0:T(8,128)(2,1)} %get-tuple-element.97.refs_3_) | copy-start | bytes 24580
  84.2 21.6 %copy-start.5 = (f32[48,2048]{1,0:T(8,128)S(1)}, f32[48,2048]{1,0:T(8,128)}, u32[]{:S(2)}) copy-start(f32[48,2048]{1,0:T(8,128)} %get-tuple-element.93.near_ref) | copy-start | bytes 1179652
  86.6 8.0 %collective-permute-start.11 = (bf16[64,1024]{1,0:T(8,128)(2,1)S(1)}, bf16[64,1024]{1,0:T(8,128)(2,1)S(1)}, u32[]{:S(2)}, u32[]{:S(2)}) collective-permute-start(bf16[64,1024]{1,0:T(8,128)(2,1)S(1)} %get-tuple-element.112), channel_id=1, source_target_pairs={{0,2},{1,3},{2,0},{3,1},{4,6},{5,7},{6,4},{7,5},{8,10},{9,11},{10,... | collective-permute-start | bytes 393224 | tf_op jit(solution)/shard_map/ppermute | solution.py:67
  87.2 9.5 %collective-permute-start.12 = (bf16[64,1024]{1,0:T(8,128)(2,1)S(1)}, bf16[64,1024]{1,0:T(8,128)(2,1)S(1)}, u32[]{:S(2)}, u32[]{:S(2)}) collective-permute-start(bf16[64,1024]{1,0:T(8,128)(2,1)S(1)} %get-tuple-element.113), channel_id=1, source_target_pairs={{0,4},{1,5},{2,6},{3,7},{4,0},{5,1},{6,2},{7,3},{8,12},{9,13},{10,... | collective-permute-start | bytes 393224 | tf_op jit(solution)/shard_map/ppermute | solution.py:67
  89.2 7.5 %collective-permute-start.13 = (bf16[64,1024]{1,0:T(8,128)(2,1)S(1)}, bf16[64,1024]{1,0:T(8,128)(2,1)S(1)}, u32[]{:S(2)}, u32[]{:S(2)}) collective-permute-start(bf16[64,1024]{1,0:T(8,128)(2,1)S(1)} %get-tuple-element.114), channel_id=1, source_target_pairs={{0,6},{1,7},{2,4},{3,5},{4,2},{5,3},{6,0},{7,1},{8,14},{9,15},{10,... | collective-permute-start | bytes 393224 | tf_op jit(solution)/shard_map/ppermute | solution.py:67
  90.6 8.9 %collective-permute-start.8 = (bf16[32,1024]{1,0:T(8,128)(2,1)S(1)}, bf16[32,1024]{1,0:T(8,128)(2,1)S(1)}, u32[]{:S(2)}, u32[]{:S(2)}) collective-permute-start(bf16[32,1024]{1,0:T(8,128)(2,1)S(1)} %get-tuple-element.107), channel_id=1, source_target_pairs={{0,8},{1,9},{2,10},{3,11},{4,12},{5,13},{6,14},{7,15},{8,0},{9,1},... | collective-permute-start | bytes 196616 | tf_op jit(solution)/shard_map/ppermute | solution.py:67
  93.9 8.3 %collective-permute-start.9 = (bf16[32,1024]{1,0:T(8,128)(2,1)S(1)}, bf16[32,1024]{1,0:T(8,128)(2,1)S(1)}, u32[]{:S(2)}, u32[]{:S(2)}) collective-permute-start(bf16[32,1024]{1,0:T(8,128)(2,1)S(1)} %get-tuple-element.108), channel_id=1, source_target_pairs={{0,16},{1,17},{2,18},{3,19},{4,20},{5,21},{6,22},{7,23},{8,24},{9,... | collective-permute-start | bytes 196616 | tf_op jit(solution)/shard_map/ppermute | solution.py:67
  94.6 7.6 %collective-permute-start.10 = (bf16[32,1024]{1,0:T(8,128)(2,1)S(1)}, bf16[32,1024]{1,0:T(8,128)(2,1)S(1)}, u32[]{:S(2)}, u32[]{:S(2)}) collective-permute-start(bf16[32,1024]{1,0:T(8,128)(2,1)S(1)} %get-tuple-element.109), channel_id=1, source_target_pairs={{0,24},{1,25},{2,26},{3,27},{4,28},{5,29},{6,30},{7,31},{8,16},{9,... | collective-permute-start | bytes 196616 | tf_op jit(solution)/shard_map/ppermute | solution.py:67
  97.0 6.0 %collective-permute-start.14 = (bf16[32,1024]{1,0:T(8,128)(2,1)S(1)}, bf16[32,1024]{1,0:T(8,128)(2,1)S(1)}, u32[]{:S(2)}, u32[]{:S(2)}) collective-permute-start(bf16[32,1024]{1,0:T(8,128)(2,1)S(1)} %get-tuple-element.116), channel_id=1, source_target_pairs={{0,8},{1,9},{2,10},{3,11},{4,12},{5,13},{6,14},{7,15},{8,0},{9,1},... | collective-permute-start | bytes 196616 | tf_op jit(solution)/shard_map/ppermute | solution.py:67
  98.7 7.1 %collective-permute-start.15 = (bf16[32,1024]{1,0:T(8,128)(2,1)S(1)}, bf16[32,1024]{1,0:T(8,128)(2,1)S(1)}, u32[]{:S(2)}, u32[]{:S(2)}) collective-permute-start(bf16[32,1024]{1,0:T(8,128)(2,1)S(1)} %get-tuple-element.117), channel_id=1, source_target_pairs={{0,16},{1,17},{2,18},{3,19},{4,20},{5,21},{6,22},{7,23},{8,24},{9,... | collective-permute-start | bytes 196616 | tf_op jit(solution)/shard_map/ppermute | solution.py:67
  99.5 6.4 %collective-permute-start.16 = (bf16[32,1024]{1,0:T(8,128)(2,1)S(1)}, bf16[32,1024]{1,0:T(8,128)(2,1)S(1)}, u32[]{:S(2)}, u32[]{:S(2)}) collective-permute-start(bf16[32,1024]{1,0:T(8,128)(2,1)S(1)} %get-tuple-element.118), channel_id=1, source_target_pairs={{0,24},{1,25},{2,26},{3,27},{4,28},{5,29},{6,30},{7,31},{8,16},{9,... | collective-permute-start | bytes 196616 | tf_op jit(solution)/shard_map/ppermute | solution.py:67

commit v7 on v6

--- a/solution.py
+++ b/solution.py
@@ -10,6 +10,7 @@
 CAP = 16
 TAIL = 8
 DECAYS = 3
+BANDS = 4
 ATTN_EPS = 1e-05
 NORM_EPS = 1e-06
 PLANES = 4
@@ -214,7 +215,7 @@
     return att * lax.rsqrt(jnp.mean(att * att, axis=-1, keepdims=True) + ATTN_EPS)
 
 
-def rows_kernel(k_ref, near_ref, keep_ref, other_ref, again_ref, fgain_ref, disp_ref, sent_ref, mixed_ref):
+def rows_kernel(k_ref, near_ref, keep_ref, other_ref, again_ref, fgain_ref, disp_ref, sent_hbm, mixed_ref, sent_ref, sems):
     hd = keep_ref.shape[1]
     half = keep_ref.shape[0] // hd
     k = k_ref[0]
@@ -230,7 +231,14 @@
     mixed = mixed_ref[...]
     scale = lax.rsqrt(jnp.mean(mixed * mixed, axis=-1, keepdims=True) + NORM_EPS)
     ffn = (mixed * scale * fgain_ref[...]).astype(BF16)
-    sent_ref[...] = mm(disp_ref[...], ffn).astype(BF16)
+    puts = []
+    band = sent_ref.shape[0] // BANDS
+    for b in range(BANDS):
+        here = pl.ds(b * band, band)
+        sent_ref[here, :] = mm(disp_ref[here, :], ffn).astype(BF16)
+        puts.append(copy(sent_ref.at[here], sent_hbm.at[here], sems, b))
+    for c in puts:
+        c.wait()
 
 
 def mixed_kernel(k_ref, from_ref, lifted_ref, inside_ref, stream_ref, keep_ref, other_ref, again_ref, base_ref, near_ref, mixed_ref):
@@ -562,8 +570,8 @@
         grid=(1,),
         out_shape=sds((slots, width), BF16),
         in_specs=[SMEM] + [full(a) for a in window],
-        out_specs=full(sds((slots, width), BF16)),
-        scratch_shapes=[pltpu.VMEM((resp, width), F32)],
+        out_specs=HBM,
+        scratch_shapes=[pltpu.VMEM((resp, width), F32), pltpu.VMEM((slots, width), BF16), DMA((BANDS,))],
         compiler_params=params(8),
         name="rows",
     )(bit, *window)

time: 107 us -> 107 us (level)
  no operation moved by 1% of the time
where the time goes in v7:
time: 107 us
  Pallas kernels  34.4 us (32%)
  starting transfers between devices  30.9 us (29%)
  waiting for transfers between devices  27.1 us (25%)
  blocking collectives  12.7 us (12%)
    all_to_all x2, waiting for transfers between devices, across_pairs(): return lax.all_to_all(x, BOTH, 0, 0, tiled=True, axis_index_groups=groups)  21.1 us
    ppermute x12, starting transfers between devices, apart(): lax.ppermute(x, BOTH, [(i, i ^ distance) for i in range(lax.axis_size(BOT...  17.6 us
    all_to_all x1, blocking collectives, across_pairs(): return lax.all_to_all(x, BOTH, 0, 0, tiled=True, axis_index_groups=groups)  12.7 us
    all_to_all x2, starting transfers between devices, across_pairs(): return lax.all_to_all(x, BOTH, 0, 0, tiled=True, axis_index_groups=groups)  11.9 us
    pallas_call x1, Pallas kernels, shards(): pl.pallas_call(functools.partial(expert_kernel, count=count, step=step),...  6.87 us
    pallas_call x1, Pallas kernels, shards(): pl.pallas_call(inside_kernel, grid=(2,), out_shape=[sds((tok, width), F32...  6.84 us
    ppermute x12, waiting for transfers between devices, apart(): lax.ppermute(x, BOTH, [(i, i ^ distance) for i in range(lax.axis_size(BOT...  4.45 us
    pallas_call x1, Pallas kernels, shards(): pl.pallas_call(mixed_kernel, grid=(2,), out_shape=[sds((tok, width), BF16...  4.07 us
  transfers between devices with their start and end apart: 19, of which 7 were waited for; matrix products, arithmetic and copies ran while one was open for 1% of the time, Pallas kernels for 20%

profile of v7, /device:TPU:0, one launch (start us, length us, event | category | flops | bytes accessed | tf_op | source)
XLA Modules:
  0.0 106.8 jit_solution(14443264754365349164)
XLA Ops:
  0.0 3.4 %states.1 = (f32[1032,128]{1,0:T(8,128)}, f32[1032,128]{1,0:T(8,128)}) custom-call(s32[1]{0:T(128)} %bitcast.k_ref, bf16[256,2048]{1,0:T(8,128)(2,1)} %key_ref.1, bf16[256,2048]{1,0:T(8,128)(2,1)} %val_ref.1, f32[16,256]{1,0:T(8,128)} %dec_ref.1), custom_call_target="tpu_custom_call" | custom-call | flops 134217728 | bytes 3145728 | tf_op jit(solution)/shard_map/states/pallas_call | solution.py:471
  3.4 0.5 collective-permute-start
  3.9 1.9 %route.1 = (bf16[256,32]{1,0:T(8,128)(2,1)}, bf16[4,16,128]{2,1,0:T(8,128)(2,1)}) custom-call(s32[8,256]{1,0:T(8,128)} %bitcast.17, f32[8,256]{1,0:T(8,128)} %bitcast.18, s32[1,256]{1,0:T(1,128)} %bitcast.15), custom_call_target="tpu_custom_call" | custom-call | flops 134217728 | bytes 1048576 | tf_op jit(solution)/shard_map/route/pallas_call | solution.py:492
  5.9 0.0 collective-permute-done.recv_ref
  5.9 0.2 collective-permute-start.1
  6.1 0.3 collective-permute-start.2
  6.4 0.2 collective-permute-start.3
  6.6 0.1 copy-done.13
  6.7 2.4 %pair.1 = (bf16[16,80,128]{2,1,0:T(8,128)(2,1)}, f32[1032,128]{1,0:T(8,128)}) custom-call(s32[1]{0:T(128)} %bitcast.k_ref, f32[1032,128]{1,0:T(8,128)} %get-tuple-element.62.own_ref, f32[1032,128]{1,0:T(8,128)} %copy-done.13, bf16[4,16,128]{2,1,0:T(8,128)(2,1)} %get-tuple-element.67.notes_ref), custom_call_target="tpu_custom_call" | custom-call | tf_op jit(solution)/shard_map/pair/pallas_call | solution.py:507
  9.0 8.1 %all-to-all-start = ((bf16[16,80,128]{2,1,0:T(8,128)(2,1)}), bf16[16,80,128]{2,1,0:T(8,128)(2,1)S(1)}, u32[]{:S(2)}, u32[]{:S(2)}) async-start(bf16[16,80,128]{2,1,0:T(8,128)(2,1)} %get-tuple-element.68), calls=%async_computation | async-start | bytes 655360 | tf_op jit(solution)/shard_map/all_to_all | solution.py:74
  17.2 0.0 copy-start.11
  17.2 0.0 copy-start.12
  17.2 6.8 %inside.1 = (f32[256,2048]{1,0:T(8,128)}, bf16[256,2048]{1,0:T(8,128)(2,1)}, f32[96,2048]{1,0:T(8,128)}) custom-call(s32[1,256]{1,0:T(1,128)} %bitcast.16, f32[16,256]{1,0:T(8,128)} %dec_ref.1, bf16[256,2048]{1,0:T(8,128)(2,1)} %q_ref.1, bf16[256,2048]{1,0:T(8,128)(2,1)} %key_ref.1, bf16[256,2048]{1,0:T(8,128)(2,1)} %val_ref.1, bf16[256,2048]{1,0:T(8,128)(2,1)} %stream_ref.3), custom_call_target="tpu_custom_call" | custom-call | flops 536870912 | bytes 6291456 | tf_op jit(solution)/shard_map/inside/pallas_call | solution.py:519
  24.0 4.9 %all-to-all-done.in_ref = bf16[16,80,128]{2,1,0:T(8,128)(2,1)S(1)} async-done(((bf16[16,80,128]{2,1,0:T(8,128)(2,1)}), bf16[16,80,128]{2,1,0:T(8,128)(2,1)S(1)}, u32[]{:S(2)}, u32[]{:S(2)}) %all-to-all-start) | async-done | bytes 327712 | tf_op jit(solution)/shard_map/all_to_all | solution.py:74
  28.9 0.1 scan.1
  29.0 12.7 %all_to_all.15 = bf16[16,64,128]{2,1,0:T(8,128)(2,1)S(1)} all-to-all(bf16[16,64,128]{2,1,0:T(8,128)(2,1)S(1)} %scan.1), channel_id=1, replica_groups={{0,2,4,6,8,10,12,14,16,18,20,22,24,26,28,30},{1,3,5,7,9,11,13,15,17,19,..., dimensions={0} | all-to-all | bytes 524288 | tf_op jit(solution)/shard_map/all_to_all | solution.py:74
  41.7 0.0 collective-permute-done.1.g1
  41.7 0.0 collective-permute-done.2.u1
  41.7 0.0 collective-permute-done.3.d1
  41.7 0.0 copy-done.4
  41.7 0.2 split.1
  41.9 0.1 collective-permute-start.4
  42.0 1.5 %collective-permute-done.4.other_ref = bf16[1024,128]{1,0:T(8,128)(2,1)S(1)} collective-permute-done((bf16[1024,128]{1,0:T(8,128)(2,1)S(1)}, bf16[1024,128]{1,0:T(8,128)(2,1)S(1)}, u32[]{:S(2)}, u32[]{:S(2)}) %collective-permute-start.4) | collective-permute-done | bytes 262176 | tf_op jit(solution)/shard_map/ppermute | solution.py:64
  43.5 0.0 copy-done.10
  43.5 0.0 copy-start.14
  43.5 1.8 %rows.1 = bf16[256,2048]{1,0:T(8,128)(2,1)} custom-call(s32[1]{0:T(128)} %bitcast.k_ref, f32[96,2048]{1,0:T(8,128)S(1)} %copy-done.3, bf16[1024,128]{1,0:T(8,128)(2,1)S(1)} %get-tuple-element.85.keep_ref, bf16[1024,128]{1,0:T(8,128)(2,1)S(1)} %collective-permute-done.4.other_ref, f32[1,2048]{1,0:T(1,128)S(1)} %bitcast.13, f32[1,2048]{1,0:T(1,128)S(1)} %bitcast.14, ...), custom_call_target="tpu_custom_call" | custom-call | tf_op jit(solution)/shard_map/rows/pallas_call | solution.py:568
  45.4 0.0 copy-done
  45.4 0.0 copy-done.1
  45.4 0.0 copy-done.2
  45.4 3.8 %all-to-all-start.2 = ((bf16[16,16,2048]{2,1,0:T(8,128)(2,1)}), bf16[16,16,2048]{2,1,0:T(8,128)(2,1)S(1)}, u32[]{:S(2)}, u32[]{:S(2)}) async-start(bf16[16,16,2048]{2,1,0:T(8,128)(2,1)} %bitcast.8), calls=%async_computation.2 | async-start | bytes 2097152 | tf_op jit(solution)/shard_map/all_to_all | solution.py:74
  49.2 2.8 %plan.1 = (bf16[128,32]{1,0:T(8,128)(2,1)}, bf16[128,32]{1,0:T(8,128)(2,1)}, bf16[128,32]{1,0:T(8,128)(2,1)}, bf16[128,32]{1,0:T(8,128)(2,1)}) custom-call(s32[1]{0:T(128)} %bitcast.9.at_ref, s32[1]{0:T(128)} %bitcast.10.plane_ref, bf16[16,80,128]{2,1,0:T(8,128)(2,1)} %copy-done), custom_call_target="tpu_custom_call" | custom-call | flops 16777216 | bytes 1048576 | tf_op jit(solution)/shard_map/plan/pallas_call | solution.py:534
  52.1 0.6 fusion
  53.4 4.1 %mixed.1 = (bf16[256,2048]{1,0:T(8,128)(2,1)}, f32[48,2048]{1,0:T(8,128)}) custom-call(s32[1]{0:T(128)} %bitcast.k_ref, s32[1]{0:T(128)S(6)} %min.7.from_ref, bf16[256,2048]{1,0:T(8,128)(2,1)} %get-tuple-element.83.lifted_ref, f32[256,2048]{1,0:T(8,128)} %get-tuple-element.84.inside_ref, bf16[256,2048]{1,0:T(8,128)(2,1)} %stream_ref.3, ...), custom_call_target="tpu_custom_call" | custom-call | flops 134217728 | bytes 7340032 | tf_op jit(solution)/shard_map/mixed/pallas_call | solution.py:588
  57.4 16.2 %all-to-all-done.2.x_hbm = bf16[16,16,2048]{2,1,0:T(8,128)(2,1)S(1)} async-done(((bf16[16,16,2048]{2,1,0:T(8,128)(2,1)}), bf16[16,16,2048]{2,1,0:T(8,128)(2,1)S(1)}, u32[]{:S(2)}, u32[]{:S(2)}) %all-to-all-start.2) | async-done | bytes 1048608 | tf_op jit(solution)/shard_map/all_to_all | solution.py:74
  73.6 6.9 %expert.1 = (bf16[64,1024]{1,0:T(8,128)(2,1)S(1)}, bf16[64,1024]{1,0:T(8,128)(2,1)S(1)}, bf16[64,1024]{1,0:T(8,128)(2,1)S(1)}, bf16[64,1024]{1,0:T(8,128)(2,1)S(1)}, bf16[2,256,512]{2,1,0:T(8,128)(2,1)S(1)}) custom-call(s32[1]{0:T(128)} %bitcast.9.at_ref, s32[1]{0:T(128)} %bitcast.10.plane_ref, bf16[16,16,2048]{2,1,0:T(8,128)(2,1)S(1)} %all-to-all-done.2.x_hbm, ...), custom_call_target="tpu_custom_call" | custom-call | flops 2684354560 | bytes 12582912 | tf_op jit(solution)/shard_map/expert/pallas_call | solution.py:607
  80.5 0.6 collective-permute-start.5
  81.1 2.0 %collective-permute-start.6 = (bf16[64,1024]{1,0:T(8,128)(2,1)S(1)}, bf16[64,1024]{1,0:T(8,128)(2,1)S(1)}, u32[]{:S(2)}, u32[]{:S(2)}) collective-permute-start(bf16[64,1024]{1,0:T(8,128)(2,1)S(1)} %get-tuple-element.104), channel_id=1, source_target_pairs={{0,4},{1,5},{2,6},{3,7},{4,0},{5,1},{6,2},{7,3},{8,12},{9,13},{10,... | collective-permute-start | bytes 393224 | tf_op jit(solution)/shard_map/ppermute | solution.py:68
  83.1 1.0 collective-permute-start.7
  84.1 2.3 %down.1 = (bf16[64,1024]{1,0:T(8,128)(2,1)S(1)}, bf16[64,1024]{1,0:T(8,128)(2,1)S(1)}, bf16[64,1024]{1,0:T(8,128)(2,1)S(1)}, bf16[64,1024]{1,0:T(8,128)(2,1)S(1)}) custom-call(bf16[2,256,512]{2,1,0:T(8,128)(2,1)S(1)} %get-tuple-element.110.hid_ref, bf16[512,2048]{1,0:T(8,128)(2,1)} %d0.1, bf16[512,2048]{1,0:T(8,128)(2,1)} %collective-permute-done.3.d1), custom_call_target="tpu_custom_call" | custom-call | flops 536870912 | bytes 2097152 | tf_op jit(solution)/shard_map/down/pallas_call | solution.py:623
  86.4 0.6 collective-permute-start.11
  87.1 2.0 %collective-permute-start.12 = (bf16[64,1024]{1,0:T(8,128)(2,1)S(1)}, bf16[64,1024]{1,0:T(8,128)(2,1)S(1)}, u32[]{:S(2)}, u32[]{:S(2)}) collective-permute-start(bf16[64,1024]{1,0:T(8,128)(2,1)S(1)} %get-tuple-element.113), channel_id=1, source_target_pairs={{0,4},{1,5},{2,6},{3,7},{4,0},{5,1},{6,2},{7,3},{8,12},{9,13},{10,... | collective-permute-start | bytes 393224 | tf_op jit(solution)/shard_map/ppermute | solution.py:68
  89.0 0.0 collective-permute-done.5.refs_5_
  89.0 1.0 collective-permute-start.13
  90.0 0.0 collective-permute-done.6.refs_6_
  90.0 0.1 collective-permute-done.7.refs_7_
  90.1 0.0 copy-done.6
  90.1 0.3 combine.2
  90.5 3.3 %collective-permute-start.8 = (bf16[32,1024]{1,0:T(8,128)(2,1)S(1)}, bf16[32,1024]{1,0:T(8,128)(2,1)S(1)}, u32[]{:S(2)}, u32[]{:S(2)}) collective-permute-start(bf16[32,1024]{1,0:T(8,128)(2,1)S(1)} %get-tuple-element.107), channel_id=1, source_target_pairs={{0,8},{1,9},{2,10},{3,11},{4,12},{5,13},{6,14},{7,15},{8,0},{9,1},... | collective-permute-start | bytes 196616 | tf_op jit(solution)/shard_map/ppermute | solution.py:68
  93.8 0.7 collective-permute-start.9
  94.4 0.0 collective-permute-done.11.refs_5_
  94.4 2.1 %collective-permute-start.10 = (bf16[32,1024]{1,0:T(8,128)(2,1)S(1)}, bf16[32,1024]{1,0:T(8,128)(2,1)S(1)}, u32[]{:S(2)}, u32[]{:S(2)}) collective-permute-start(bf16[32,1024]{1,0:T(8,128)(2,1)S(1)} %get-tuple-element.109), channel_id=1, source_target_pairs={{0,24},{1,25},{2,26},{3,27},{4,28},{5,29},{6,30},{7,31},{8,16},{9,... | collective-permute-start | bytes 196616 | tf_op jit(solution)/shard_map/ppermute | solution.py:68
  96.5 0.0 collective-permute-done.12.refs_6_
  96.5 0.0 collective-permute-done.13.refs_7_
  96.5 0.3 combine.3
  96.9 1.7 %collective-permute-start.14 = (bf16[32,1024]{1,0:T(8,128)(2,1)S(1)}, bf16[32,1024]{1,0:T(8,128)(2,1)S(1)}, u32[]{:S(2)}, u32[]{:S(2)}) collective-permute-start(bf16[32,1024]{1,0:T(8,128)(2,1)S(1)} %get-tuple-element.116), channel_id=1, source_target_pairs={{0,8},{1,9},{2,10},{3,11},{4,12},{5,13},{6,14},{7,15},{8,0},{9,1},... | collective-permute-start | bytes 196616 | tf_op jit(solution)/shard_map/ppermute | solution.py:68
  98.6 0.7 collective-permute-start.15
  99.3 0.0 collective-permute-done.8.refs_1_
  99.3 2.0 %collective-permute-start.16 = (bf16[32,1024]{1,0:T(8,128)(2,1)S(1)}, bf16[32,1024]{1,0:T(8,128)(2,1)S(1)}, u32[]{:S(2)}, u32[]{:S(2)}) collective-permute-start(bf16[32,1024]{1,0:T(8,128)(2,1)S(1)} %get-tuple-element.118), channel_id=1, source_target_pairs={{0,24},{1,25},{2,26},{3,27},{4,28},{5,29},{6,30},{7,31},{8,16},{9,... | collective-permute-start | bytes 196616 | tf_op jit(solution)/shard_map/ppermute | solution.py:68
  101.3 0.7 collective-permute-done.9.refs_2_
  102.1 0.0 collective-permute-done.10.refs_3_
  102.1 0.8 collective-permute-done.14.refs_5_
  102.9 2.8 %collective-permute-done.15.refs_6_ = bf16[32,1024]{1,0:T(8,128)(2,1)S(1)} collective-permute-done((bf16[32,1024]{1,0:T(8,128)(2,1)S(1)}, bf16[32,1024]{1,0:T(8,128)(2,1)S(1)}, u32[]{:S(2)}, u32[]{:S(2)}) %collective-permute-start.15) | collective-permute-done | bytes 65568 | tf_op jit(solution)/shard_map/ppermute | solution.py:68
  105.7 0.0 collective-permute-done.16.refs_7_
  105.7 1.0 final.1
  (20 shorter events, 0.0 us)
Async XLA Ops:
  3.4 2.5 %collective-permute-start = (f32[1032,128]{1,0:T(8,128)}, f32[1032,128]{1,0:T(8,128)S(1)}, u32[]{:S(2)}, u32[]{:S(2)}) collective-permute-start(f32[1032,128]{1,0:T(8,128)} %get-tuple-element.63), channel_id=1, source_target_pairs={{0,1},{1,0},{2,3},{3,2},{4,5},{5,4},{6,7},{7,6},{8,9},{9,8},{10,11... | collective-permute-start | bytes 1585160 | tf_op jit(solution)/shard_map/ppermute | solution.py:64
  5.9 0.8 copy-start.13
  5.9 35.8 %collective-permute-start.1 = (bf16[2048,512]{1,0:T(8,128)(2,1)}, bf16[2048,512]{1,0:T(8,128)(2,1)}, u32[]{:S(2)}, u32[]{:S(2)}) collective-permute-start(bf16[2048,512]{1,0:T(8,128)(2,1)} %g0), channel_id=1, source_target_pairs={{0,1},{1,0},{2,3},{3,2},{4,5},{5,4},{6,7},{7,6},{8,9},{9,8},{10,11... | collective-permute-start | bytes 6291464 | tf_op jit(solution)/shard_map/ppermute | solution.py:64
  6.1 35.6 %collective-permute-start.2 = (bf16[2048,512]{1,0:T(8,128)(2,1)}, bf16[2048,512]{1,0:T(8,128)(2,1)}, u32[]{:S(2)}, u32[]{:S(2)}) collective-permute-start(bf16[2048,512]{1,0:T(8,128)(2,1)} %u0), channel_id=1, source_target_pairs={{0,1},{1,0},{2,3},{3,2},{4,5},{5,4},{6,7},{7,6},{8,9},{9,8},{10,11... | collective-permute-start | bytes 6291464 | tf_op jit(solution)/shard_map/ppermute | solution.py:64
  6.4 35.3 %collective-permute-start.3 = (bf16[512,2048]{1,0:T(8,128)(2,1)}, bf16[512,2048]{1,0:T(8,128)(2,1)}, u32[]{:S(2)}, u32[]{:S(2)}) collective-permute-start(bf16[512,2048]{1,0:T(8,128)(2,1)} %d0.1), channel_id=1, source_target_pairs={{0,1},{1,0},{2,3},{3,2},{4,5},{5,4},{6,7},{7,6},{8,9},{9,8},{10,11... | collective-permute-start | bytes 6291464 | tf_op jit(solution)/shard_map/ppermute | solution.py:64
  9.0 19.9 %all-to-all-start = ((bf16[16,80,128]{2,1,0:T(8,128)(2,1)}), bf16[16,80,128]{2,1,0:T(8,128)(2,1)S(1)}, u32[]{:S(2)}, u32[]{:S(2)}) async-start(bf16[16,80,128]{2,1,0:T(8,128)(2,1)} %get-tuple-element.68), calls=%async_computation | async-start | bytes 655360 | tf_op jit(solution)/shard_map/all_to_all | solution.py:74
  17.1 24.5 %copy-start.4 = (f32[1032,128]{1,0:T(8,128)S(1)}, f32[1032,128]{1,0:T(8,128)}, u32[]{:S(2)}) copy-start(f32[1032,128]{1,0:T(8,128)} %get-tuple-element.77.first_ref) | copy-start | bytes 1585156
  17.2 26.4 %copy-start.10 = (bf16[256,32]{1,0:T(8,128)(2,1)S(1)}, bf16[256,32]{1,0:T(8,128)(2,1)}, u32[]{:S(2)}) copy-start(bf16[256,32]{1,0:T(8,128)(2,1)} %get-tuple-element.82.disp_ref) | copy-start | bytes 49156
  17.2 26.3 %copy-start.11 = (f32[2048]{0:T(1024)S(1)}, f32[2048]{0:T(1024)}, u32[]{:S(2)}) copy-start(f32[2048]{0:T(1024)} %param.18) | copy-start | bytes 24580
  17.2 26.3 %copy-start.12 = (f32[2048]{0:T(1024)S(1)}, f32[2048]{0:T(1024)}, u32[]{:S(2)}) copy-start(f32[2048]{0:T(1024)} %param.19) | copy-start | bytes 24580
  24.0 19.5 %copy-start.3 = (f32[96,2048]{1,0:T(8,128)S(1)}, f32[96,2048]{1,0:T(8,128)}, u32[]{:S(2)}) copy-start(f32[96,2048]{1,0:T(8,128)} %get-tuple-element.80.near_ref) | copy-start | bytes 2359300
  28.9 16.5 %copy-start = (bf16[16,80,128]{2,1,0:T(8,128)(2,1)}, bf16[16,80,128]{2,1,0:T(8,128)(2,1)S(1)}, u32[]{:S(2)}) copy-start(bf16[16,80,128]{2,1,0:T(8,128)(2,1)S(1)} %all-to-all-done.in_ref) | copy-start | bytes 983044
  41.9 3.5 %copy-start.1 = (bf16[1024,128]{1,0:T(8,128)(2,1)}, bf16[1024,128]{1,0:T(8,128)(2,1)S(1)}, u32[]{:S(2)}) copy-start(bf16[1024,128]{1,0:T(8,128)(2,1)S(1)} %get-tuple-element.85.keep_ref) | copy-start | bytes 786436
  41.9 1.6 %collective-permute-start.4 = (bf16[1024,128]{1,0:T(8,128)(2,1)S(1)}, bf16[1024,128]{1,0:T(8,128)(2,1)S(1)}, u32[]{:S(2)}, u32[]{:S(2)}) collective-permute-start(bf16[1024,128]{1,0:T(8,128)(2,1)S(1)} %get-tuple-element.81), channel_id=1, source_target_pairs={{0,1},{1,0},{2,3},{3,2},{4,5},{5,4},{6,7},{7,6},{8,9},{9,8},{10,11... | collective-permute-start | bytes 786440 | tf_op jit(solution)/shard_map/ppermute | solution.py:64
  43.5 1.9 %copy-start.2 = (bf16[1024,128]{1,0:T(8,128)(2,1)}, bf16[1024,128]{1,0:T(8,128)(2,1)S(1)}, u32[]{:S(2)}) copy-start(bf16[1024,128]{1,0:T(8,128)(2,1)S(1)} %collective-permute-done.4.other_ref) | copy-start | bytes 786436
  43.5 8.6 %copy-start.14 = (s32[256]{0:T(256)S(1)}, s32[256]{0:T(256)}, u32[]{:S(2)}) copy-start(s32[256]{0:T(256)} %param.22) | copy-start | bytes 3076
  45.4 28.3 %all-to-all-start.2 = ((bf16[16,16,2048]{2,1,0:T(8,128)(2,1)}), bf16[16,16,2048]{2,1,0:T(8,128)(2,1)S(1)}, u32[]{:S(2)}, u32[]{:S(2)}) async-start(bf16[16,16,2048]{2,1,0:T(8,128)(2,1)} %bitcast.8), calls=%async_computation.2 | async-start | bytes 2097152 | tf_op jit(solution)/shard_map/all_to_all | solution.py:74
  80.5 8.5 %collective-permute-start.5 = (bf16[64,1024]{1,0:T(8,128)(2,1)S(1)}, bf16[64,1024]{1,0:T(8,128)(2,1)S(1)}, u32[]{:S(2)}, u32[]{:S(2)}) collective-permute-start(bf16[64,1024]{1,0:T(8,128)(2,1)S(1)} %get-tuple-element.103), channel_id=1, source_target_pairs={{0,2},{1,3},{2,0},{3,1},{4,6},{5,7},{6,4},{7,5},{8,10},{9,11},{10,... | collective-permute-start | bytes 393224 | tf_op jit(solution)/shard_map/ppermute | solution.py:68
  81.1 8.9 %collective-permute-start.6 = (bf16[64,1024]{1,0:T(8,128)(2,1)S(1)}, bf16[64,1024]{1,0:T(8,128)(2,1)S(1)}, u32[]{:S(2)}, u32[]{:S(2)}) collective-permute-start(bf16[64,1024]{1,0:T(8,128)(2,1)S(1)} %get-tuple-element.104), channel_id=1, source_target_pairs={{0,4},{1,5},{2,6},{3,7},{4,0},{5,1},{6,2},{7,3},{8,12},{9,13},{10,... | collective-permute-start | bytes 393224 | tf_op jit(solution)/shard_map/ppermute | solution.py:68
  83.1 7.0 %collective-permute-start.7 = (bf16[64,1024]{1,0:T(8,128)(2,1)S(1)}, bf16[64,1024]{1,0:T(8,128)(2,1)S(1)}, u32[]{:S(2)}, u32[]{:S(2)}) collective-permute-start(bf16[64,1024]{1,0:T(8,128)(2,1)S(1)} %get-tuple-element.105), channel_id=1, source_target_pairs={{0,6},{1,7},{2,4},{3,5},{4,2},{5,3},{6,0},{7,1},{8,14},{9,15},{10,... | collective-permute-start | bytes 393224 | tf_op jit(solution)/shard_map/ppermute | solution.py:68
  84.1 6.0 %copy-start.6 = (bf16[128,32]{1,0:T(8,128)(2,1)S(1)}, bf16[128,32]{1,0:T(8,128)(2,1)}, u32[]{:S(2)}) copy-start(bf16[128,32]{1,0:T(8,128)(2,1)} %get-tuple-element.94.refs_0_) | copy-start | bytes 24580
  84.1 6.0 %copy-start.7 = (bf16[128,32]{1,0:T(8,128)(2,1)S(1)}, bf16[128,32]{1,0:T(8,128)(2,1)}, u32[]{:S(2)}) copy-start(bf16[128,32]{1,0:T(8,128)(2,1)} %get-tuple-element.95.refs_1_) | copy-start | bytes 24580
  84.1 6.0 %copy-start.8 = (bf16[128,32]{1,0:T(8,128)(2,1)S(1)}, bf16[128,32]{1,0:T(8,128)(2,1)}, u32[]{:S(2)}) copy-start(bf16[128,32]{1,0:T(8,128)(2,1)} %get-tuple-element.96.refs_2_) | copy-start | bytes 24580
  84.1 6.0 %copy-start.9 = (bf16[128,32]{1,0:T(8,128)(2,1)S(1)}, bf16[128,32]{1,0:T(8,128)(2,1)}, u32[]{:S(2)}) copy-start(bf16[128,32]{1,0:T(8,128)(2,1)} %get-tuple-element.97.refs_3_) | copy-start | bytes 24580
  84.1 21.6 %copy-start.5 = (f32[48,2048]{1,0:T(8,128)S(1)}, f32[48,2048]{1,0:T(8,128)}, u32[]{:S(2)}) copy-start(f32[48,2048]{1,0:T(8,128)} %get-tuple-element.93.near_ref) | copy-start | bytes 1179652
  86.4 8.0 %collective-permute-start.11 = (bf16[64,1024]{1,0:T(8,128)(2,1)S(1)}, bf16[64,1024]{1,0:T(8,128)(2,1)S(1)}, u32[]{:S(2)}, u32[]{:S(2)}) collective-permute-start(bf16[64,1024]{1,0:T(8,128)(2,1)S(1)} %get-tuple-element.112), channel_id=1, source_target_pairs={{0,2},{1,3},{2,0},{3,1},{4,6},{5,7},{6,4},{7,5},{8,10},{9,11},{10,... | collective-permute-start | bytes 393224 | tf_op jit(solution)/shard_map/ppermute | solution.py:68
  87.1 9.5 %collective-permute-start.12 = (bf16[64,1024]{1,0:T(8,128)(2,1)S(1)}, bf16[64,1024]{1,0:T(8,128)(2,1)S(1)}, u32[]{:S(2)}, u32[]{:S(2)}) collective-permute-start(bf16[64,1024]{1,0:T(8,128)(2,1)S(1)} %get-tuple-element.113), channel_id=1, source_target_pairs={{0,4},{1,5},{2,6},{3,7},{4,0},{5,1},{6,2},{7,3},{8,12},{9,13},{10,... | collective-permute-start | bytes 393224 | tf_op jit(solution)/shard_map/ppermute | solution.py:68
  89.0 7.5 %collective-permute-start.13 = (bf16[64,1024]{1,0:T(8,128)(2,1)S(1)}, bf16[64,1024]{1,0:T(8,128)(2,1)S(1)}, u32[]{:S(2)}, u32[]{:S(2)}) collective-permute-start(bf16[64,1024]{1,0:T(8,128)(2,1)S(1)} %get-tuple-element.114), channel_id=1, source_target_pairs={{0,6},{1,7},{2,4},{3,5},{4,2},{5,3},{6,0},{7,1},{8,14},{9,15},{10,... | collective-permute-start | bytes 393224 | tf_op jit(solution)/shard_map/ppermute | solution.py:68
  90.5 8.9 %collective-permute-start.8 = (bf16[32,1024]{1,0:T(8,128)(2,1)S(1)}, bf16[32,1024]{1,0:T(8,128)(2,1)S(1)}, u32[]{:S(2)}, u32[]{:S(2)}) collective-permute-start(bf16[32,1024]{1,0:T(8,128)(2,1)S(1)} %get-tuple-element.107), channel_id=1, source_target_pairs={{0,8},{1,9},{2,10},{3,11},{4,12},{5,13},{6,14},{7,15},{8,0},{9,1},... | collective-permute-start | bytes 196616 | tf_op jit(solution)/shard_map/ppermute | solution.py:68
  93.8 8.3 %collective-permute-start.9 = (bf16[32,1024]{1,0:T(8,128)(2,1)S(1)}, bf16[32,1024]{1,0:T(8,128)(2,1)S(1)}, u32[]{:S(2)}, u32[]{:S(2)}) collective-permute-start(bf16[32,1024]{1,0:T(8,128)(2,1)S(1)} %get-tuple-element.108), channel_id=1, source_target_pairs={{0,16},{1,17},{2,18},{3,19},{4,20},{5,21},{6,22},{7,23},{8,24},{9,... | collective-permute-start | bytes 196616 | tf_op jit(solution)/shard_map/ppermute | solution.py:68
  94.4 7.7 %collective-permute-start.10 = (bf16[32,1024]{1,0:T(8,128)(2,1)S(1)}, bf16[32,1024]{1,0:T(8,128)(2,1)S(1)}, u32[]{:S(2)}, u32[]{:S(2)}) collective-permute-start(bf16[32,1024]{1,0:T(8,128)(2,1)S(1)} %get-tuple-element.109), channel_id=1, source_target_pairs={{0,24},{1,25},{2,26},{3,27},{4,28},{5,29},{6,30},{7,31},{8,16},{9,... | collective-permute-start | bytes 196616 | tf_op jit(solution)/shard_map/ppermute | solution.py:68
  96.9 6.0 %collective-permute-start.14 = (bf16[32,1024]{1,0:T(8,128)(2,1)S(1)}, bf16[32,1024]{1,0:T(8,128)(2,1)S(1)}, u32[]{:S(2)}, u32[]{:S(2)}) collective-permute-start(bf16[32,1024]{1,0:T(8,128)(2,1)S(1)} %get-tuple-element.116), channel_id=1, source_target_pairs={{0,8},{1,9},{2,10},{3,11},{4,12},{5,13},{6,14},{7,15},{8,0},{9,1},... | collective-permute-start | bytes 196616 | tf_op jit(solution)/shard_map/ppermute | solution.py:68
  98.6 7.1 %collective-permute-start.15 = (bf16[32,1024]{1,0:T(8,128)(2,1)S(1)}, bf16[32,1024]{1,0:T(8,128)(2,1)S(1)}, u32[]{:S(2)}, u32[]{:S(2)}) collective-permute-start(bf16[32,1024]{1,0:T(8,128)(2,1)S(1)} %get-tuple-element.117), channel_id=1, source_target_pairs={{0,16},{1,17},{2,18},{3,19},{4,20},{5,21},{6,22},{7,23},{8,24},{9,... | collective-permute-start | bytes 196616 | tf_op jit(solution)/shard_map/ppermute | solution.py:68
  99.3 6.4 %collective-permute-start.16 = (bf16[32,1024]{1,0:T(8,128)(2,1)S(1)}, bf16[32,1024]{1,0:T(8,128)(2,1)S(1)}, u32[]{:S(2)}, u32[]{:S(2)}) collective-permute-start(bf16[32,1024]{1,0:T(8,128)(2,1)S(1)} %get-tuple-element.118), channel_id=1, source_target_pairs={{0,24},{1,25},{2,26},{3,27},{4,28},{5,29},{6,30},{7,31},{8,16},{9,... | collective-permute-start | bytes 196616 | tf_op jit(solution)/shard_map/ppermute | solution.py:68

commit v8 on v6

--- a/solution.py
+++ b/solution.py
@@ -214,19 +214,27 @@
     return att * lax.rsqrt(jnp.mean(att * att, axis=-1, keepdims=True) + ATTN_EPS)
 
 
-def rows_kernel(k_ref, near_ref, keep_ref, other_ref, again_ref, fgain_ref, disp_ref, sent_ref, mixed_ref):
-    hd = keep_ref.shape[1]
-    half = keep_ref.shape[0] // hd
+def half_rows(first, near_ref, state_ref, again_ref, mixed_ref, base):
+    hd = state_ref.shape[1]
+    resp = near_ref.shape[0] // 3
+    for j in range(state_ref.shape[0] // hd):
+        cols = pl.ds(pl.multiple_of(first + j * hd, hd), hd)
+        lifted = near_ref[resp : 2 * resp, cols].astype(BF16)
+        att = near_ref[:resp, cols] + mm(lifted, state_ref[j * hd : (j + 1) * hd, :], 1, 1)
+        here = pl.ds(pl.multiple_of(base + j * hd, hd), hd)
+        mixed_ref[:, here] = near_ref[2 * resp :, cols] + head_norm(att) * again_ref[:, cols]
+
+
+def mine_kernel(k_ref, near_ref, keep_ref, again_ref, mixed_ref):
+    half_rows(k_ref[0] * keep_ref.shape[0], near_ref, keep_ref, again_ref, mixed_ref, 0)
+
+
+def rows_kernel(k_ref, near_ref, mine_ref, other_ref, again_ref, fgain_ref, disp_ref, sent_ref, mixed_ref):
+    span = other_ref.shape[0]
     k = k_ref[0]
-    resp = near_ref.shape[0] // 3
-    for r in range(2 * half):
-        side = r // half
-        off = pl.multiple_of((side ^ k) * (half * hd) + (r % half) * hd, hd)
-        cols = pl.ds(off, hd)
-        src = keep_ref if side == 0 else other_ref
-        lifted = near_ref[resp : 2 * resp, cols].astype(BF16)
-        att = near_ref[:resp, cols] + mm(lifted, src[(r % half) * hd : (r % half + 1) * hd, :], 1, 1)
-        mixed_ref[:, cols] = near_ref[2 * resp :, cols] + head_norm(att) * again_ref[:, cols]
+    other = pl.multiple_of((1 - k) * span, span)
+    half_rows(other, near_ref, other_ref, again_ref, mixed_ref, other)
+    mixed_ref[:, pl.ds(pl.multiple_of(k * span, span), span)] = mine_ref[...]
     mixed = mixed_ref[...]
     scale = lax.rsqrt(jnp.mean(mixed * mixed, axis=-1, keepdims=True) + NORM_EPS)
     ffn = (mixed * scale * fgain_ref[...]).astype(BF16)
@@ -529,7 +537,7 @@
         out_shape=[table] * planes,
         in_specs=[SMEM, SMEM, full(gathered)],
         out_specs=[full(table)] * planes,
-        compiler_params=params(),
+        compiler_params=params(8),
         cost_estimate=cost(1 << 24, 1 << 20),
         name="plan",
     )(at, plane, gathered)
@@ -556,7 +564,18 @@
     other = partner(give)
 
     again = attn_gain.reshape(1, width)
-    window = (nearby, keep, other, again, ffn_gain.reshape(1, width), disp)
+    first_half = (nearby, keep, again)
+    mine = pl.pallas_call(
+        mine_kernel,
+        grid=(1,),
+        out_shape=sds((resp, width // 2), F32),
+        in_specs=[SMEM] + [full(a) for a in first_half],
+        out_specs=full(sds((resp, width // 2), F32)),
+        compiler_params=params(8),
+        cost_estimate=cost(2 * resp * width * hd, 1 << 20),
+        name="mine",
+    )(bit, *first_half)
+    window = (nearby, mine, other, again, ffn_gain.reshape(1, width), disp)
     sent = pl.pallas_call(
         rows_kernel,
         grid=(1,),

time: 107 us -> 107 us (level)
  waiting for transfers between devices: 27 us -> 28.4 us
  Pallas kernels: 34.5 us -> 33.2 us
    all_to_all x2, waiting for transfers between devices: 21.1 us -> 22.7 us  [across_pairs(): return lax.all_to_all(x, BOTH, 0, 0, tiled=True, axis_index_groups=groups)]
    pallas_call x1, Pallas kernels: 2.83 us -> 1.25 us  [shards(): pl.pallas_call(functools.partial(plan_kernel, planes=planes, rows=rows),...]
  transfers between devices with their start and end apart: 19 -> 19, of which waited for: 7 -> 7; matrix products, arithmetic and copies ran while one was open for 1% -> 1% of each run, Pallas kernels for 20% -> 19%
where the time goes in v8:
time: 107 us
  Pallas kernels  33.2 us (31%)
  starting transfers between devices  30.8 us (29%)
  waiting for transfers between devices  28.4 us (27%)
  blocking collectives  12.7 us (12%)
    all_to_all x2, waiting for transfers between devices, across_pairs(): return lax.all_to_all(x, BOTH, 0, 0, tiled=True, axis_index_groups=groups)  22.7 us
    ppermute x12, starting transfers between devices, apart(): lax.ppermute(x, BOTH, [(i, i ^ distance) for i in range(lax.axis_size(BOT...  17.6 us
    all_to_all x1, blocking collectives, across_pairs(): return lax.all_to_all(x, BOTH, 0, 0, tiled=True, axis_index_groups=groups)  12.7 us
    all_to_all x2, starting transfers between devices, across_pairs(): return lax.all_to_all(x, BOTH, 0, 0, tiled=True, axis_index_groups=groups)  11.9 us
    pallas_call x1, Pallas kernels, shards(): pl.pallas_call(functools.partial(expert_kernel, count=count, step=step),...  6.87 us
    pallas_call x1, Pallas kernels, shards(): pl.pallas_call(inside_kernel, grid=(2,), out_shape=[sds((tok, width), F32...  6.84 us
    ppermute x12, waiting for transfers between devices, apart(): lax.ppermute(x, BOTH, [(i, i ^ distance) for i in range(lax.axis_size(BOT...  4.51 us
    pallas_call x1, Pallas kernels, shards(): pl.pallas_call(mixed_kernel, grid=(2,), out_shape=[sds((tok, width), BF16...  4.05 us
  transfers between devices with their start and end apart: 19, of which 7 were waited for; matrix products, arithmetic and copies ran while one was open for 1% of the time, Pallas kernels for 19%

profile of v8, /device:TPU:0, one launch (start us, length us, event | category | flops | bytes accessed | tf_op | source)
XLA Modules:
  0.0 106.8 jit_solution(12568170473791776330)
XLA Ops:
  0.0 3.4 %states.1 = (f32[1032,128]{1,0:T(8,128)}, f32[1032,128]{1,0:T(8,128)}) custom-call(s32[1]{0:T(128)} %bitcast.k_ref, bf16[256,2048]{1,0:T(8,128)(2,1)} %key_ref.1, bf16[256,2048]{1,0:T(8,128)(2,1)} %val_ref.1, f32[16,256]{1,0:T(8,128)} %dec_ref.1), custom_call_target="tpu_custom_call" | custom-call | flops 134217728 | bytes 3145728 | tf_op jit(solution)/shard_map/states/pallas_call | solution.py:471
  3.4 0.5 collective-permute-start
  3.9 1.9 %route.1 = (bf16[256,32]{1,0:T(8,128)(2,1)}, bf16[4,16,128]{2,1,0:T(8,128)(2,1)}) custom-call(s32[8,256]{1,0:T(8,128)} %bitcast.18, f32[8,256]{1,0:T(8,128)} %bitcast.19, s32[1,256]{1,0:T(1,128)} %bitcast.16), custom_call_target="tpu_custom_call" | custom-call | flops 134217728 | bytes 1048576 | tf_op jit(solution)/shard_map/route/pallas_call | solution.py:492
  5.9 0.0 collective-permute-done.recv_ref
  5.9 0.2 collective-permute-start.1
  6.1 0.3 collective-permute-start.2
  6.4 0.2 collective-permute-start.3
  6.6 0.1 copy-done.8
  6.7 2.4 %pair.1 = (bf16[16,80,128]{2,1,0:T(8,128)(2,1)}, f32[1032,128]{1,0:T(8,128)}) custom-call(s32[1]{0:T(128)} %bitcast.k_ref, f32[1032,128]{1,0:T(8,128)} %get-tuple-element.62.own_ref, f32[1032,128]{1,0:T(8,128)} %copy-done.8, bf16[4,16,128]{2,1,0:T(8,128)(2,1)} %get-tuple-element.67.notes_ref), custom_call_target="tpu_custom_call" | custom-call | tf_op jit(solution)/shard_map/pair/pallas_call | solution.py:507
  9.1 8.1 %all-to-all-start = ((bf16[16,80,128]{2,1,0:T(8,128)(2,1)}), bf16[16,80,128]{2,1,0:T(8,128)(2,1)S(1)}, u32[]{:S(2)}, u32[]{:S(2)}) async-start(bf16[16,80,128]{2,1,0:T(8,128)(2,1)} %get-tuple-element.68), calls=%async_computation | async-start | bytes 655360 | tf_op jit(solution)/shard_map/all_to_all | solution.py:73
  17.1 0.0 copy-start.3
  17.1 0.0 copy-start.5
  17.2 6.8 %inside.1 = (f32[256,2048]{1,0:T(8,128)}, bf16[256,2048]{1,0:T(8,128)(2,1)}, f32[96,2048]{1,0:T(8,128)}) custom-call(s32[1,256]{1,0:T(1,128)} %bitcast.17, f32[16,256]{1,0:T(8,128)} %dec_ref.1, bf16[256,2048]{1,0:T(8,128)(2,1)} %q_ref.1, bf16[256,2048]{1,0:T(8,128)(2,1)} %key_ref.1, bf16[256,2048]{1,0:T(8,128)(2,1)} %val_ref.1, bf16[256,2048]{1,0:T(8,128)(2,1)} %stream_ref.3), custom_call_target="tpu_custom_call" | custom-call | flops 536870912 | bytes 6291456 | tf_op jit(solution)/shard_map/inside/pallas_call | solution.py:519
  24.0 0.0 copy-start.7
  24.0 4.9 %all-to-all-done.in_ref = bf16[16,80,128]{2,1,0:T(8,128)(2,1)S(1)} async-done(((bf16[16,80,128]{2,1,0:T(8,128)(2,1)}), bf16[16,80,128]{2,1,0:T(8,128)(2,1)S(1)}, u32[]{:S(2)}, u32[]{:S(2)}) %all-to-all-start) | async-done | bytes 327712 | tf_op jit(solution)/shard_map/all_to_all | solution.py:73
  28.9 0.1 scan.1
  29.0 12.7 %all_to_all.15 = bf16[16,64,128]{2,1,0:T(8,128)(2,1)S(1)} all-to-all(bf16[16,64,128]{2,1,0:T(8,128)(2,1)S(1)} %scan.1), channel_id=1, replica_groups={{0,2,4,6,8,10,12,14,16,18,20,22,24,26,28,30},{1,3,5,7,9,11,13,15,17,19,..., dimensions={0} | all-to-all | bytes 524288 | tf_op jit(solution)/shard_map/all_to_all | solution.py:73
  41.7 0.0 collective-permute-done.1.g1
  41.7 0.0 collective-permute-done.2.u1
  41.7 0.0 collective-permute-done.3.d1
  41.7 0.0 copy-done.3
  41.7 0.2 split.1
  41.9 0.0 copy-start.2
  41.9 0.1 collective-permute-start.4
  42.0 0.0 copy-done.5
  42.0 0.3 mine.1.mine_ref
  42.4 1.1 %collective-permute-done.4.other_ref = bf16[1024,128]{1,0:T(8,128)(2,1)S(1)} collective-permute-done((bf16[1024,128]{1,0:T(8,128)(2,1)S(1)}, bf16[1024,128]{1,0:T(8,128)(2,1)S(1)}, u32[]{:S(2)}, u32[]{:S(2)}) %collective-permute-start.4) | collective-permute-done | bytes 262176 | tf_op jit(solution)/shard_map/ppermute | solution.py:63
  43.5 0.0 copy-done.6
  43.5 1.9 %rows.1 = bf16[256,2048]{1,0:T(8,128)(2,1)} custom-call(s32[1]{0:T(128)} %bitcast.k_ref, f32[96,2048]{1,0:T(8,128)S(1)} %copy-done, f32[32,1024]{1,0:T(8,128)S(1)} %mine.1.mine_ref, bf16[1024,128]{1,0:T(8,128)(2,1)S(1)} %collective-permute-done.4.other_ref, f32[1,2048]{1,0:T(1,128)S(1)} %bitcast.14, f32[1,2048]{1,0:T(1,128)S(1)} %bitcast.15, ...), custom_call_target="tpu_custom_call" | custom-call | tf_op jit(solution)/shard_map/rows/pallas_call | solution.py:579
  45.4 0.0 copy-done.2
  45.4 3.8 %all-to-all-start.2 = ((bf16[16,16,2048]{2,1,0:T(8,128)(2,1)}), bf16[16,16,2048]{2,1,0:T(8,128)(2,1)S(1)}, u32[]{:S(2)}, u32[]{:S(2)}) async-start(bf16[16,16,2048]{2,1,0:T(8,128)(2,1)} %bitcast.8), calls=%async_computation.2 | async-start | bytes 2097152 | tf_op jit(solution)/shard_map/all_to_all | solution.py:73
  49.3 1.3 %plan.1 = (bf16[128,32]{1,0:T(8,128)(2,1)S(1)}, bf16[128,32]{1,0:T(8,128)(2,1)S(1)}, bf16[128,32]{1,0:T(8,128)(2,1)S(1)}, bf16[128,32]{1,0:T(8,128)(2,1)S(1)}) custom-call(s32[1]{0:T(128)} %bitcast.9.at_ref, s32[1]{0:T(128)} %bitcast.10.plane_ref, bf16[16,80,128]{2,1,0:T(8,128)(2,1)S(1)} %all-to-all-done.in_ref), custom_call_target="tpu_custom_call" | custom-call | flops 16777216 | bytes 1048576 | tf_op jit(solution)/shard_map/plan/pallas_call | solution.py:534
  50.5 0.6 fusion
  51.8 4.0 %mixed.1 = (bf16[256,2048]{1,0:T(8,128)(2,1)}, f32[48,2048]{1,0:T(8,128)}) custom-call(s32[1]{0:T(128)} %bitcast.k_ref, s32[1]{0:T(128)S(6)} %min.7.from_ref, bf16[256,2048]{1,0:T(8,128)(2,1)} %get-tuple-element.83.lifted_ref, f32[256,2048]{1,0:T(8,128)} %get-tuple-element.84.inside_ref, bf16[256,2048]{1,0:T(8,128)(2,1)} %stream_ref.3, ...), custom_call_target="tpu_custom_call" | custom-call | flops 134217728 | bytes 7340032 | tf_op jit(solution)/shard_map/mixed/pallas_call | solution.py:599
  55.9 17.8 %all-to-all-done.2.x_hbm = bf16[16,16,2048]{2,1,0:T(8,128)(2,1)S(1)} async-done(((bf16[16,16,2048]{2,1,0:T(8,128)(2,1)}), bf16[16,16,2048]{2,1,0:T(8,128)(2,1)S(1)}, u32[]{:S(2)}, u32[]{:S(2)}) %all-to-all-start.2) | async-done | bytes 1048608 | tf_op jit(solution)/shard_map/all_to_all | solution.py:73
  73.7 6.9 %expert.1 = (bf16[64,1024]{1,0:T(8,128)(2,1)S(1)}, bf16[64,1024]{1,0:T(8,128)(2,1)S(1)}, bf16[64,1024]{1,0:T(8,128)(2,1)S(1)}, bf16[64,1024]{1,0:T(8,128)(2,1)S(1)}, bf16[2,256,512]{2,1,0:T(8,128)(2,1)S(1)}) custom-call(s32[1]{0:T(128)} %bitcast.9.at_ref, s32[1]{0:T(128)} %bitcast.10.plane_ref, bf16[16,16,2048]{2,1,0:T(8,128)(2,1)S(1)} %all-to-all-done.2.x_hbm, ...), custom_call_target="tpu_custom_call" | custom-call | flops 2684354560 | bytes 12582912 | tf_op jit(solution)/shard_map/expert/pallas_call | solution.py:618
  80.5 0.6 collective-permute-start.5
  81.2 2.0 %collective-permute-start.6 = (bf16[64,1024]{1,0:T(8,128)(2,1)S(1)}, bf16[64,1024]{1,0:T(8,128)(2,1)S(1)}, u32[]{:S(2)}, u32[]{:S(2)}) collective-permute-start(bf16[64,1024]{1,0:T(8,128)(2,1)S(1)} %get-tuple-element.104), channel_id=1, source_target_pairs={{0,4},{1,5},{2,6},{3,7},{4,0},{5,1},{6,2},{7,3},{8,12},{9,13},{10,... | collective-permute-start | bytes 393224 | tf_op jit(solution)/shard_map/ppermute | solution.py:67
  83.1 1.0 collective-permute-start.7
  84.1 2.3 %down.1 = (bf16[64,1024]{1,0:T(8,128)(2,1)S(1)}, bf16[64,1024]{1,0:T(8,128)(2,1)S(1)}, bf16[64,1024]{1,0:T(8,128)(2,1)S(1)}, bf16[64,1024]{1,0:T(8,128)(2,1)S(1)}) custom-call(bf16[2,256,512]{2,1,0:T(8,128)(2,1)S(1)} %get-tuple-element.110.hid_ref, bf16[512,2048]{1,0:T(8,128)(2,1)} %d0.1, bf16[512,2048]{1,0:T(8,128)(2,1)} %collective-permute-done.3.d1), custom_call_target="tpu_custom_call" | custom-call | flops 536870912 | bytes 2097152 | tf_op jit(solution)/shard_map/down/pallas_call | solution.py:634
  86.4 0.6 collective-permute-start.11
  87.1 2.0 %collective-permute-start.12 = (bf16[64,1024]{1,0:T(8,128)(2,1)S(1)}, bf16[64,1024]{1,0:T(8,128)(2,1)S(1)}, u32[]{:S(2)}, u32[]{:S(2)}) collective-permute-start(bf16[64,1024]{1,0:T(8,128)(2,1)S(1)} %get-tuple-element.113), channel_id=1, source_target_pairs={{0,4},{1,5},{2,6},{3,7},{4,0},{5,1},{6,2},{7,3},{8,12},{9,13},{10,... | collective-permute-start | bytes 393224 | tf_op jit(solution)/shard_map/ppermute | solution.py:67
  89.0 0.0 collective-permute-done.5.refs_5_
  89.0 1.0 collective-permute-start.13
  90.0 0.0 collective-permute-done.6.refs_6_
  90.0 0.1 collective-permute-done.7.refs_7_
  90.1 0.3 combine.2
  90.5 3.3 %collective-permute-start.8 = (bf16[32,1024]{1,0:T(8,128)(2,1)S(1)}, bf16[32,1024]{1,0:T(8,128)(2,1)S(1)}, u32[]{:S(2)}, u32[]{:S(2)}) collective-permute-start(bf16[32,1024]{1,0:T(8,128)(2,1)S(1)} %get-tuple-element.107), channel_id=1, source_target_pairs={{0,8},{1,9},{2,10},{3,11},{4,12},{5,13},{6,14},{7,15},{8,0},{9,1},... | collective-permute-start | bytes 196616 | tf_op jit(solution)/shard_map/ppermute | solution.py:67
  93.8 0.6 collective-permute-start.9
  94.4 0.0 collective-permute-done.11.refs_5_
  94.4 2.2 %collective-permute-start.10 = (bf16[32,1024]{1,0:T(8,128)(2,1)S(1)}, bf16[32,1024]{1,0:T(8,128)(2,1)S(1)}, u32[]{:S(2)}, u32[]{:S(2)}) collective-permute-start(bf16[32,1024]{1,0:T(8,128)(2,1)S(1)} %get-tuple-element.109), channel_id=1, source_target_pairs={{0,24},{1,25},{2,26},{3,27},{4,28},{5,29},{6,30},{7,31},{8,16},{9,... | collective-permute-start | bytes 196616 | tf_op jit(solution)/shard_map/ppermute | solution.py:67
  96.5 0.0 collective-permute-done.12.refs_6_
  96.5 0.0 collective-permute-done.13.refs_7_
  96.5 0.3 combine.3
  96.9 1.7 %collective-permute-start.14 = (bf16[32,1024]{1,0:T(8,128)(2,1)S(1)}, bf16[32,1024]{1,0:T(8,128)(2,1)S(1)}, u32[]{:S(2)}, u32[]{:S(2)}) collective-permute-start(bf16[32,1024]{1,0:T(8,128)(2,1)S(1)} %get-tuple-element.116), channel_id=1, source_target_pairs={{0,8},{1,9},{2,10},{3,11},{4,12},{5,13},{6,14},{7,15},{8,0},{9,1},... | collective-permute-start | bytes 196616 | tf_op jit(solution)/shard_map/ppermute | solution.py:67
  98.6 0.7 collective-permute-start.15
  99.3 0.0 collective-permute-done.8.refs_1_
  99.3 2.0 %collective-permute-start.16 = (bf16[32,1024]{1,0:T(8,128)(2,1)S(1)}, bf16[32,1024]{1,0:T(8,128)(2,1)S(1)}, u32[]{:S(2)}, u32[]{:S(2)}) collective-permute-start(bf16[32,1024]{1,0:T(8,128)(2,1)S(1)} %get-tuple-element.118), channel_id=1, source_target_pairs={{0,24},{1,25},{2,26},{3,27},{4,28},{5,29},{6,30},{7,31},{8,16},{9,... | collective-permute-start | bytes 196616 | tf_op jit(solution)/shard_map/ppermute | solution.py:67
  101.3 0.7 collective-permute-done.9.refs_2_
  102.1 0.0 collective-permute-done.10.refs_3_
  102.1 0.8 collective-permute-done.14.refs_5_
  102.9 2.8 %collective-permute-done.15.refs_6_ = bf16[32,1024]{1,0:T(8,128)(2,1)S(1)} collective-permute-done((bf16[32,1024]{1,0:T(8,128)(2,1)S(1)}, bf16[32,1024]{1,0:T(8,128)(2,1)S(1)}, u32[]{:S(2)}, u32[]{:S(2)}) %collective-permute-start.15) | collective-permute-done | bytes 65568 | tf_op jit(solution)/shard_map/ppermute | solution.py:67
  105.7 0.0 collective-permute-done.16.refs_7_
  105.7 1.0 final.1
  (11 shorter events, 0.0 us)
Async XLA Ops:
  3.4 2.5 %collective-permute-start = (f32[1032,128]{1,0:T(8,128)}, f32[1032,128]{1,0:T(8,128)S(1)}, u32[]{:S(2)}, u32[]{:S(2)}) collective-permute-start(f32[1032,128]{1,0:T(8,128)} %get-tuple-element.63), channel_id=1, source_target_pairs={{0,1},{1,0},{2,3},{3,2},{4,5},{5,4},{6,7},{7,6},{8,9},{9,8},{10,11... | collective-permute-start | bytes 1585160 | tf_op jit(solution)/shard_map/ppermute | solution.py:63
  5.9 0.8 copy-start.8
  5.9 35.8 %collective-permute-start.1 = (bf16[2048,512]{1,0:T(8,128)(2,1)}, bf16[2048,512]{1,0:T(8,128)(2,1)}, u32[]{:S(2)}, u32[]{:S(2)}) collective-permute-start(bf16[2048,512]{1,0:T(8,128)(2,1)} %g0), channel_id=1, source_target_pairs={{0,1},{1,0},{2,3},{3,2},{4,5},{5,4},{6,7},{7,6},{8,9},{9,8},{10,11... | collective-permute-start | bytes 6291464 | tf_op jit(solution)/shard_map/ppermute | solution.py:63
  6.1 35.6 %collective-permute-start.2 = (bf16[2048,512]{1,0:T(8,128)(2,1)}, bf16[2048,512]{1,0:T(8,128)(2,1)}, u32[]{:S(2)}, u32[]{:S(2)}) collective-permute-start(bf16[2048,512]{1,0:T(8,128)(2,1)} %u0), channel_id=1, source_target_pairs={{0,1},{1,0},{2,3},{3,2},{4,5},{5,4},{6,7},{7,6},{8,9},{9,8},{10,11... | collective-permute-start | bytes 6291464 | tf_op jit(solution)/shard_map/ppermute | solution.py:63
  6.4 35.3 %collective-permute-start.3 = (bf16[512,2048]{1,0:T(8,128)(2,1)}, bf16[512,2048]{1,0:T(8,128)(2,1)}, u32[]{:S(2)}, u32[]{:S(2)}) collective-permute-start(bf16[512,2048]{1,0:T(8,128)(2,1)} %d0.1), channel_id=1, source_target_pairs={{0,1},{1,0},{2,3},{3,2},{4,5},{5,4},{6,7},{7,6},{8,9},{9,8},{10,11... | collective-permute-start | bytes 6291464 | tf_op jit(solution)/shard_map/ppermute | solution.py:63
  9.1 19.9 %all-to-all-start = ((bf16[16,80,128]{2,1,0:T(8,128)(2,1)}), bf16[16,80,128]{2,1,0:T(8,128)(2,1)S(1)}, u32[]{:S(2)}, u32[]{:S(2)}) async-start(bf16[16,80,128]{2,1,0:T(8,128)(2,1)} %get-tuple-element.68), calls=%async_computation | async-start | bytes 655360 | tf_op jit(solution)/shard_map/all_to_all | solution.py:73
  17.1 24.6 %copy-start.3 = (f32[1032,128]{1,0:T(8,128)S(1)}, f32[1032,128]{1,0:T(8,128)}, u32[]{:S(2)}) copy-start(f32[1032,128]{1,0:T(8,128)} %get-tuple-element.77.first_ref) | copy-start | bytes 1585156
  17.1 24.9 %copy-start.5 = (f32[2048]{0:T(1024)S(1)}, f32[2048]{0:T(1024)}, u32[]{:S(2)}) copy-start(f32[2048]{0:T(1024)} %param.18) | copy-start | bytes 24580
  24.0 18.0 %copy-start = (f32[96,2048]{1,0:T(8,128)S(1)}, f32[96,2048]{1,0:T(8,128)}, u32[]{:S(2)}) copy-start(f32[96,2048]{1,0:T(8,128)} %get-tuple-element.80.near_ref) | copy-start | bytes 2359300
  24.0 19.5 %copy-start.6 = (bf16[256,32]{1,0:T(8,128)(2,1)S(1)}, bf16[256,32]{1,0:T(8,128)(2,1)}, u32[]{:S(2)}) copy-start(bf16[256,32]{1,0:T(8,128)(2,1)} %get-tuple-element.82.disp_ref) | copy-start | bytes 49156
  24.0 19.5 %copy-start.7 = (f32[2048]{0:T(1024)S(1)}, f32[2048]{0:T(1024)}, u32[]{:S(2)}) copy-start(f32[2048]{0:T(1024)} %param.19) | copy-start | bytes 24580
  41.9 3.5 %copy-start.2 = (bf16[1024,128]{1,0:T(8,128)(2,1)}, bf16[1024,128]{1,0:T(8,128)(2,1)S(1)}, u32[]{:S(2)}) copy-start(bf16[1024,128]{1,0:T(8,128)(2,1)S(1)} %get-tuple-element.85.keep_ref) | copy-start | bytes 786436
  41.9 1.6 %collective-permute-start.4 = (bf16[1024,128]{1,0:T(8,128)(2,1)S(1)}, bf16[1024,128]{1,0:T(8,128)(2,1)S(1)}, u32[]{:S(2)}, u32[]{:S(2)}) collective-permute-start(bf16[1024,128]{1,0:T(8,128)(2,1)S(1)} %get-tuple-element.81), channel_id=1, source_target_pairs={{0,1},{1,0},{2,3},{3,2},{4,5},{5,4},{6,7},{7,6},{8,9},{9,8},{10,11... | collective-permute-start | bytes 786440 | tf_op jit(solution)/shard_map/ppermute | solution.py:63
  43.5 1.9 %copy-start.1 = (bf16[1024,128]{1,0:T(8,128)(2,1)}, bf16[1024,128]{1,0:T(8,128)(2,1)S(1)}, u32[]{:S(2)}) copy-start(bf16[1024,128]{1,0:T(8,128)(2,1)S(1)} %collective-permute-done.4.other_ref) | copy-start | bytes 786436
  43.5 7.0 %copy-start.9 = (s32[256]{0:T(256)S(1)}, s32[256]{0:T(256)}, u32[]{:S(2)}) copy-start(s32[256]{0:T(256)} %param.22) | copy-start | bytes 3076
  45.4 28.2 %all-to-all-start.2 = ((bf16[16,16,2048]{2,1,0:T(8,128)(2,1)}), bf16[16,16,2048]{2,1,0:T(8,128)(2,1)S(1)}, u32[]{:S(2)}, u32[]{:S(2)}) async-start(bf16[16,16,2048]{2,1,0:T(8,128)(2,1)} %bitcast.8), calls=%async_computation.2 | async-start | bytes 2097152 | tf_op jit(solution)/shard_map/all_to_all | solution.py:73
  80.5 8.5 %collective-permute-start.5 = (bf16[64,1024]{1,0:T(8,128)(2,1)S(1)}, bf16[64,1024]{1,0:T(8,128)(2,1)S(1)}, u32[]{:S(2)}, u32[]{:S(2)}) collective-permute-start(bf16[64,1024]{1,0:T(8,128)(2,1)S(1)} %get-tuple-element.103), channel_id=1, source_target_pairs={{0,2},{1,3},{2,0},{3,1},{4,6},{5,7},{6,4},{7,5},{8,10},{9,11},{10,... | collective-permute-start | bytes 393224 | tf_op jit(solution)/shard_map/ppermute | solution.py:67
  81.2 8.8 %collective-permute-start.6 = (bf16[64,1024]{1,0:T(8,128)(2,1)S(1)}, bf16[64,1024]{1,0:T(8,128)(2,1)S(1)}, u32[]{:S(2)}, u32[]{:S(2)}) collective-permute-start(bf16[64,1024]{1,0:T(8,128)(2,1)S(1)} %get-tuple-element.104), channel_id=1, source_target_pairs={{0,4},{1,5},{2,6},{3,7},{4,0},{5,1},{6,2},{7,3},{8,12},{9,13},{10,... | collective-permute-start | bytes 393224 | tf_op jit(solution)/shard_map/ppermute | solution.py:67
  83.1 7.0 %collective-permute-start.7 = (bf16[64,1024]{1,0:T(8,128)(2,1)S(1)}, bf16[64,1024]{1,0:T(8,128)(2,1)S(1)}, u32[]{:S(2)}, u32[]{:S(2)}) collective-permute-start(bf16[64,1024]{1,0:T(8,128)(2,1)S(1)} %get-tuple-element.105), channel_id=1, source_target_pairs={{0,6},{1,7},{2,4},{3,5},{4,2},{5,3},{6,0},{7,1},{8,14},{9,15},{10,... | collective-permute-start | bytes 393224 | tf_op jit(solution)/shard_map/ppermute | solution.py:67
  84.1 21.6 %copy-start.4 = (f32[48,2048]{1,0:T(8,128)S(1)}, f32[48,2048]{1,0:T(8,128)}, u32[]{:S(2)}) copy-start(f32[48,2048]{1,0:T(8,128)} %get-tuple-element.93.near_ref) | copy-start | bytes 1179652
  86.4 7.9 %collective-permute-start.11 = (bf16[64,1024]{1,0:T(8,128)(2,1)S(1)}, bf16[64,1024]{1,0:T(8,128)(2,1)S(1)}, u32[]{:S(2)}, u32[]{:S(2)}) collective-permute-start(bf16[64,1024]{1,0:T(8,128)(2,1)S(1)} %get-tuple-element.112), channel_id=1, source_target_pairs={{0,2},{1,3},{2,0},{3,1},{4,6},{5,7},{6,4},{7,5},{8,10},{9,11},{10,... | collective-permute-start | bytes 393224 | tf_op jit(solution)/shard_map/ppermute | solution.py:67
  87.1 9.5 %collective-permute-start.12 = (bf16[64,1024]{1,0:T(8,128)(2,1)S(1)}, bf16[64,1024]{1,0:T(8,128)(2,1)S(1)}, u32[]{:S(2)}, u32[]{:S(2)}) collective-permute-start(bf16[64,1024]{1,0:T(8,128)(2,1)S(1)} %get-tuple-element.113), channel_id=1, source_target_pairs={{0,4},{1,5},{2,6},{3,7},{4,0},{5,1},{6,2},{7,3},{8,12},{9,13},{10,... | collective-permute-start | bytes 393224 | tf_op jit(solution)/shard_map/ppermute | solution.py:67
  89.0 7.5 %collective-permute-start.13 = (bf16[64,1024]{1,0:T(8,128)(2,1)S(1)}, bf16[64,1024]{1,0:T(8,128)(2,1)S(1)}, u32[]{:S(2)}, u32[]{:S(2)}) collective-permute-start(bf16[64,1024]{1,0:T(8,128)(2,1)S(1)} %get-tuple-element.114), channel_id=1, source_target_pairs={{0,6},{1,7},{2,4},{3,5},{4,2},{5,3},{6,0},{7,1},{8,14},{9,15},{10,... | collective-permute-start | bytes 393224 | tf_op jit(solution)/shard_map/ppermute | solution.py:67
  90.5 8.9 %collective-permute-start.8 = (bf16[32,1024]{1,0:T(8,128)(2,1)S(1)}, bf16[32,1024]{1,0:T(8,128)(2,1)S(1)}, u32[]{:S(2)}, u32[]{:S(2)}) collective-permute-start(bf16[32,1024]{1,0:T(8,128)(2,1)S(1)} %get-tuple-element.107), channel_id=1, source_target_pairs={{0,8},{1,9},{2,10},{3,11},{4,12},{5,13},{6,14},{7,15},{8,0},{9,1},... | collective-permute-start | bytes 196616 | tf_op jit(solution)/shard_map/ppermute | solution.py:67
  93.8 8.3 %collective-permute-start.9 = (bf16[32,1024]{1,0:T(8,128)(2,1)S(1)}, bf16[32,1024]{1,0:T(8,128)(2,1)S(1)}, u32[]{:S(2)}, u32[]{:S(2)}) collective-permute-start(bf16[32,1024]{1,0:T(8,128)(2,1)S(1)} %get-tuple-element.108), channel_id=1, source_target_pairs={{0,16},{1,17},{2,18},{3,19},{4,20},{5,21},{6,22},{7,23},{8,24},{9,... | collective-permute-start | bytes 196616 | tf_op jit(solution)/shard_map/ppermute | solution.py:67
  94.4 7.7 %collective-permute-start.10 = (bf16[32,1024]{1,0:T(8,128)(2,1)S(1)}, bf16[32,1024]{1,0:T(8,128)(2,1)S(1)}, u32[]{:S(2)}, u32[]{:S(2)}) collective-permute-start(bf16[32,1024]{1,0:T(8,128)(2,1)S(1)} %get-tuple-element.109), channel_id=1, source_target_pairs={{0,24},{1,25},{2,26},{3,27},{4,28},{5,29},{6,30},{7,31},{8,16},{9,... | collective-permute-start | bytes 196616 | tf_op jit(solution)/shard_map/ppermute | solution.py:67
  96.9 6.0 %collective-permute-start.14 = (bf16[32,1024]{1,0:T(8,128)(2,1)S(1)}, bf16[32,1024]{1,0:T(8,128)(2,1)S(1)}, u32[]{:S(2)}, u32[]{:S(2)}) collective-permute-start(bf16[32,1024]{1,0:T(8,128)(2,1)S(1)} %get-tuple-element.116), channel_id=1, source_target_pairs={{0,8},{1,9},{2,10},{3,11},{4,12},{5,13},{6,14},{7,15},{8,0},{9,1},... | collective-permute-start | bytes 196616 | tf_op jit(solution)/shard_map/ppermute | solution.py:67
  98.6 7.1 %collective-permute-start.15 = (bf16[32,1024]{1,0:T(8,128)(2,1)S(1)}, bf16[32,1024]{1,0:T(8,128)(2,1)S(1)}, u32[]{:S(2)}, u32[]{:S(2)}) collective-permute-start(bf16[32,1024]{1,0:T(8,128)(2,1)S(1)} %get-tuple-element.117), channel_id=1, source_target_pairs={{0,16},{1,17},{2,18},{3,19},{4,20},{5,21},{6,22},{7,23},{8,24},{9,... | collective-permute-start | bytes 196616 | tf_op jit(solution)/shard_map/ppermute | solution.py:67
  99.3 6.4 %collective-permute-start.16 = (bf16[32,1024]{1,0:T(8,128)(2,1)S(1)}, bf16[32,1024]{1,0:T(8,128)(2,1)S(1)}, u32[]{:S(2)}, u32[]{:S(2)}) collective-permute-start(bf16[32,1024]{1,0:T(8,128)(2,1)S(1)} %get-tuple-element.118), channel_id=1, source_target_pairs={{0,24},{1,25},{2,26},{3,27},{4,28},{5,29},{6,30},{7,31},{8,16},{9,... | collective-permute-start | bytes 196616 | tf_op jit(solution)/shard_map/ppermute | solution.py:67
